TPU v7x, 32 devices: a whole 2x2x4 slice. The times are simulated.
32 devices in a mesh: comp: 4 (over z), tile: 8 (over y, x, core).
Axes of the slice: x: 2, y: 2, z: 4, core: 2. Of those that a mesh axis runs over, the one named last changes fastest.
Arguments:
- atm_flux: float32 [8, 32768], P(None, ('comp', 'tile')), may hold values from -6 to 6
- intersection_weight: float32 [256, 4, 128, 128], P(('comp', 'tile')), may hold values from -0.5 to 0.5
- dest_tile: int32 [256, 4], P(('comp', 'tile')), may hold values from 0 to 7, all different within a row; in each aligned block of 8 rows (0 to 7, 8 to 15, ...) at most 4 rows name the same one
- dest_block: int32 [256, 4], P(('comp', 'tile')), may hold values from 0 to 31
- block_count: int32 [256], P(('comp', 'tile')), may hold values from 2 to 4
- sea_height: float32 [128, 1024], P('comp', 'tile'), may hold values from -6 to 6
- velocity_x: float32 [128, 1024], P('comp', 'tile'), may hold values from -3 to 3
- velocity_y: float32 [128, 1024], P('comp', 'tile'), may hold values from -3 to 3
- depth: float32 [128, 1024], P('comp', 'tile'), may hold values from 0.3 to 1
- sea_mask: int32 [128, 1024], P('comp', 'tile'), may hold values 0 or 1
Outputs:
- forcing: float32 [8, 128, 1024], P(None, 'comp', 'tile')
- height_out: float32 [128, 1024], P('comp', 'tile')
- flow_x: float32 [128, 1024], P('comp', 'tile')
- flow_y: float32 [128, 1024], P('comp', 'tile')
Inputs may be any that keep to these rules, and one draw needn't show every extreme that they name: `dest_tile`: within the 8 rows of one device no tile number is named more than 4 times, and some device names some tile exactly 4 times; each row names 4 different tiles of its own section. Slots k with k < block_count carry weights; the others are padding.
All inputs are finite; a program needn't handle non-finite values. No bound on the sum of `sea_mask` on one device may be relied on, other than what follows from the above.
Results may differ from a plain program's by a relative error of at most 0.000094.
Values sent between devices are 32-bit elements; how exact they have to be, the bound alone decides.
No kernel may reach another device: no remote copies, remote signals or barrier semaphores. Data moves between devices by JAX's collectives and lax.ppermute only.
A program may use at most 64 MiB of HBM per device.

v0:
```python
import jax
import jax.numpy as jnp
from jax import lax
from jax.sharding import PartitionSpec as P

NSUB = 8


def extended(cells, sides, width):
    for axis, dim in sides:
        count = lax.axis_size(axis)
        ends = count - 1
        head = lax.slice_in_dim(cells, 0, width, axis=dim)
        tail = lax.slice_in_dim(cells, cells.shape[dim] - width, cells.shape[dim], axis=dim)
        cells = jnp.concatenate(
            [
                lax.ppermute(tail, axis, [(i, (i + 1) % count) for i in range(ends)]),
                cells,
                lax.ppermute(head, axis, [((i + 1) % count, i) for i in range(ends)]),
            ],
            axis=dim,
        )
    return cells


def cols_inner(padded):
    return 0.5 * (padded[..., 1:-1, 2:] - padded[..., 1:-1, :-2])


def rows_inner(padded):
    return 0.5 * (padded[..., 2:, 1:-1] - padded[..., :-2, 1:-1])


def local(
    atm_flux,
    intersection_weight,
    dest_tile,
    dest_block,
    block_count,
    sea_height,
    velocity_x,
    velocity_y,
    depth,
    sea_mask,
):
    blocks_here, slots_per = dest_tile.shape
    fields = atm_flux.shape[0]
    atm_width = intersection_weight.shape[2]
    ocean_width = intersection_weight.shape[3]
    rows_here, cols_here = sea_height.shape
    ocean_blocks = rows_here * cols_here // ocean_width
    slot_total = blocks_here * slots_per
    highest = lax.Precision.HIGHEST
    pieces = atm_flux.reshape(fields, blocks_here, atm_width).transpose(1, 0, 2)
    partial_value = jnp.einsum("bfa,bkao->bkfo", pieces, intersection_weight, precision=highest)
    slot_live = (jnp.arange(slots_per, dtype=jnp.int32)[None, :] < block_count[:, None]).astype(
        jnp.float32
    )
    partial_value = (partial_value * slot_live[:, :, None, None]).reshape(
        slot_total, fields * ocean_width
    )
    tile_of = dest_tile.reshape(slot_total)
    block_of = dest_block.reshape(slot_total)
    target = tile_of * ocean_blocks + block_of
    row_index = jnp.arange(lax.axis_size("tile") * ocean_blocks, dtype=jnp.int32)
    select = (row_index[:, None] == target[None, :]).astype(jnp.float32)
    summed = lax.psum_scatter(
        jnp.dot(select, partial_value, precision=highest), "tile", scatter_dimension=0, tiled=True
    )
    sea_float = sea_mask.astype(jnp.float32)
    grid = summed.reshape(ocean_blocks, fields, ocean_width).transpose(1, 0, 2)
    forcing = grid * sea_float
    row_global = lax.axis_index("comp") * rows_here + jnp.arange(rows_here, dtype=jnp.int32)
    row_frac = row_global.astype(jnp.float32) / float(rows_here * lax.axis_size("comp"))
    coriolis = (0.02 + 0.06 * row_frac)[:, None] * jnp.ones((rows_here, cols_here), jnp.float32)
    wind_x = 0.05 * forcing[0] * (1.0 / depth)
    wind_y = 0.05 * forcing[1] * (1.0 / depth)
    fresh = 0.1 * forcing[2]
    height, flow_u, flow_v = (sea_height, velocity_x, velocity_y)
    for cycle in range(NSUB):
        flows = jnp.stack([depth * flow_u, depth * flow_v])
        flow_rim = extended(flows, (("comp", 1), ("tile", 2)), 1)
        spread = cols_inner(flow_rim[0]) + rows_inner(flow_rim[1])
        height = sea_float * (height - 0.4 * spread + fresh)
        height_pad = extended(height, (("comp", 0), ("tile", 1)), 1)
        next_u = sea_float * (
            0.98 * flow_u - 0.4 * cols_inner(height_pad) + coriolis * flow_v + wind_x
        )
        next_v = sea_float * (
            0.98 * flow_v - 0.4 * rows_inner(height_pad) - coriolis * flow_u + wind_y
        )
        flow_u, flow_v = (next_u, next_v)
    return (forcing, height, flow_u, flow_v)


def solution(mesh):
    in_specs = (
        P(None, ("comp", "tile")),
        P(("comp", "tile"), None, None, None),
        P(("comp", "tile"), None),
        P(("comp", "tile"), None),
        P(("comp", "tile")),
        P("comp", "tile"),
        P("comp", "tile"),
        P("comp", "tile"),
        P("comp", "tile"),
        P("comp", "tile"),
    )
    out_specs = (P(None, "comp", "tile"), P("comp", "tile"), P("comp", "tile"), P("comp", "tile"))
    return jax.shard_map(local, mesh=mesh, in_specs=in_specs, out_specs=out_specs, check_vma=False)
```

profile of v0, /device:TPU:19, one launch (start us, length us, event | category | flops | bytes accessed | tf_op | source)
XLA Modules:
  0.0 308.1 jit_solution(9800774132401068133)
XLA Ops:
  27.4 22.3 %reduce-scatter.2.cloned.1.call-done = f32[32,1024]{1,0:T(8,128)} async-done(((f32[256,1024]{1,0:T(8,128)}), f32[32,1024]{1,0:T(8,128)}) %reduce-scatter.2.cloned.1.call-update) | async-done | bytes 131088 | tf_op jit(solution)/shard_map/reduce_scatter | solution.py:67
  57.2 5.2 %collective-permute-start.7 = (f32[34,1]{1,0:T(8,128)S(1)}, f32[34,1]{1,0:T(8,128)S(1)}, u32[]{:S(2)}, u32[]{:S(2)}) collective-permute-start(f32[34,1]{1,0:T(8,128)S(1)} %get-tuple-element.114), channel_id=1, source_target_pairs={{0,1},{1,2},{2,3},{3,4},{4,5},{5,6},{6,7},{8,9},{9,10},{10,11},{11... | collective-permute-start | bytes 416 | tf_op jit(solution)/shard_map/ppermute | solution.py:17
  64.4 4.0 %collective-permute-done.6 = f32[34,1]{1,0:T(8,128)S(1)} collective-permute-done((f32[34,1]{1,0:T(8,128)S(1)}, f32[34,1]{1,0:T(8,128)S(1)}, u32[]{:S(2)}, u32[]{:S(2)}) %collective-permute-start.6) | collective-permute-done | bytes 168 | tf_op jit(solution)/shard_map/ppermute | solution.py:19
  77.0 4.5 %collective-permute-start.10 = (f32[2,34,1]{2,1,0:T(8,128)S(1)}, f32[2,34,1]{2,1,0:T(8,128)S(1)}, u32[]{:S(2)}, u32[]{:S(2)}) collective-permute-start(f32[2,34,1]{2,1,0:T(8,128)S(1)} %get-tuple-element.79), channel_id=1, source_target_pairs={{0,1},{1,2},{2,3},{3,4},{4,5},{5,6},{6,7},{8,9},{9,10},{10,11},{11... | collective-permute-start | bytes 824 | tf_op jit(solution)/shard_map/ppermute | solution.py:17
  89.2 6.6 %collective-permute-start.15 = (f32[34,1]{1,0:T(8,128)S(1)}, f32[34,1]{1,0:T(8,128)S(1)}, u32[]{:S(2)}, u32[]{:S(2)}) collective-permute-start(f32[34,1]{1,0:T(8,128)S(1)} %get-tuple-element.112), channel_id=1, source_target_pairs={{0,1},{1,2},{2,3},{3,4},{4,5},{5,6},{6,7},{8,9},{9,10},{10,11},{11... | collective-permute-start | bytes 416 | tf_op jit(solution)/shard_map/ppermute | solution.py:17
  97.7 4.1 %collective-permute-done.14 = f32[34,1]{1,0:T(8,128)S(1)} collective-permute-done((f32[34,1]{1,0:T(8,128)S(1)}, f32[34,1]{1,0:T(8,128)S(1)}, u32[]{:S(2)}, u32[]{:S(2)}) %collective-permute-start.14) | collective-permute-done | bytes 168 | tf_op jit(solution)/shard_map/ppermute | solution.py:19
  110.1 4.5 %collective-permute-start.18 = (f32[2,34,1]{2,1,0:T(8,128)S(1)}, f32[2,34,1]{2,1,0:T(8,128)S(1)}, u32[]{:S(2)}, u32[]{:S(2)}) collective-permute-start(f32[2,34,1]{2,1,0:T(8,128)S(1)} %get-tuple-element.77), channel_id=1, source_target_pairs={{0,1},{1,2},{2,3},{3,4},{4,5},{5,6},{6,7},{8,9},{9,10},{10,11},{11... | collective-permute-start | bytes 824 | tf_op jit(solution)/shard_map/ppermute | solution.py:17
  122.3 6.3 %collective-permute-start.23 = (f32[34,1]{1,0:T(8,128)S(1)}, f32[34,1]{1,0:T(8,128)S(1)}, u32[]{:S(2)}, u32[]{:S(2)}) collective-permute-start(f32[34,1]{1,0:T(8,128)S(1)} %get-tuple-element.110), channel_id=1, source_target_pairs={{0,1},{1,2},{2,3},{3,4},{4,5},{5,6},{6,7},{8,9},{9,10},{10,11},{11... | collective-permute-start | bytes 416 | tf_op jit(solution)/shard_map/ppermute | solution.py:17
  130.5 4.1 %collective-permute-done.22 = f32[34,1]{1,0:T(8,128)S(1)} collective-permute-done((f32[34,1]{1,0:T(8,128)S(1)}, f32[34,1]{1,0:T(8,128)S(1)}, u32[]{:S(2)}, u32[]{:S(2)}) %collective-permute-start.22) | collective-permute-done | bytes 168 | tf_op jit(solution)/shard_map/ppermute | solution.py:19
  143.0 4.5 %collective-permute-start.26 = (f32[2,34,1]{2,1,0:T(8,128)S(1)}, f32[2,34,1]{2,1,0:T(8,128)S(1)}, u32[]{:S(2)}, u32[]{:S(2)}) collective-permute-start(f32[2,34,1]{2,1,0:T(8,128)S(1)} %get-tuple-element.75), channel_id=1, source_target_pairs={{0,1},{1,2},{2,3},{3,4},{4,5},{5,6},{6,7},{8,9},{9,10},{10,11},{11... | collective-permute-start | bytes 824 | tf_op jit(solution)/shard_map/ppermute | solution.py:17
  155.1 6.3 %collective-permute-start.31 = (f32[34,1]{1,0:T(8,128)S(1)}, f32[34,1]{1,0:T(8,128)S(1)}, u32[]{:S(2)}, u32[]{:S(2)}) collective-permute-start(f32[34,1]{1,0:T(8,128)S(1)} %get-tuple-element.108), channel_id=1, source_target_pairs={{0,1},{1,2},{2,3},{3,4},{4,5},{5,6},{6,7},{8,9},{9,10},{10,11},{11... | collective-permute-start | bytes 416 | tf_op jit(solution)/shard_map/ppermute | solution.py:17
  163.4 4.1 %collective-permute-done.30 = f32[34,1]{1,0:T(8,128)S(1)} collective-permute-done((f32[34,1]{1,0:T(8,128)S(1)}, f32[34,1]{1,0:T(8,128)S(1)}, u32[]{:S(2)}, u32[]{:S(2)}) %collective-permute-start.30) | collective-permute-done | bytes 168 | tf_op jit(solution)/shard_map/ppermute | solution.py:19
  175.8 4.5 %collective-permute-start.34 = (f32[2,34,1]{2,1,0:T(8,128)S(1)}, f32[2,34,1]{2,1,0:T(8,128)S(1)}, u32[]{:S(2)}, u32[]{:S(2)}) collective-permute-start(f32[2,34,1]{2,1,0:T(8,128)S(1)} %get-tuple-element.73), channel_id=1, source_target_pairs={{0,1},{1,2},{2,3},{3,4},{4,5},{5,6},{6,7},{8,9},{9,10},{10,11},{11... | collective-permute-start | bytes 824 | tf_op jit(solution)/shard_map/ppermute | solution.py:17
  188.0 6.3 %collective-permute-start.39 = (f32[34,1]{1,0:T(8,128)S(1)}, f32[34,1]{1,0:T(8,128)S(1)}, u32[]{:S(2)}, u32[]{:S(2)}) collective-permute-start(f32[34,1]{1,0:T(8,128)S(1)} %get-tuple-element.106), channel_id=1, source_target_pairs={{0,1},{1,2},{2,3},{3,4},{4,5},{5,6},{6,7},{8,9},{9,10},{10,11},{11... | collective-permute-start | bytes 416 | tf_op jit(solution)/shard_map/ppermute | solution.py:17
  196.2 4.1 %collective-permute-done.38 = f32[34,1]{1,0:T(8,128)S(1)} collective-permute-done((f32[34,1]{1,0:T(8,128)S(1)}, f32[34,1]{1,0:T(8,128)S(1)}, u32[]{:S(2)}, u32[]{:S(2)}) %collective-permute-start.38) | collective-permute-done | bytes 168 | tf_op jit(solution)/shard_map/ppermute | solution.py:19
  208.7 4.5 %collective-permute-start.42 = (f32[2,34,1]{2,1,0:T(8,128)S(1)}, f32[2,34,1]{2,1,0:T(8,128)S(1)}, u32[]{:S(2)}, u32[]{:S(2)}) collective-permute-start(f32[2,34,1]{2,1,0:T(8,128)S(1)} %get-tuple-element.71), channel_id=1, source_target_pairs={{0,1},{1,2},{2,3},{3,4},{4,5},{5,6},{6,7},{8,9},{9,10},{10,11},{11... | collective-permute-start | bytes 824 | tf_op jit(solution)/shard_map/ppermute | solution.py:17
  220.8 6.3 %collective-permute-start.47 = (f32[34,1]{1,0:T(8,128)S(1)}, f32[34,1]{1,0:T(8,128)S(1)}, u32[]{:S(2)}, u32[]{:S(2)}) collective-permute-start(f32[34,1]{1,0:T(8,128)S(1)} %get-tuple-element.104), channel_id=1, source_target_pairs={{0,1},{1,2},{2,3},{3,4},{4,5},{5,6},{6,7},{8,9},{9,10},{10,11},{11... | collective-permute-start | bytes 416 | tf_op jit(solution)/shard_map/ppermute | solution.py:17
  229.1 4.1 %collective-permute-done.46 = f32[34,1]{1,0:T(8,128)S(1)} collective-permute-done((f32[34,1]{1,0:T(8,128)S(1)}, f32[34,1]{1,0:T(8,128)S(1)}, u32[]{:S(2)}, u32[]{:S(2)}) %collective-permute-start.46) | collective-permute-done | bytes 168 | tf_op jit(solution)/shard_map/ppermute | solution.py:19
  241.5 4.5 %collective-permute-start.50 = (f32[2,34,1]{2,1,0:T(8,128)S(1)}, f32[2,34,1]{2,1,0:T(8,128)S(1)}, u32[]{:S(2)}, u32[]{:S(2)}) collective-permute-start(f32[2,34,1]{2,1,0:T(8,128)S(1)} %get-tuple-element.69), channel_id=1, source_target_pairs={{0,1},{1,2},{2,3},{3,4},{4,5},{5,6},{6,7},{8,9},{9,10},{10,11},{11... | collective-permute-start | bytes 824 | tf_op jit(solution)/shard_map/ppermute | solution.py:17
  253.7 6.3 %collective-permute-start.55 = (f32[34,1]{1,0:T(8,128)S(1)}, f32[34,1]{1,0:T(8,128)S(1)}, u32[]{:S(2)}, u32[]{:S(2)}) collective-permute-start(f32[34,1]{1,0:T(8,128)S(1)} %get-tuple-element.102), channel_id=1, source_target_pairs={{0,1},{1,2},{2,3},{3,4},{4,5},{5,6},{6,7},{8,9},{9,10},{10,11},{11... | collective-permute-start | bytes 416 | tf_op jit(solution)/shard_map/ppermute | solution.py:17
  261.9 4.1 %collective-permute-done.54 = f32[34,1]{1,0:T(8,128)S(1)} collective-permute-done((f32[34,1]{1,0:T(8,128)S(1)}, f32[34,1]{1,0:T(8,128)S(1)}, u32[]{:S(2)}, u32[]{:S(2)}) %collective-permute-start.54) | collective-permute-done | bytes 168 | tf_op jit(solution)/shard_map/ppermute | solution.py:19
  274.4 4.5 %collective-permute-start.58 = (f32[2,34,1]{2,1,0:T(8,128)S(1)}, f32[2,34,1]{2,1,0:T(8,128)S(1)}, u32[]{:S(2)}, u32[]{:S(2)}) collective-permute-start(f32[2,34,1]{2,1,0:T(8,128)S(1)} %get-tuple-element.67), channel_id=1, source_target_pairs={{0,1},{1,2},{2,3},{3,4},{4,5},{5,6},{6,7},{8,9},{9,10},{10,11},{11... | collective-permute-start | bytes 824 | tf_op jit(solution)/shard_map/ppermute | solution.py:17
  288.0 6.6 %collective-permute-start.63 = (f32[34,1]{1,0:T(8,128)S(1)}, f32[34,1]{1,0:T(8,128)S(1)}, u32[]{:S(2)}, u32[]{:S(2)}) collective-permute-start(f32[34,1]{1,0:T(8,128)S(1)} %get-tuple-element.100), channel_id=1, source_target_pairs={{0,1},{1,2},{2,3},{3,4},{4,5},{5,6},{6,7},{8,9},{9,10},{10,11},{11... | collective-permute-start | bytes 416 | tf_op jit(solution)/shard_map/ppermute | solution.py:17
  296.5 4.1 %collective-permute-done.62 = f32[34,1]{1,0:T(8,128)S(1)} collective-permute-done((f32[34,1]{1,0:T(8,128)S(1)}, f32[34,1]{1,0:T(8,128)S(1)}, u32[]{:S(2)}, u32[]{:S(2)}) %collective-permute-start.62) | collective-permute-done | bytes 168 | tf_op jit(solution)/shard_map/ppermute | solution.py:19
  (213 shorter events, 156.4 us)
Async XLA Ops:
  7.2 42.4 %reduce-scatter.2.cloned.1.call-start = ((), (), s32[]{:S(2)}) async-start(), calls=%async_computation.1 | async-start | bytes 1179648 | tf_op jit(solution)/shard_map/reduce_scatter | solution.py:67
  19.1 7.1 %collective-permute-start.3 = (f32[2,34,1]{2,1,0:T(8,128)S(1)}, f32[2,34,1]{2,1,0:T(8,128)S(1)}, u32[]{:S(2)}, u32[]{:S(2)}) collective-permute-start(f32[2,34,1]{2,1,0:T(8,128)S(1)} %get-tuple-element.82), channel_id=1, source_target_pairs={{1,0},{2,1},{3,2},{4,3},{5,4},{6,5},{7,6},{9,8},{10,9},{11,10},{12... | collective-permute-start | bytes 824 | tf_op jit(solution)/shard_map/ppermute | solution.py:19
  57.2 7.2 %collective-permute-start.7 = (f32[34,1]{1,0:T(8,128)S(1)}, f32[34,1]{1,0:T(8,128)S(1)}, u32[]{:S(2)}, u32[]{:S(2)}) collective-permute-start(f32[34,1]{1,0:T(8,128)S(1)} %get-tuple-element.114), channel_id=1, source_target_pairs={{0,1},{1,2},{2,3},{3,4},{4,5},{5,6},{6,7},{8,9},{9,10},{10,11},{11... | collective-permute-start | bytes 416 | tf_op jit(solution)/shard_map/ppermute | solution.py:17
  62.4 6.0 %collective-permute-start.6 = (f32[34,1]{1,0:T(8,128)S(1)}, f32[34,1]{1,0:T(8,128)S(1)}, u32[]{:S(2)}, u32[]{:S(2)}) collective-permute-start(f32[34,1]{1,0:T(8,128)S(1)} %get-tuple-element.113), channel_id=1, source_target_pairs={{1,0},{2,1},{3,2},{4,3},{5,4},{6,5},{7,6},{9,8},{10,9},{11,10},{12... | collective-permute-start | bytes 416 | tf_op jit(solution)/shard_map/ppermute | solution.py:19
  75.1 6.5 %collective-permute-start.11 = (f32[2,34,1]{2,1,0:T(8,128)S(1)}, f32[2,34,1]{2,1,0:T(8,128)S(1)}, u32[]{:S(2)}, u32[]{:S(2)}) collective-permute-start(f32[2,34,1]{2,1,0:T(8,128)S(1)} %get-tuple-element.80), channel_id=1, source_target_pairs={{1,0},{2,1},{3,2},{4,3},{5,4},{6,5},{7,6},{9,8},{10,9},{11,10},{12... | collective-permute-start | bytes 824 | tf_op jit(solution)/shard_map/ppermute | solution.py:19
  89.2 8.5 %collective-permute-start.15 = (f32[34,1]{1,0:T(8,128)S(1)}, f32[34,1]{1,0:T(8,128)S(1)}, u32[]{:S(2)}, u32[]{:S(2)}) collective-permute-start(f32[34,1]{1,0:T(8,128)S(1)} %get-tuple-element.112), channel_id=1, source_target_pairs={{0,1},{1,2},{2,3},{3,4},{4,5},{5,6},{6,7},{8,9},{9,10},{10,11},{11... | collective-permute-start | bytes 416 | tf_op jit(solution)/shard_map/ppermute | solution.py:17
  95.8 6.0 %collective-permute-start.14 = (f32[34,1]{1,0:T(8,128)S(1)}, f32[34,1]{1,0:T(8,128)S(1)}, u32[]{:S(2)}, u32[]{:S(2)}) collective-permute-start(f32[34,1]{1,0:T(8,128)S(1)} %get-tuple-element.111), channel_id=1, source_target_pairs={{1,0},{2,1},{3,2},{4,3},{5,4},{6,5},{7,6},{9,8},{10,9},{11,10},{12... | collective-permute-start | bytes 416 | tf_op jit(solution)/shard_map/ppermute | solution.py:19
  108.2 6.5 %collective-permute-start.19 = (f32[2,34,1]{2,1,0:T(8,128)S(1)}, f32[2,34,1]{2,1,0:T(8,128)S(1)}, u32[]{:S(2)}, u32[]{:S(2)}) collective-permute-start(f32[2,34,1]{2,1,0:T(8,128)S(1)} %get-tuple-element.78), channel_id=1, source_target_pairs={{1,0},{2,1},{3,2},{4,3},{5,4},{6,5},{7,6},{9,8},{10,9},{11,10},{12... | collective-permute-start | bytes 824 | tf_op jit(solution)/shard_map/ppermute | solution.py:19
  122.3 8.3 %collective-permute-start.23 = (f32[34,1]{1,0:T(8,128)S(1)}, f32[34,1]{1,0:T(8,128)S(1)}, u32[]{:S(2)}, u32[]{:S(2)}) collective-permute-start(f32[34,1]{1,0:T(8,128)S(1)} %get-tuple-element.110), channel_id=1, source_target_pairs={{0,1},{1,2},{2,3},{3,4},{4,5},{5,6},{6,7},{8,9},{9,10},{10,11},{11... | collective-permute-start | bytes 416 | tf_op jit(solution)/shard_map/ppermute | solution.py:17
  128.6 6.0 %collective-permute-start.22 = (f32[34,1]{1,0:T(8,128)S(1)}, f32[34,1]{1,0:T(8,128)S(1)}, u32[]{:S(2)}, u32[]{:S(2)}) collective-permute-start(f32[34,1]{1,0:T(8,128)S(1)} %get-tuple-element.109), channel_id=1, source_target_pairs={{1,0},{2,1},{3,2},{4,3},{5,4},{6,5},{7,6},{9,8},{10,9},{11,10},{12... | collective-permute-start | bytes 416 | tf_op jit(solution)/shard_map/ppermute | solution.py:19
  141.0 6.5 %collective-permute-start.27 = (f32[2,34,1]{2,1,0:T(8,128)S(1)}, f32[2,34,1]{2,1,0:T(8,128)S(1)}, u32[]{:S(2)}, u32[]{:S(2)}) collective-permute-start(f32[2,34,1]{2,1,0:T(8,128)S(1)} %get-tuple-element.76), channel_id=1, source_target_pairs={{1,0},{2,1},{3,2},{4,3},{5,4},{6,5},{7,6},{9,8},{10,9},{11,10},{12... | collective-permute-start | bytes 824 | tf_op jit(solution)/shard_map/ppermute | solution.py:19
  155.1 8.3 %collective-permute-start.31 = (f32[34,1]{1,0:T(8,128)S(1)}, f32[34,1]{1,0:T(8,128)S(1)}, u32[]{:S(2)}, u32[]{:S(2)}) collective-permute-start(f32[34,1]{1,0:T(8,128)S(1)} %get-tuple-element.108), channel_id=1, source_target_pairs={{0,1},{1,2},{2,3},{3,4},{4,5},{5,6},{6,7},{8,9},{9,10},{10,11},{11... | collective-permute-start | bytes 416 | tf_op jit(solution)/shard_map/ppermute | solution.py:17
  161.4 6.0 %collective-permute-start.30 = (f32[34,1]{1,0:T(8,128)S(1)}, f32[34,1]{1,0:T(8,128)S(1)}, u32[]{:S(2)}, u32[]{:S(2)}) collective-permute-start(f32[34,1]{1,0:T(8,128)S(1)} %get-tuple-element.107), channel_id=1, source_target_pairs={{1,0},{2,1},{3,2},{4,3},{5,4},{6,5},{7,6},{9,8},{10,9},{11,10},{12... | collective-permute-start | bytes 416 | tf_op jit(solution)/shard_map/ppermute | solution.py:19
  173.9 6.5 %collective-permute-start.35 = (f32[2,34,1]{2,1,0:T(8,128)S(1)}, f32[2,34,1]{2,1,0:T(8,128)S(1)}, u32[]{:S(2)}, u32[]{:S(2)}) collective-permute-start(f32[2,34,1]{2,1,0:T(8,128)S(1)} %get-tuple-element.74), channel_id=1, source_target_pairs={{1,0},{2,1},{3,2},{4,3},{5,4},{6,5},{7,6},{9,8},{10,9},{11,10},{12... | collective-permute-start | bytes 824 | tf_op jit(solution)/shard_map/ppermute | solution.py:19
  188.0 8.3 %collective-permute-start.39 = (f32[34,1]{1,0:T(8,128)S(1)}, f32[34,1]{1,0:T(8,128)S(1)}, u32[]{:S(2)}, u32[]{:S(2)}) collective-permute-start(f32[34,1]{1,0:T(8,128)S(1)} %get-tuple-element.106), channel_id=1, source_target_pairs={{0,1},{1,2},{2,3},{3,4},{4,5},{5,6},{6,7},{8,9},{9,10},{10,11},{11... | collective-permute-start | bytes 416 | tf_op jit(solution)/shard_map/ppermute | solution.py:17
  194.3 6.0 %collective-permute-start.38 = (f32[34,1]{1,0:T(8,128)S(1)}, f32[34,1]{1,0:T(8,128)S(1)}, u32[]{:S(2)}, u32[]{:S(2)}) collective-permute-start(f32[34,1]{1,0:T(8,128)S(1)} %get-tuple-element.105), channel_id=1, source_target_pairs={{1,0},{2,1},{3,2},{4,3},{5,4},{6,5},{7,6},{9,8},{10,9},{11,10},{12... | collective-permute-start | bytes 416 | tf_op jit(solution)/shard_map/ppermute | solution.py:19
  206.7 6.5 %collective-permute-start.43 = (f32[2,34,1]{2,1,0:T(8,128)S(1)}, f32[2,34,1]{2,1,0:T(8,128)S(1)}, u32[]{:S(2)}, u32[]{:S(2)}) collective-permute-start(f32[2,34,1]{2,1,0:T(8,128)S(1)} %get-tuple-element.72), channel_id=1, source_target_pairs={{1,0},{2,1},{3,2},{4,3},{5,4},{6,5},{7,6},{9,8},{10,9},{11,10},{12... | collective-permute-start | bytes 824 | tf_op jit(solution)/shard_map/ppermute | solution.py:19
  220.8 8.3 %collective-permute-start.47 = (f32[34,1]{1,0:T(8,128)S(1)}, f32[34,1]{1,0:T(8,128)S(1)}, u32[]{:S(2)}, u32[]{:S(2)}) collective-permute-start(f32[34,1]{1,0:T(8,128)S(1)} %get-tuple-element.104), channel_id=1, source_target_pairs={{0,1},{1,2},{2,3},{3,4},{4,5},{5,6},{6,7},{8,9},{9,10},{10,11},{11... | collective-permute-start | bytes 416 | tf_op jit(solution)/shard_map/ppermute | solution.py:17
  239.6 6.5 %collective-permute-start.51 = (f32[2,34,1]{2,1,0:T(8,128)S(1)}, f32[2,34,1]{2,1,0:T(8,128)S(1)}, u32[]{:S(2)}, u32[]{:S(2)}) collective-permute-start(f32[2,34,1]{2,1,0:T(8,128)S(1)} %get-tuple-element.70), channel_id=1, source_target_pairs={{1,0},{2,1},{3,2},{4,3},{5,4},{6,5},{7,6},{9,8},{10,9},{11,10},{12... | collective-permute-start | bytes 824 | tf_op jit(solution)/shard_map/ppermute | solution.py:19
  253.7 8.3 %collective-permute-start.55 = (f32[34,1]{1,0:T(8,128)S(1)}, f32[34,1]{1,0:T(8,128)S(1)}, u32[]{:S(2)}, u32[]{:S(2)}) collective-permute-start(f32[34,1]{1,0:T(8,128)S(1)} %get-tuple-element.102), channel_id=1, source_target_pairs={{0,1},{1,2},{2,3},{3,4},{4,5},{5,6},{6,7},{8,9},{9,10},{10,11},{11... | collective-permute-start | bytes 416 | tf_op jit(solution)/shard_map/ppermute | solution.py:17
  260.0 6.0 %collective-permute-start.54 = (f32[34,1]{1,0:T(8,128)S(1)}, f32[34,1]{1,0:T(8,128)S(1)}, u32[]{:S(2)}, u32[]{:S(2)}) collective-permute-start(f32[34,1]{1,0:T(8,128)S(1)} %get-tuple-element.101), channel_id=1, source_target_pairs={{1,0},{2,1},{3,2},{4,3},{5,4},{6,5},{7,6},{9,8},{10,9},{11,10},{12... | collective-permute-start | bytes 416 | tf_op jit(solution)/shard_map/ppermute | solution.py:19
  272.4 6.5 %collective-permute-start.59 = (f32[2,34,1]{2,1,0:T(8,128)S(1)}, f32[2,34,1]{2,1,0:T(8,128)S(1)}, u32[]{:S(2)}, u32[]{:S(2)}) collective-permute-start(f32[2,34,1]{2,1,0:T(8,128)S(1)} %get-tuple-element.68), channel_id=1, source_target_pairs={{1,0},{2,1},{3,2},{4,3},{5,4},{6,5},{7,6},{9,8},{10,9},{11,10},{12... | collective-permute-start | bytes 824 | tf_op jit(solution)/shard_map/ppermute | solution.py:19
  288.0 8.5 %collective-permute-start.63 = (f32[34,1]{1,0:T(8,128)S(1)}, f32[34,1]{1,0:T(8,128)S(1)}, u32[]{:S(2)}, u32[]{:S(2)}) collective-permute-start(f32[34,1]{1,0:T(8,128)S(1)} %get-tuple-element.100), channel_id=1, source_target_pairs={{0,1},{1,2},{2,3},{3,4},{4,5},{5,6},{6,7},{8,9},{9,10},{10,11},{11... | collective-permute-start | bytes 416 | tf_op jit(solution)/shard_map/ppermute | solution.py:17
  294.5 6.0 %collective-permute-start.62 = (f32[34,1]{1,0:T(8,128)S(1)}, f32[34,1]{1,0:T(8,128)S(1)}, u32[]{:S(2)}, u32[]{:S(2)}) collective-permute-start(f32[34,1]{1,0:T(8,128)S(1)} %get-tuple-element.99), channel_id=1, source_target_pairs={{1,0},{2,1},{3,2},{4,3},{5,4},{6,5},{7,6},{9,8},{10,9},{11,10},{12... | collective-permute-start | bytes 416 | tf_op jit(solution)/shard_map/ppermute | solution.py:19
  (49 other events, 523.0 us)
Sparse Core Ops, SparseCore 0:
  12.7 36.8 reduce-scatter.1
where the time goes:
time: 310 us; the launch traced here: 308 us
  starting transfers between devices  202 us (65%)
  waiting for transfers between devices  80.2 us (26%)
  between operations  15.3 us (5%)
  other arithmetic  5.58 us (2%)
  matrix products  3.53 us (1%)
    ppermute x32, starting transfers between devices, extended(): lax.ppermute(tail, axis, [(i, (i + 1) % count) for i in range(ends)])  138 us
    ppermute x32, starting transfers between devices, extended(): lax.ppermute(head, axis, [((i + 1) % count, i) for i in range(ends)])  64.2 us
    ppermute x32, waiting for transfers between devices, extended(): lax.ppermute(head, axis, [((i + 1) % count, i) for i in range(ends)])  34.9 us
    ppermute x32, waiting for transfers between devices, extended(): lax.ppermute(tail, axis, [(i, (i + 1) % count) for i in range(ends)])  23 us
    reduce_scatter x1, waiting for transfers between devices, local(): lax.psum_scatter(jnp.dot(select, partial_value, precision=highest), 'tile...  22.3 us
  transfers between devices with their start and end apart: 65, of which 33 were waited for; matrix products, arithmetic and copies ran while one was open for 0% of the time, Pallas kernels for 0%

commit v1 on v0

v1 whole, which is shorter than its diff:
```python
import functools

import jax
import jax.numpy as jnp
from jax import lax
from jax.experimental import pallas as pl
from jax.experimental.pallas import tpu as pltpu
from jax.sharding import PartitionSpec as P

NSUB = 8
HALO = 2 * NSUB
CAP = 4
LANES = 128
WET = 3
F32 = jnp.float32
BF16 = jnp.bfloat16
VMEM = pl.BlockSpec(memory_space=pltpu.VMEM)
SMEM = pl.BlockSpec(memory_space=pltpu.SMEM)
HBM = pl.BlockSpec(memory_space=pltpu.HBM)


def halves(x):
    high = x.astype(BF16)
    return high, (x - high.astype(F32)).astype(BF16)


def lanes_of(rows):
    return lax.broadcasted_iota(jnp.int32, (rows, LANES), 1)


def remap_kernel(
    flux_far, weight, tile_far, block_far, count_far, height, vel_x, vel_y, depth, mask,
    send, own, flux, stage, dest_tile, dest_block, count, sea_int, table, seen, sems,
):
    slots, blocks = dest_tile.shape
    fields, rows = flux.shape[0], height.shape[0]
    tiles = send.shape[0]
    base = CAP * fields
    moves = [(tile_far, dest_tile), (block_far, dest_block), (count_far, count)]
    moves += [(flux_far, flux), (mask, sea_int)]
    moves += [(x, own.at[q * rows : (q + 1) * rows]) for q, x in enumerate((height, vel_x, vel_y, depth))]
    moves += [(weight.at[b], stage.at[b]) for b in range(blocks)]
    copies = [pltpu.make_async_copy(x, y, sems.at[i]) for i, (x, y) in enumerate(moves)]
    for copy in copies:
        copy.start()
    for t in range(tiles):
        seen[t] = 0
        for r in range(CAP):
            table[t * CAP + r] = -1
        send[t, 0:base, :] = jnp.zeros((base, LANES), F32)
    for copy in copies[:3]:
        copy.wait()
    places = []
    for b in range(blocks):
        live = count[b]
        for k in range(slots):
            t = dest_tile[k, b]
            r = jnp.minimum(seen[t], CAP - 1)
            seen[t] = r + 1
            table[t * CAP + r] = jnp.where(k < live, dest_block[k, b], -1)
            places.append((t, r))
    for copy in copies[3:9]:
        copy.wait()
    state = [own[q * rows : (q + 1) * rows] for q in range(4)]
    sea = sea_int[...].astype(F32)
    own[4 * rows : 5 * rows] = sea
    lane16 = lanes_of(16)
    lane8 = lanes_of(8)
    row8 = lax.broadcasted_iota(jnp.int32, (8, LANES), 0)

    def edges(first):
        packed = jnp.zeros((16, LANES), F32)
        for half in range(2):
            for q in range(4):
                to = 64 * half + 16 * q
                moved = pltpu.roll(state[q][16 * half : 16 * half + 16], (to - first) % LANES, 1)
                packed = jnp.where((lane16 >= to) & (lane16 < to + 16), moved, packed)
        small = jnp.zeros((8, LANES), F32)
        for g in range(4):
            moved = pltpu.roll(sea[8 * g : 8 * g + 8], (16 * g - first) % LANES, 1)
            small = jnp.where((lane8 >= 16 * g) & (lane8 < 16 * g + 16), moved, small)
        return packed, small

    to_right = edges(LANES - HALO)
    to_left = edges(0)
    me = lax.axis_index("tile")

    for b in range(blocks):
        copies[9 + b].wait()
        high, low = halves(flux[:, b * LANES : (b + 1) * LANES])
        left = jnp.concatenate(
            [
                jnp.concatenate([high, low], axis=0),
                jnp.concatenate([high, jnp.zeros_like(low)], axis=0),
            ],
            axis=1,
        )
        for k in range(slots):
            w_high, w_low = halves(stage[b, k])
            both = jnp.dot(
                left, jnp.concatenate([w_high, w_low], axis=0), preferred_element_type=F32
            )
            t, r = places[b * slots + k]
            send[t, pl.ds(pl.multiple_of(r * fields, fields), fields), :] = both[:fields] + both[fields:]

    for t in range(tiles):
        toward_right = me < t
        packed = jnp.where(toward_right, to_right[0], to_left[0])
        small = jnp.where(toward_right, to_right[1], to_left[1])
        send[t, base : base + 16, :] = packed
        lefts, rights = max(t - 1, 0), min(t + 1, tiles - 1)
        out = small
        for f in range(WET):
            to = 64 + 16 * f
            part_l = send[lefts, pl.ds(f, CAP, stride=fields), :]
            part_r = send[rights, pl.ds(f, CAP, stride=fields), :]
            part_l = pltpu.roll(part_l, (to - (LANES - HALO)) % LANES, 1)
            part_r = pltpu.roll(part_r, to, 1)
            part = jnp.concatenate([part_l, part_r], axis=0)
            out = jnp.where((lane8 >= to) & (lane8 < to + 16), part, out)
        side = jnp.full((8, LANES), -1, jnp.int32)
        main = jnp.full((8, LANES), -1, jnp.int32)
        for r in range(CAP):
            if t > 0:
                side = jnp.where(row8 == r, table[lefts * CAP + r], side)
            if t < tiles - 1:
                named = table[rights * CAP + r]
                side = jnp.where(row8 == CAP + r, jnp.where(named < 0, -1, named + 32), side)
            main = jnp.where(row8 == r, table[t * CAP + r], main)
        out = jnp.where(lane8 == 112, side.astype(F32), out)
        out = jnp.where(lane8 == 113, main.astype(F32), out)
        send[t, base + 16 : base + 24, :] = out


def place_kernel(recv, state, forcing, wet_out, up, down, left, right, *, tiles):
    fields, rows = forcing.shape[:2]
    chunk = recv.shape[0] // tiles
    base = CAP * fields
    tail = base + 16
    names = jnp.concatenate([recv[pl.ds(tail + j, tiles, stride=chunk), :] for j in range(8)], axis=0)

    def one_hot(ids):
        lane = lanes_of(ids.shape[0]).astype(F32)
        return jnp.where(lane == ids, 1.0, 0.0).T

    hot_side = one_hot(names[:, 112:113])[: 2 * rows].astype(BF16)
    hot_main = one_hot(names[: CAP * tiles, 113:114])[:rows].astype(BF16)

    def spread(hot, values):
        high, low = halves(values)
        return jnp.dot(hot, high, preferred_element_type=F32) + jnp.dot(
            hot, low, preferred_element_type=F32
        )

    own = [state[q * rows : (q + 1) * rows] for q in range(5)]
    sea = own[4]
    for f in range(fields):
        values = jnp.concatenate(
            [recv[pl.ds(r * fields + f, tiles, stride=chunk), :] for r in range(CAP)], axis=0
        )
        grid = spread(hot_main, values) * sea
        forcing[f] = grid
        if f < WET:
            wet_out[f * rows : (f + 1) * rows] = grid
            own.append(grid)
    sides = spread(hot_side, names)
    lane = lanes_of(rows)
    me = lax.axis_index("tile")
    for which, out in ((0, left), (1, right)):
        source = jnp.maximum(me - 1, 0) if which == 0 else jnp.minimum(me + 1, tiles - 1)
        exists = (me > 0) if which == 0 else (me < tiles - 1)
        start = pl.multiple_of(source * chunk + base, 8)
        packed = recv[pl.ds(start, 16), :]
        small = recv[pl.ds(start + 16, 8), :]
        whole = jnp.concatenate([packed, pltpu.roll(packed, 64, 1)], axis=0)
        sea_part = jnp.concatenate(
            [pltpu.roll(small, (64 - 16 * g) % LANES, 1) for g in range(4)], axis=0
        )
        driven = pltpu.roll(sides[which * rows : (which + 1) * rows], 16, 1)
        full = jnp.where(lane < 64, whole, jnp.where(lane < 80, sea_part, driven))
        full = jnp.where(exists, full, 0.0)
        out[...] = full
        at = (5 + WET) * 16 + which * 16
        up[at : at + 16, :] = full[:16]
        down[at : at + 16, :] = full[rows - 16 :]
    for q, field in enumerate(own):
        up[16 * q : 16 * q + 16, :] = field[:16]
        down[16 * q : 16 * q + 16, :] = field[rows - 16 :]


def cycle_kernel(
    state, wet, left, right, above, below, height_out, flow_x, flow_y, *, comps
):
    rows = height_out.shape[0]
    total = rows + 2 * HALO
    count = 5 + WET
    own = [state[q * rows : (q + 1) * rows] for q in range(5)]
    own += [wet[f * rows : (f + 1) * rows] for f in range(WET)]
    at = count * 16
    side_l = jnp.concatenate([above[at : at + 16], left[...], below[at : at + 16]], axis=0)
    side_r = jnp.concatenate([above[at + 16 : at + 32], right[...], below[at + 16 : at + 32]], axis=0)
    lane = lanes_of(total)
    wide = []
    for q in range(count):
        center = jnp.concatenate(
            [above[16 * q : 16 * q + 16], own[q], below[16 * q : 16 * q + 16]], axis=0
        )
        from_l = pltpu.roll(side_l, (LANES - HALO - 16 * q) % LANES, 1)
        from_r = pltpu.roll(side_r, (LANES - 16 * q) % LANES, 1)
        side = jnp.where(lane < HALO, from_r, jnp.where(lane >= LANES - HALO, from_l, 0.0))
        wide.append(jnp.concatenate([center, side], axis=1))
    eta, u, v, deep, sea, push_x, push_y, rain = wide
    shape = (total, 2 * LANES)
    row = lax.axis_index("comp") * rows - HALO + lax.broadcasted_iota(jnp.int32, shape, 0)
    frac = row.astype(F32) / float(rows * comps)
    turn = (0.02 + 0.06 * frac) * sea
    inverse = jnp.where(deep > 0.0, 1.0 / jnp.where(deep > 0.0, deep, 1.0), 0.0)
    wind_x = sea * (0.05 * push_x * inverse)
    wind_y = sea * (0.05 * push_y * inverse)
    fresh = sea * (0.1 * rain)
    slope = 0.2 * sea
    deep = 0.2 * deep

    def cols(x):
        return pltpu.roll(x, 2 * LANES - 1, 1) - pltpu.roll(x, 1, 1)

    def lines(x):
        return pltpu.roll(x, total - 1, 0) - pltpu.roll(x, 1, 0)

    through_x, through_y = deep * u, deep * v
    eta, u, v = sea * eta, sea * u, sea * v
    for _ in range(NSUB):
        eta = eta + fresh - sea * (cols(through_x) + lines(through_y))
        next_u = 0.98 * u - slope * cols(eta) + turn * v + wind_x
        next_v = 0.98 * v - slope * lines(eta) - turn * u + wind_y
        u, v = next_u, next_v
        through_x, through_y = deep * u, deep * v
    height_out[...] = eta[HALO : HALO + rows, :LANES]
    flow_x[...] = u[HALO : HALO + rows, :LANES]
    flow_y[...] = v[HALO : HALO + rows, :LANES]


def local(tiles, comps, flux, weight, dest_tile, dest_block, count, height, vel_x, vel_y, depth, mask):
    fields = flux.shape[0]
    blocks, slots = dest_tile.shape
    rows, cols = height.shape
    chunk = CAP * fields + 24
    state = (height, vel_x, vel_y, depth, mask)
    plane = jax.ShapeDtypeStruct((rows, cols), F32)
    params = pltpu.CompilerParams(vmem_limit_bytes=16 * 1024 * 1024)

    def near(*shape):
        return pltpu.VMEM(shape, F32)

    def far(x):
        return pltpu.with_memory_space_constraint(x, pltpu.HBM)

    send, own = pl.pallas_call(
        remap_kernel,
        out_shape=[near(tiles, chunk, LANES), near(5 * rows, cols)],
        in_specs=[HBM] * 10,
        out_specs=[VMEM] * 2,
        scratch_shapes=[
            pltpu.VMEM(flux.shape, F32),
            pltpu.VMEM(weight.shape, F32),
            pltpu.SMEM((slots, blocks), jnp.int32),
            pltpu.SMEM((slots, blocks), jnp.int32),
            pltpu.SMEM((blocks,), jnp.int32),
            pltpu.VMEM((rows, cols), jnp.int32),
            pltpu.SMEM((tiles * CAP,), jnp.int32),
            pltpu.SMEM((tiles,), jnp.int32),
            pltpu.SemaphoreType.DMA((9 + blocks,)),
        ],
        compiler_params=params,
        name="remap",
    )(*map(far, (flux, weight, dest_tile.T, dest_block.T, count, *state)))
    recv = lax.all_to_all(send, "tile", 0, 0, tiled=True).reshape(tiles * chunk, LANES)
    message = near((5 + WET + 2) * 16, LANES)
    forcing, wet, up, down, left, right = pl.pallas_call(
        functools.partial(place_kernel, tiles=tiles),
        out_shape=[
            jax.ShapeDtypeStruct((fields, rows, cols), F32), near(WET * rows, cols),
            message, message, near(rows, cols), near(rows, cols),
        ],
        in_specs=[VMEM] * 2,
        out_specs=[VMEM] * 6,
        compiler_params=params,
        name="place",
    )(recv, own)
    above = lax.ppermute(down, "comp", [(i, i + 1) for i in range(comps - 1)])
    below = lax.ppermute(up, "comp", [(i + 1, i) for i in range(comps - 1)])
    outs = pl.pallas_call(
        functools.partial(cycle_kernel, comps=comps),
        out_shape=[plane] * 3,
        in_specs=[VMEM] * 6,
        out_specs=[VMEM] * 3,
        compiler_params=params,
        name="cycles",
    )(own, wet, left, right, above, below)
    return (forcing, *outs)


def solution(mesh):
    both = ("comp", "tile")
    grid = P("comp", "tile")
    in_specs = (P(None, both), P(both, None, None, None), P(both, None), P(both, None), P(both)) + (grid,) * 5
    out_specs = (P(None, "comp", "tile"), grid, grid, grid)
    body = functools.partial(local, mesh.shape["tile"], mesh.shape["comp"])
    return jax.shard_map(body, mesh=mesh, in_specs=in_specs, out_specs=out_specs, check_vma=False)
```

time: 310 us -> 28 us (0.09)
  the two profiles are of different devices: /device:TPU:19 before, /device:TPU:0 now
where the time goes in v1:
time: 28 us; the launch traced here: 27.7 us
  blocking collectives  11.6 us (41%)
  Pallas kernels  5.69 us (20%)
  waiting for transfers between devices  5.03 us (18%)
  starting transfers between devices  4.76 us (17%)
  between operations  0.66 us (2%)
    all_to_all x1, blocking collectives, local(): lax.all_to_all(send, 'tile', 0, 0, tiled=True).reshape(tiles * chunk, LANES)  11.6 us
    ppermute x1, waiting for transfers between devices, local(): below = lax.ppermute(up, 'comp', [(i + 1, i) for i in range(comps - 1)])  4.3 us
    ppermute x1, starting transfers between devices, local(): above = lax.ppermute(down, 'comp', [(i, i + 1) for i in range(comps - 1)])  3.47 us
    pallas_call x1, Pallas kernels, local(): pl.pallas_call(remap_kernel, out_shape=[near(tiles, chunk, LANES), near(5...  2.59 us
    pallas_call x1, Pallas kernels, local(): pl.pallas_call(functools.partial(cycle_kernel, comps=comps), out_shape=[p...  2.13 us
    ppermute x1, starting transfers between devices, local(): below = lax.ppermute(up, 'comp', [(i + 1, i) for i in range(comps - 1)])  1.29 us
    pallas_call x1, Pallas kernels, local(): pl.pallas_call(functools.partial(place_kernel, tiles=tiles), out_shape=[j...  0.97 us
    ppermute x1, waiting for transfers between devices, local(): above = lax.ppermute(down, 'comp', [(i, i + 1) for i in range(comps - 1)])  0.74 us
  transfers between devices with their start and end apart: 2, of which 2 were waited for; matrix products, arithmetic and copies ran while one was open for 0% of the time, Pallas kernels for 0%

profile of v1, /device:TPU:0, one launch (start us, length us, event | category | flops | bytes accessed | tf_op | source)
XLA Modules:
  0.0 27.7 jit_solution(9820943289748247484)
XLA Ops:
  0.6 2.6 %remap.1 = (f32[8,56,128]{2,1,0:T(8,128)S(1)}, f32[160,128]{1,0:T(8,128)S(1)}) custom-call(f32[8,1024]{1,0:T(8,128)} %flux_far.1, f32[8,4,128,128]{3,2,1,0:T(8,128)} %weight.1, s32[4,8]{1,0:T(4,128)} %bitcast.4, s32[4,8]{1,0:T(4,128)} %bitcast.5, s32[8]{0:T(128)} %count_far.1, f32[32,128]{1,0:T(8,128)} %height.1, f32[32,128]{1,0:T(8,128)} %vel_x.1, ...), custom_call_target="tpu_custom_call" | custom-call | tf_op jit(solution)/shard_map/remap/pallas_call | solution.py:258
  3.2 11.6 %all_to_all.5 = f32[8,56,128]{2,1,0:T(8,128)S(1)} all-to-all(f32[8,56,128]{2,1,0:T(8,128)S(1)} %get-tuple-element.15), channel_id=1, replica_groups=mesh['comp'=4,'tile'=8] {'tile'}, dimensions={0} | all-to-all | bytes 458752 | tf_op jit(solution)/shard_map/all_to_all | solution.py:277
  14.8 1.0 %place.1 = (f32[8,32,128]{2,1,0:T(8,128)}, f32[96,128]{1,0:T(8,128)S(1)}, f32[160,128]{1,0:T(8,128)S(1)}, f32[160,128]{1,0:T(8,128)S(1)}, f32[32,128]{1,0:T(8,128)S(1)}, /*index=5*/f32[32,128]{1,0:T(8,128)S(1)}) custom-call(f32[448,128]{1,0:T(8,128)S(1)} %bitcast.3, f32[160,128]{1,0:T(8,128)S(1)} %get-tuple-element.16.state), custom_call_target="tpu_custom_call" | custom-call | tf_op jit(solution)/shard_map/place/pallas_call | solution.py:279
  15.8 3.5 %collective-permute-start = (f32[160,128]{1,0:T(8,128)S(1)}, f32[160,128]{1,0:T(8,128)S(1)}, u32[]{:S(2)}, u32[]{:S(2)}) collective-permute-start(f32[160,128]{1,0:T(8,128)S(1)} %get-tuple-element.21), channel_id=1, source_target_pairs={{0,8},{8,16},{16,24},{1,9},{9,17},{17,25},{2,10},{10,18},{18,26},{... | collective-permute-start | bytes 245768 | tf_op jit(solution)/shard_map/ppermute | solution.py:290
  19.2 1.3 %collective-permute-start.1 = (f32[160,128]{1,0:T(8,128)S(1)}, f32[160,128]{1,0:T(8,128)S(1)}, u32[]{:S(2)}, u32[]{:S(2)}) collective-permute-start(f32[160,128]{1,0:T(8,128)S(1)} %get-tuple-element.22), channel_id=1, source_target_pairs={{8,0},{16,8},{24,16},{9,1},{17,9},{25,17},{10,2},{18,10},{26,18},{... | collective-permute-start | bytes 245768 | tf_op jit(solution)/shard_map/ppermute | solution.py:291
  20.5 0.7 %collective-permute-done.above = f32[160,128]{1,0:T(8,128)S(1)} collective-permute-done((f32[160,128]{1,0:T(8,128)S(1)}, f32[160,128]{1,0:T(8,128)S(1)}, u32[]{:S(2)}, u32[]{:S(2)}) %collective-permute-start) | collective-permute-done | bytes 81952 | tf_op jit(solution)/shard_map/ppermute | solution.py:290
  21.3 4.3 %collective-permute-done.1.below = f32[160,128]{1,0:T(8,128)S(1)} collective-permute-done((f32[160,128]{1,0:T(8,128)S(1)}, f32[160,128]{1,0:T(8,128)S(1)}, u32[]{:S(2)}, u32[]{:S(2)}) %collective-permute-start.1) | collective-permute-done | bytes 81952 | tf_op jit(solution)/shard_map/ppermute | solution.py:291
  25.6 2.1 %cycles.1 = (f32[32,128]{1,0:T(8,128)}, f32[32,128]{1,0:T(8,128)}, f32[32,128]{1,0:T(8,128)}) custom-call(f32[160,128]{1,0:T(8,128)S(1)} %get-tuple-element.16.state, f32[96,128]{1,0:T(8,128)S(1)} %get-tuple-element.18.wet, f32[32,128]{1,0:T(8,128)S(1)} %get-tuple-element.19.left, f32[32,128]{1,0:T(8,128)S(1)} %get-tuple-element.20.right, ...), custom_call_target="tpu_custom_call" | custom-call | tf_op jit(solution)/shard_map/cycles/pallas_call | solution.py:292
Async XLA Ops:
  15.8 5.5 %collective-permute-start = (f32[160,128]{1,0:T(8,128)S(1)}, f32[160,128]{1,0:T(8,128)S(1)}, u32[]{:S(2)}, u32[]{:S(2)}) collective-permute-start(f32[160,128]{1,0:T(8,128)S(1)} %get-tuple-element.21), channel_id=1, source_target_pairs={{0,8},{8,16},{16,24},{1,9},{9,17},{17,25},{2,10},{10,18},{18,26},{... | collective-permute-start | bytes 245768 | tf_op jit(solution)/shard_map/ppermute | solution.py:290
  19.2 6.3 %collective-permute-start.1 = (f32[160,128]{1,0:T(8,128)S(1)}, f32[160,128]{1,0:T(8,128)S(1)}, u32[]{:S(2)}, u32[]{:S(2)}) collective-permute-start(f32[160,128]{1,0:T(8,128)S(1)} %get-tuple-element.22), channel_id=1, source_target_pairs={{8,0},{16,8},{24,16},{9,1},{17,9},{25,17},{10,2},{18,10},{26,18},{... | collective-permute-start | bytes 245768 | tf_op jit(solution)/shard_map/ppermute | solution.py:291

commit v2 on v1

--- a/solution.py
+++ b/solution.py
@@ -132,7 +132,7 @@
         send[t, base + 16 : base + 24, :] = out
 
 
-def place_kernel(recv, state, forcing, wet_out, up, down, left, right, *, tiles):
+def place_kernel(recv, state, forcing, wet, first, second, left, right, *, tiles):
     fields, rows = forcing.shape[:2]
     chunk = recv.shape[0] // tiles
     base = CAP * fields
@@ -152,8 +152,7 @@
             hot, low, preferred_element_type=F32
         )
 
-    own = [state[q * rows : (q + 1) * rows] for q in range(5)]
-    sea = own[4]
+    sea = state[4 * rows : 5 * rows]
     for f in range(fields):
         values = jnp.concatenate(
             [recv[pl.ds(r * fields + f, tiles, stride=chunk), :] for r in range(CAP)], axis=0
@@ -161,8 +160,7 @@
         grid = spread(hot_main, values) * sea
         forcing[f] = grid
         if f < WET:
-            wet_out[f * rows : (f + 1) * rows] = grid
-            own.append(grid)
+            wet[f * rows : (f + 1) * rows] = grid
     sides = spread(hot_side, names)
     lane = lanes_of(rows)
     me = lax.axis_index("tile")
@@ -180,18 +178,21 @@
         full = jnp.where(lane < 64, whole, jnp.where(lane < 80, sea_part, driven))
         full = jnp.where(exists, full, 0.0)
         out[...] = full
-        at = (5 + WET) * 16 + which * 16
-        up[at : at + 16, :] = full[:16]
-        down[at : at + 16, :] = full[rows - 16 :]
-    for q, field in enumerate(own):
-        up[16 * q : 16 * q + 16, :] = field[:16]
-        down[16 * q : 16 * q + 16, :] = field[rows - 16 :]
+    even = lax.axis_index("comp") % 2 == 0
+    for message, low in ((first, even), (second, jnp.logical_not(even))):
+        start = pl.multiple_of(jnp.where(low, rows - HALO, 0), 8)
+        parts = [(state, q) for q in range(5)] + [(wet, f) for f in range(WET)] + [(left, 0), (right, 0)]
+        for i, (ref, q) in enumerate(parts):
+            message[i * HALO : (i + 1) * HALO, :] = ref[pl.ds(q * rows + start, HALO), :]
 
 
 def cycle_kernel(
-    state, wet, left, right, above, below, height_out, flow_x, flow_y, *, comps
+    state, wet, left, right, first, second, height_out, flow_x, flow_y, *, comps
 ):
     rows = height_out.shape[0]
+    even = lax.axis_index("comp") % 2 == 0
+    first, second = first[...], second[...]
+    above, below = jnp.where(even, second, first), jnp.where(even, first, second)
     total = rows + 2 * HALO
     count = 5 + WET
     own = [state[q * rows : (q + 1) * rows] for q in range(5)]
@@ -212,6 +213,8 @@
     eta, u, v, deep, sea, push_x, push_y, rain = wide
     shape = (total, 2 * LANES)
     row = lax.axis_index("comp") * rows - HALO + lax.broadcasted_iota(jnp.int32, shape, 0)
+    inside = (row >= 0) & (row < rows * comps)
+    deep, sea = jnp.where(inside, deep, 0.0), jnp.where(inside, sea, 0.0)
     frac = row.astype(F32) / float(rows * comps)
     turn = (0.02 + 0.06 * frac) * sea
     inverse = jnp.where(deep > 0.0, 1.0 / jnp.where(deep > 0.0, deep, 1.0), 0.0)
@@ -238,6 +241,16 @@
     height_out[...] = eta[HALO : HALO + rows, :LANES]
     flow_x[...] = u[HALO : HALO + rows, :LANES]
     flow_y[...] = v[HALO : HALO + rows, :LANES]
+
+
+def swaps(parity, comps, tiles):
+    pairs = []
+    for s in range(comps):
+        other = s + 1 if s % 2 == parity else s - 1
+        for t in range(tiles):
+            there = other * tiles + t if 0 <= other < comps else s * tiles + (t ^ 1)
+            pairs.append((s * tiles + t, there))
+    return pairs
 
 
 def local(tiles, comps, flux, weight, dest_tile, dest_block, count, height, vel_x, vel_y, depth, mask):
@@ -276,7 +289,7 @@
     )(*map(far, (flux, weight, dest_tile.T, dest_block.T, count, *state)))
     recv = lax.all_to_all(send, "tile", 0, 0, tiled=True).reshape(tiles * chunk, LANES)
     message = near((5 + WET + 2) * 16, LANES)
-    forcing, wet, up, down, left, right = pl.pallas_call(
+    forcing, wet, first, second, left, right = pl.pallas_call(
         functools.partial(place_kernel, tiles=tiles),
         out_shape=[
             jax.ShapeDtypeStruct((fields, rows, cols), F32), near(WET * rows, cols),
@@ -287,8 +300,10 @@
         compiler_params=params,
         name="place",
     )(recv, own)
-    above = lax.ppermute(down, "comp", [(i, i + 1) for i in range(comps - 1)])
-    below = lax.ppermute(up, "comp", [(i + 1, i) for i in range(comps - 1)])
+    received = [
+        lax.ppermute(x, ("comp", "tile"), swaps(parity, comps, tiles))
+        for parity, x in enumerate((first, second))
+    ]
     outs = pl.pallas_call(
         functools.partial(cycle_kernel, comps=comps),
         out_shape=[plane] * 3,
@@ -296,7 +311,7 @@
         out_specs=[VMEM] * 3,
         compiler_params=params,
         name="cycles",
-    )(own, wet, left, right, above, below)
+    )(own, wet, left, right, *received)
     return (forcing, *outs)
 
 

time: 28 us -> 22.7 us (0.81)
  starting transfers between devices: 4.76 us -> 1.58 us
  waiting for transfers between devices: 5.03 us -> 2.86 us
    ppermute x2, starting transfers between devices: 4.76 us -> 1.58 us  [local(): lax.ppermute(x, ('comp', 'tile'), swaps(parity, comps, tiles))]
    ppermute x2, waiting for transfers between devices: 5.03 us -> 2.86 us  [local(): lax.ppermute(x, ('comp', 'tile'), swaps(parity, comps, tiles))]
  transfers between devices with their start and end apart: 2 -> 2, of which waited for: 2 -> 1; matrix products, arithmetic and copies ran while one was open for 0% -> 0% of each run, Pallas kernels for 0% -> 0%
where the time goes in v2:
time: 22.7 us; the launch traced here: 22.3 us
  blocking collectives  11.6 us (51%)
  Pallas kernels  5.7 us (25%)
  waiting for transfers between devices  2.86 us (13%)
  starting transfers between devices  1.58 us (7%)
  between operations  0.65 us (3%)
    all_to_all x1, blocking collectives, local(): lax.all_to_all(send, 'tile', 0, 0, tiled=True).reshape(tiles * chunk, LANES)  11.6 us
    ppermute x2, waiting for transfers between devices, local(): lax.ppermute(x, ('comp', 'tile'), swaps(parity, comps, tiles))  2.86 us
    pallas_call x1, Pallas kernels, local(): pl.pallas_call(remap_kernel, out_shape=[near(tiles, chunk, LANES), near(5...  2.59 us
    pallas_call x1, Pallas kernels, local(): pl.pallas_call(functools.partial(cycle_kernel, comps=comps), out_shape=[p...  2.13 us
    ppermute x2, starting transfers between devices, local(): lax.ppermute(x, ('comp', 'tile'), swaps(parity, comps, tiles))  1.58 us
    pallas_call x1, Pallas kernels, local(): pl.pallas_call(functools.partial(place_kernel, tiles=tiles), out_shape=[j...  0.97 us
  transfers between devices with their start and end apart: 2, of which 1 were waited for; matrix products, arithmetic and copies ran while one was open for 0% of the time, Pallas kernels for 0%

profile of v2, /device:TPU:0, one launch (start us, length us, event | category | flops | bytes accessed | tf_op | source)
XLA Modules:
  0.0 22.3 jit_solution(4863142964114557308)
XLA Ops:
  0.6 2.6 %remap.1 = (f32[8,56,128]{2,1,0:T(8,128)S(1)}, f32[160,128]{1,0:T(8,128)S(1)}) custom-call(f32[8,1024]{1,0:T(8,128)} %flux_far.1, f32[8,4,128,128]{3,2,1,0:T(8,128)} %weight.1, s32[4,8]{1,0:T(4,128)} %bitcast.4, s32[4,8]{1,0:T(4,128)} %bitcast.5, s32[8]{0:T(128)} %count_far.1, f32[32,128]{1,0:T(8,128)} %height.1, f32[32,128]{1,0:T(8,128)} %vel_x.1, ...), custom_call_target="tpu_custom_call" | custom-call | tf_op jit(solution)/shard_map/remap/pallas_call | solution.py:271
  3.2 11.6 %all_to_all.5 = f32[8,56,128]{2,1,0:T(8,128)S(1)} all-to-all(f32[8,56,128]{2,1,0:T(8,128)S(1)} %get-tuple-element.15), channel_id=1, replica_groups=mesh['comp'=4,'tile'=8] {'tile'}, dimensions={0} | all-to-all | bytes 458752 | tf_op jit(solution)/shard_map/all_to_all | solution.py:290
  14.8 1.0 %place.1 = (f32[8,32,128]{2,1,0:T(8,128)}, f32[96,128]{1,0:T(8,128)S(1)}, f32[160,128]{1,0:T(8,128)S(1)}, f32[160,128]{1,0:T(8,128)S(1)}, f32[32,128]{1,0:T(8,128)S(1)}, /*index=5*/f32[32,128]{1,0:T(8,128)S(1)}) custom-call(f32[448,128]{1,0:T(8,128)S(1)} %bitcast.3, f32[160,128]{1,0:T(8,128)S(1)} %get-tuple-element.16.state), custom_call_target="tpu_custom_call" | custom-call | tf_op jit(solution)/shard_map/place/pallas_call | solution.py:292
  15.8 1.6 %collective-permute-start = (f32[160,128]{1,0:T(8,128)S(1)}, f32[160,128]{1,0:T(8,128)S(1)}, u32[]{:S(2)}, u32[]{:S(2)}) collective-permute-start(f32[160,128]{1,0:T(8,128)S(1)} %get-tuple-element.21), channel_id=1, source_target_pairs={{0,8},{1,9},{2,10},{3,11},{4,12},{5,13},{6,14},{7,15},{8,0},{9,1},... | collective-permute-start | bytes 245768 | tf_op jit(solution)/shard_map/ppermute | solution.py:304
  17.3 0.0 collective-permute-start.1
  17.3 2.9 %collective-permute-done.first = f32[160,128]{1,0:T(8,128)S(1)} collective-permute-done((f32[160,128]{1,0:T(8,128)S(1)}, f32[160,128]{1,0:T(8,128)S(1)}, u32[]{:S(2)}, u32[]{:S(2)}) %collective-permute-start) | collective-permute-done | bytes 81952 | tf_op jit(solution)/shard_map/ppermute | solution.py:304
  20.2 0.0 collective-permute-done.1.second
  20.2 2.1 %cycles.1 = (f32[32,128]{1,0:T(8,128)}, f32[32,128]{1,0:T(8,128)}, f32[32,128]{1,0:T(8,128)}) custom-call(f32[160,128]{1,0:T(8,128)S(1)} %get-tuple-element.16.state, f32[96,128]{1,0:T(8,128)S(1)} %get-tuple-element.18.wet, f32[32,128]{1,0:T(8,128)S(1)} %get-tuple-element.19.left, f32[32,128]{1,0:T(8,128)S(1)} %get-tuple-element.20.right, ...), custom_call_target="tpu_custom_call" | custom-call | tf_op jit(solution)/shard_map/cycles/pallas_call | solution.py:307
Async XLA Ops:
  15.8 4.4 %collective-permute-start = (f32[160,128]{1,0:T(8,128)S(1)}, f32[160,128]{1,0:T(8,128)S(1)}, u32[]{:S(2)}, u32[]{:S(2)}) collective-permute-start(f32[160,128]{1,0:T(8,128)S(1)} %get-tuple-element.21), channel_id=1, source_target_pairs={{0,8},{1,9},{2,10},{3,11},{4,12},{5,13},{6,14},{7,15},{8,0},{9,1},... | collective-permute-start | bytes 245768 | tf_op jit(solution)/shard_map/ppermute | solution.py:304
  17.3 2.9 %collective-permute-start.1 = (f32[160,128]{1,0:T(8,128)S(1)}, f32[160,128]{1,0:T(8,128)S(1)}, u32[]{:S(2)}, u32[]{:S(2)}) collective-permute-start(f32[160,128]{1,0:T(8,128)S(1)} %get-tuple-element.22), channel_id=1, source_target_pairs={{0,1},{1,0},{2,3},{3,2},{4,5},{5,4},{6,7},{7,6},{8,16},{9,17},{10,... | collective-permute-start | bytes 245768 | tf_op jit(solution)/shard_map/ppermute | solution.py:304

commit v3 on v2

--- a/solution.py
+++ b/solution.py
@@ -86,7 +86,9 @@
     me = lax.axis_index("tile")
 
     for b in range(blocks):
-        copies[9 + b].wait()
+        if b % (blocks // 2) == 0:
+            for copy in copies[9 + b : 9 + b + blocks // 2]:
+                copy.wait()
         high, low = halves(flux[:, b * LANES : (b + 1) * LANES])
         left = jnp.concatenate(
             [
@@ -132,35 +134,45 @@
         send[t, base + 16 : base + 24, :] = out
 
 
-def place_kernel(recv, state, forcing, wet, first, second, left, right, *, tiles):
+def spread(hot, values):
+    high, low = halves(values)
+    return jnp.dot(hot, high, preferred_element_type=F32) + jnp.dot(hot, low, preferred_element_type=F32)
+
+
+def one_hot(ids):
+    lane = lanes_of(ids.shape[0]).astype(F32)
+    return jnp.where(lane == ids, 1.0, 0.0).T.astype(BF16)
+
+
+def slots_of(recv, row, tiles, count):
+    chunk = recv.shape[0] // tiles
+    return [recv[pl.ds(row + j, tiles, stride=chunk), :] for j in range(count)]
+
+
+def field_values(recv, f, fields, tiles):
+    chunk = recv.shape[0] // tiles
+    return jnp.concatenate([recv[pl.ds(r * fields + f, tiles, stride=chunk), :] for r in range(CAP)], axis=0)
+
+
+def forcing_kernel(recv, state, forcing, *, tiles):
     fields, rows = forcing.shape[:2]
+    names = jnp.concatenate(slots_of(recv, CAP * fields + 16, tiles, CAP), axis=0)
+    hot = one_hot(names[:, 113:114])[:rows]
+    sea = state[4 * rows : 5 * rows]
+    for f in range(fields):
+        forcing[f] = spread(hot, field_values(recv, f, fields, tiles)) * sea
+
+
+def place_kernel(recv, state, wet, first, second, left, right, *, tiles, fields):
+    rows = left.shape[0]
     chunk = recv.shape[0] // tiles
     base = CAP * fields
-    tail = base + 16
-    names = jnp.concatenate([recv[pl.ds(tail + j, tiles, stride=chunk), :] for j in range(8)], axis=0)
-
-    def one_hot(ids):
-        lane = lanes_of(ids.shape[0]).astype(F32)
-        return jnp.where(lane == ids, 1.0, 0.0).T
-
-    hot_side = one_hot(names[:, 112:113])[: 2 * rows].astype(BF16)
-    hot_main = one_hot(names[: CAP * tiles, 113:114])[:rows].astype(BF16)
-
-    def spread(hot, values):
-        high, low = halves(values)
-        return jnp.dot(hot, high, preferred_element_type=F32) + jnp.dot(
-            hot, low, preferred_element_type=F32
-        )
-
+    names = jnp.concatenate(slots_of(recv, base + 16, tiles, 8), axis=0)
+    hot_side = one_hot(names[:, 112:113])[: 2 * rows]
+    hot_main = one_hot(names[: CAP * tiles, 113:114])[:rows]
     sea = state[4 * rows : 5 * rows]
-    for f in range(fields):
-        values = jnp.concatenate(
-            [recv[pl.ds(r * fields + f, tiles, stride=chunk), :] for r in range(CAP)], axis=0
-        )
-        grid = spread(hot_main, values) * sea
-        forcing[f] = grid
-        if f < WET:
-            wet[f * rows : (f + 1) * rows] = grid
+    for f in range(WET):
+        wet[f * rows : (f + 1) * rows] = spread(hot_main, field_values(recv, f, fields, tiles)) * sea
     sides = spread(hot_side, names)
     lane = lanes_of(rows)
     me = lax.axis_index("tile")
@@ -289,14 +301,11 @@
     )(*map(far, (flux, weight, dest_tile.T, dest_block.T, count, *state)))
     recv = lax.all_to_all(send, "tile", 0, 0, tiled=True).reshape(tiles * chunk, LANES)
     message = near((5 + WET + 2) * 16, LANES)
-    forcing, wet, first, second, left, right = pl.pallas_call(
-        functools.partial(place_kernel, tiles=tiles),
-        out_shape=[
-            jax.ShapeDtypeStruct((fields, rows, cols), F32), near(WET * rows, cols),
-            message, message, near(rows, cols), near(rows, cols),
-        ],
+    wet, first, second, left, right = pl.pallas_call(
+        functools.partial(place_kernel, tiles=tiles, fields=fields),
+        out_shape=[near(WET * rows, cols), message, message, near(rows, cols), near(rows, cols)],
         in_specs=[VMEM] * 2,
-        out_specs=[VMEM] * 6,
+        out_specs=[VMEM] * 5,
         compiler_params=params,
         name="place",
     )(recv, own)
@@ -304,6 +313,15 @@
         lax.ppermute(x, ("comp", "tile"), swaps(parity, comps, tiles))
         for parity, x in enumerate((first, second))
     ]
+    forcing = pl.pallas_call(
+        functools.partial(forcing_kernel, tiles=tiles),
+        out_shape=jax.ShapeDtypeStruct((fields, rows, cols), F32),
+        in_specs=[VMEM] * 2,
+        out_specs=VMEM,
+        compiler_params=params,
+        cost_estimate=pl.CostEstimate(flops=10**8, bytes_accessed=4 * 2**20, transcendentals=0),
+        name="forcing",
+    )(recv, own)
     outs = pl.pallas_call(
         functools.partial(cycle_kernel, comps=comps),
         out_shape=[plane] * 3,

time: 22.7 us -> 21.7 us (0.956)
  waiting for transfers between devices: 2.86 us -> 1.9 us
    ppermute x2, waiting for transfers between devices: 2.86 us -> 1.9 us  [local(): lax.ppermute(x, ('comp', 'tile'), swaps(parity, comps, tiles))]
    pallas_call x1, Pallas kernels: 2.59 us -> 2.14 us  [local(): pl.pallas_call(remap_kernel, out_shape=[near(tiles, chunk, LANES), near(5...]
    pallas_call x1 -> x2, Pallas kernels: 0.97 us -> 1.33 us  [the longest x1 0.97 us: local(): pl.pallas_call(functools.partial(forcing_kernel, tiles=tiles), out_shape=...]
  transfers between devices with their start and end apart: 2 -> 2, of which waited for: 1 -> 1; matrix products, arithmetic and copies ran while one was open for 0% -> 0% of each run, Pallas kernels for 0% -> 5%
where the time goes in v3:
time: 21.7 us; the launch traced here: 21.4 us
  blocking collectives  11.6 us (53%)
  Pallas kernels  5.61 us (26%)
  waiting for transfers between devices  1.9 us (9%)
  starting transfers between devices  1.64 us (8%)
  between operations  0.65 us (3%)
    all_to_all x1, blocking collectives, local(): lax.all_to_all(send, 'tile', 0, 0, tiled=True).reshape(tiles * chunk, LANES)  11.6 us
    pallas_call x1, Pallas kernels, local(): pl.pallas_call(remap_kernel, out_shape=[near(tiles, chunk, LANES), near(5...  2.14 us
    pallas_call x1, Pallas kernels, local(): pl.pallas_call(functools.partial(cycle_kernel, comps=comps), out_shape=[p...  2.13 us
    ppermute x2, waiting for transfers between devices, local(): lax.ppermute(x, ('comp', 'tile'), swaps(parity, comps, tiles))  1.9 us
    ppermute x2, starting transfers between devices, local(): lax.ppermute(x, ('comp', 'tile'), swaps(parity, comps, tiles))  1.64 us
    pallas_call x1, Pallas kernels, local(): pl.pallas_call(functools.partial(forcing_kernel, tiles=tiles), out_shape=...  0.97 us
  transfers between devices with their start and end apart: 2, of which 1 were waited for; matrix products, arithmetic and copies ran while one was open for 0% of the time, Pallas kernels for 5%

profile of v3, /device:TPU:0, one launch (start us, length us, event | category | flops | bytes accessed | tf_op | source)
XLA Modules:
  0.0 21.4 jit_solution(2181878128887690038)
XLA Ops:
  0.6 2.1 %remap.1 = (f32[8,56,128]{2,1,0:T(8,128)S(1)}, f32[160,128]{1,0:T(8,128)S(1)}) custom-call(f32[8,1024]{1,0:T(8,128)} %flux_far.1, f32[8,4,128,128]{3,2,1,0:T(8,128)} %weight.1, s32[4,8]{1,0:T(4,128)} %bitcast.5, s32[4,8]{1,0:T(4,128)} %bitcast.6, s32[8]{0:T(128)} %count_far.1, f32[32,128]{1,0:T(8,128)} %height.1, f32[32,128]{1,0:T(8,128)} %vel_x.1, ...), custom_call_target="tpu_custom_call" | custom-call | tf_op jit(solution)/shard_map/remap/pallas_call | solution.py:283
  2.8 11.6 %all_to_all.5 = f32[8,56,128]{2,1,0:T(8,128)S(1)} all-to-all(f32[8,56,128]{2,1,0:T(8,128)S(1)} %get-tuple-element.14), channel_id=1, replica_groups=mesh['comp'=4,'tile'=8] {'tile'}, dimensions={0} | all-to-all | bytes 458752 | tf_op jit(solution)/shard_map/all_to_all | solution.py:302
  14.3 0.4 %place.1 = (f32[96,128]{1,0:T(8,128)S(1)}, f32[160,128]{1,0:T(8,128)S(1)}, f32[160,128]{1,0:T(8,128)S(1)}, f32[32,128]{1,0:T(8,128)S(1)}, f32[32,128]{1,0:T(8,128)S(1)}) custom-call(f32[448,128]{1,0:T(8,128)S(1)} %bitcast.3, f32[160,128]{1,0:T(8,128)S(1)} %get-tuple-element.15.state), custom_call_target="tpu_custom_call" | custom-call | tf_op jit(solution)/shard_map/place/pallas_call | solution.py:304
  14.7 1.6 %collective-permute-start = (f32[160,128]{1,0:T(8,128)S(1)}, f32[160,128]{1,0:T(8,128)S(1)}, u32[]{:S(2)}, u32[]{:S(2)}) collective-permute-start(f32[160,128]{1,0:T(8,128)S(1)} %get-tuple-element.19), channel_id=1, source_target_pairs={{0,8},{1,9},{2,10},{3,11},{4,12},{5,13},{6,14},{7,15},{8,0},{9,1},... | collective-permute-start | bytes 245768 | tf_op jit(solution)/shard_map/ppermute | solution.py:313
  16.3 0.0 collective-permute-start.1
  16.4 1.0 %forcing.1 = f32[8,32,128]{2,1,0:T(8,128)} custom-call(f32[448,128]{1,0:T(8,128)S(1)} %bitcast.4, f32[160,128]{1,0:T(8,128)S(1)} %get-tuple-element.15.state), custom_call_target="tpu_custom_call" | custom-call | flops 100000000 | bytes 4194304 | tf_op jit(solution)/shard_map/forcing/pallas_call | solution.py:316
  17.3 1.9 %collective-permute-done.first = f32[160,128]{1,0:T(8,128)S(1)} collective-permute-done((f32[160,128]{1,0:T(8,128)S(1)}, f32[160,128]{1,0:T(8,128)S(1)}, u32[]{:S(2)}, u32[]{:S(2)}) %collective-permute-start) | collective-permute-done | bytes 81952 | tf_op jit(solution)/shard_map/ppermute | solution.py:313
  19.2 0.0 collective-permute-done.1.second
  19.2 2.1 %cycles.1 = (f32[32,128]{1,0:T(8,128)}, f32[32,128]{1,0:T(8,128)}, f32[32,128]{1,0:T(8,128)}) custom-call(f32[160,128]{1,0:T(8,128)S(1)} %get-tuple-element.15.state, f32[96,128]{1,0:T(8,128)S(1)} %get-tuple-element.16.wet, f32[32,128]{1,0:T(8,128)S(1)} %get-tuple-element.17.left, f32[32,128]{1,0:T(8,128)S(1)} %get-tuple-element.18.right, ...), custom_call_target="tpu_custom_call" | custom-call | tf_op jit(solution)/shard_map/cycles/pallas_call | solution.py:325
Async XLA Ops:
  14.7 4.5 %collective-permute-start = (f32[160,128]{1,0:T(8,128)S(1)}, f32[160,128]{1,0:T(8,128)S(1)}, u32[]{:S(2)}, u32[]{:S(2)}) collective-permute-start(f32[160,128]{1,0:T(8,128)S(1)} %get-tuple-element.19), channel_id=1, source_target_pairs={{0,8},{1,9},{2,10},{3,11},{4,12},{5,13},{6,14},{7,15},{8,0},{9,1},... | collective-permute-start | bytes 245768 | tf_op jit(solution)/shard_map/ppermute | solution.py:313
  16.3 2.9 %collective-permute-start.1 = (f32[160,128]{1,0:T(8,128)S(1)}, f32[160,128]{1,0:T(8,128)S(1)}, u32[]{:S(2)}, u32[]{:S(2)}) collective-permute-start(f32[160,128]{1,0:T(8,128)S(1)} %get-tuple-element.20), channel_id=1, source_target_pairs={{0,1},{1,0},{2,3},{3,2},{4,5},{5,4},{6,7},{7,6},{8,16},{9,17},{10,... | collective-permute-start | bytes 245768 | tf_op jit(solution)/shard_map/ppermute | solution.py:313

commit v4 on v3

--- a/solution.py
+++ b/solution.py
@@ -28,14 +28,19 @@
     return lax.broadcasted_iota(jnp.int32, (rows, LANES), 1)
 
 
+def position(k, chips):
+    return lax.rem(chips - k, chips) if isinstance(k, jax.Array) else (chips - k) % chips
+
+
 def remap_kernel(
     flux_far, weight, tile_far, block_far, count_far, height, vel_x, vel_y, depth, mask,
-    send, own, flux, stage, dest_tile, dest_block, count, sea_int, table, seen, sems,
+    send, own, flux, stage, held, dest_tile, dest_block, count, sea_int, table, seen, sems, *, tiles,
 ):
     slots, blocks = dest_tile.shape
     fields, rows = flux.shape[0], height.shape[0]
-    tiles = send.shape[0]
-    base = CAP * fields
+    values = CAP * fields
+    share = values + 8
+    chips = tiles // 2
     moves = [(tile_far, dest_tile), (block_far, dest_block), (count_far, count)]
     moves += [(flux_far, flux), (mask, sea_int)]
     moves += [(x, own.at[q * rows : (q + 1) * rows]) for q, x in enumerate((height, vel_x, vel_y, depth))]
@@ -47,7 +52,7 @@
         seen[t] = 0
         for r in range(CAP):
             table[t * CAP + r] = -1
-        send[t, 0:base, :] = jnp.zeros((base, LANES), F32)
+    held[...] = jnp.zeros(held.shape, F32)
     for copy in copies[:3]:
         copy.wait()
     places = []
@@ -58,7 +63,7 @@
             r = jnp.minimum(seen[t], CAP - 1)
             seen[t] = r + 1
             table[t * CAP + r] = jnp.where(k < live, dest_block[k, b], -1)
-            places.append((t, r))
+            places.append(pl.multiple_of(t * values + r * fields, 8))
     for copy in copies[3:9]:
         copy.wait()
     state = [own[q * rows : (q + 1) * rows] for q in range(4)]
@@ -79,11 +84,14 @@
         for g in range(4):
             moved = pltpu.roll(sea[8 * g : 8 * g + 8], (16 * g - first) % LANES, 1)
             small = jnp.where((lane8 >= 16 * g) & (lane8 < 16 * g + 16), moved, small)
-        return packed, small
-
-    to_right = edges(LANES - HALO)
-    to_left = edges(0)
+        return jnp.concatenate([packed, small], axis=0)
+
     me = lax.axis_index("tile")
+    core, chip = me % 2, me // 2
+    to_right, to_left = edges(LANES - HALO), edges(0)
+    tail = 2 * chips * share
+    send[tail : tail + 24, :] = jnp.where(core == 0, to_left, to_right)
+    send[tail + 24 : tail + 48, :] = jnp.where(core == 0, to_right, to_left)
 
     for b in range(blocks):
         if b % (blocks // 2) == 0:
@@ -102,36 +110,41 @@
             both = jnp.dot(
                 left, jnp.concatenate([w_high, w_low], axis=0), preferred_element_type=F32
             )
-            t, r = places[b * slots + k]
-            send[t, pl.ds(pl.multiple_of(r * fields, fields), fields), :] = both[:fields] + both[fields:]
+            held[pl.ds(places[b * slots + k], fields), :] = both[:fields] + both[fields:]
 
     for t in range(tiles):
-        toward_right = me < t
-        packed = jnp.where(toward_right, to_right[0], to_left[0])
-        small = jnp.where(toward_right, to_right[1], to_left[1])
-        send[t, base : base + 16, :] = packed
         lefts, rights = max(t - 1, 0), min(t + 1, tiles - 1)
-        out = small
+        out = jnp.zeros((8, LANES), F32)
         for f in range(WET):
             to = 64 + 16 * f
-            part_l = send[lefts, pl.ds(f, CAP, stride=fields), :]
-            part_r = send[rights, pl.ds(f, CAP, stride=fields), :]
+            part_l = held[pl.ds(lefts * values + f, CAP, stride=fields), :]
+            part_r = held[pl.ds(rights * values + f, CAP, stride=fields), :]
             part_l = pltpu.roll(part_l, (to - (LANES - HALO)) % LANES, 1)
             part_r = pltpu.roll(part_r, to, 1)
             part = jnp.concatenate([part_l, part_r], axis=0)
             out = jnp.where((lane8 >= to) & (lane8 < to + 16), part, out)
+        mine = core == t % 2
+        offset = position(lax.bitwise_xor(chip, t // 2), chips) * share
+        shift = jnp.where(mine, 0, CAP)
         side = jnp.full((8, LANES), -1, jnp.int32)
-        main = jnp.full((8, LANES), -1, jnp.int32)
+        main = jnp.zeros((8, LANES), jnp.int32)
         for r in range(CAP):
             if t > 0:
                 side = jnp.where(row8 == r, table[lefts * CAP + r], side)
             if t < tiles - 1:
                 named = table[rights * CAP + r]
                 side = jnp.where(row8 == CAP + r, jnp.where(named < 0, -1, named + 32), side)
-            main = jnp.where(row8 == r, table[t * CAP + r], main)
+            main = jnp.where(row8 == r + shift, table[t * CAP + r], main)
         out = jnp.where(lane8 == 112, side.astype(F32), out)
         out = jnp.where(lane8 == 113, main.astype(F32), out)
-        send[t, base + 16 : base + 24, :] = out
+        at_names = jnp.where(mine, offset, chips * share + offset + values)
+        at_values = jnp.where(mine, offset + 8, chips * share + offset)
+        send[pl.ds(pl.multiple_of(at_names, 8), 8), :] = out
+        send[pl.ds(pl.multiple_of(at_values, 8), values), :] = held[t * values : (t + 1) * values, :]
+
+
+def beside(k):
+    return k & (k + 1) == 0
 
 
 def spread(hot, values):
@@ -144,50 +157,60 @@
     return jnp.where(lane == ids, 1.0, 0.0).T.astype(BF16)
 
 
-def slots_of(recv, row, tiles, count):
-    chunk = recv.shape[0] // tiles
-    return [recv[pl.ds(row + j, tiles, stride=chunk), :] for j in range(count)]
-
-
-def field_values(recv, f, fields, tiles):
-    chunk = recv.shape[0] // tiles
-    return jnp.concatenate([recv[pl.ds(r * fields + f, tiles, stride=chunk), :] for r in range(CAP)], axis=0)
-
-
-def forcing_kernel(recv, state, forcing, *, tiles):
+def field_values(boxes, f, fields):
+    return jnp.concatenate([box[pl.ds(8 + f, 2 * CAP, stride=fields), :] for box in boxes], axis=0)
+
+
+def names_of(box, values):
+    return box[0:8, :], box[8 + 2 * values : 16 + 2 * values, :]
+
+
+def hot_slots(boxes, values, rows):
+    ids = [sum(names_of(box, values)) for box in boxes]
+    return one_hot(jnp.concatenate(ids, axis=0)[:, 113:114])[:rows]
+
+
+def forcing_kernel(*refs):
+    boxes, state, forcing = refs[:-2], refs[-2], refs[-1]
     fields, rows = forcing.shape[:2]
-    names = jnp.concatenate(slots_of(recv, CAP * fields + 16, tiles, CAP), axis=0)
-    hot = one_hot(names[:, 113:114])[:rows]
+    hot = hot_slots(boxes, CAP * fields, rows)
     sea = state[4 * rows : 5 * rows]
     for f in range(fields):
-        forcing[f] = spread(hot, field_values(recv, f, fields, tiles)) * sea
-
-
-def place_kernel(recv, state, wet, first, second, left, right, *, tiles, fields):
+        forcing[f] = spread(hot, field_values(boxes, f, fields)) * sea
+
+
+def place_kernel(*refs, fields):
+    boxes = refs[:-6]
+    state, wet, first, second, left, right = refs[-6:]
     rows = left.shape[0]
-    chunk = recv.shape[0] // tiles
-    base = CAP * fields
-    names = jnp.concatenate(slots_of(recv, base + 16, tiles, 8), axis=0)
+    chips = len(boxes)
+    values = CAP * fields
+    names = jnp.concatenate([x for box in boxes for x in names_of(box, values)], axis=0)
     hot_side = one_hot(names[:, 112:113])[: 2 * rows]
-    hot_main = one_hot(names[: CAP * tiles, 113:114])[:rows]
+    hot_main = hot_slots(boxes, values, rows)
     sea = state[4 * rows : 5 * rows]
     for f in range(WET):
-        wet[f * rows : (f + 1) * rows] = spread(hot_main, field_values(recv, f, fields, tiles)) * sea
+        wet[f * rows : (f + 1) * rows] = spread(hot_main, field_values(boxes, f, fields)) * sea
     sides = spread(hot_side, names)
     lane = lanes_of(rows)
     me = lax.axis_index("tile")
+    core, chip = me % 2, me // 2
+    beyond = jnp.where(core == 0, chip - 1, chip + 1)
+    at = 16 + 2 * values
+    facing = boxes[0][at : at + 24, :]
+    away = jnp.zeros((24, LANES), F32)
+    for k in filter(beside, range(1, chips)):
+        away = jnp.where(beyond == lax.bitwise_xor(chip, k), boxes[k][at : at + 24, :], away)
     for which, out in ((0, left), (1, right)):
-        source = jnp.maximum(me - 1, 0) if which == 0 else jnp.minimum(me + 1, tiles - 1)
-        exists = (me > 0) if which == 0 else (me < tiles - 1)
-        start = pl.multiple_of(source * chunk + base, 8)
-        packed = recv[pl.ds(start, 16), :]
-        small = recv[pl.ds(start + 16, 8), :]
+        edge = jnp.where(core == which, away, facing)
+        packed, small = edge[:16], edge[16:]
         whole = jnp.concatenate([packed, pltpu.roll(packed, 64, 1)], axis=0)
         sea_part = jnp.concatenate(
             [pltpu.roll(small, (64 - 16 * g) % LANES, 1) for g in range(4)], axis=0
         )
         driven = pltpu.roll(sides[which * rows : (which + 1) * rows], 16, 1)
         full = jnp.where(lane < 64, whole, jnp.where(lane < 80, sea_part, driven))
+        exists = (me > 0) if which == 0 else (me < 2 * chips - 1)
         full = jnp.where(exists, full, 0.0)
         out[...] = full
     even = lax.axis_index("comp") % 2 == 0
@@ -269,7 +292,6 @@
     fields = flux.shape[0]
     blocks, slots = dest_tile.shape
     rows, cols = height.shape
-    chunk = CAP * fields + 24
     state = (height, vel_x, vel_y, depth, mask)
     plane = jax.ShapeDtypeStruct((rows, cols), F32)
     params = pltpu.CompilerParams(vmem_limit_bytes=16 * 1024 * 1024)
@@ -280,14 +302,18 @@
     def far(x):
         return pltpu.with_memory_space_constraint(x, pltpu.HBM)
 
+    values = CAP * fields
+    share = values + 8
+    chips = tiles // 2
     send, own = pl.pallas_call(
-        remap_kernel,
-        out_shape=[near(tiles, chunk, LANES), near(5 * rows, cols)],
+        functools.partial(remap_kernel, tiles=tiles),
+        out_shape=[near(2 * chips * share + 48, LANES), near(5 * rows, cols)],
         in_specs=[HBM] * 10,
         out_specs=[VMEM] * 2,
         scratch_shapes=[
             pltpu.VMEM(flux.shape, F32),
             pltpu.VMEM(weight.shape, F32),
+            pltpu.VMEM((tiles * values, LANES), F32),
             pltpu.SMEM((slots, blocks), jnp.int32),
             pltpu.SMEM((slots, blocks), jnp.int32),
             pltpu.SMEM((blocks,), jnp.int32),
@@ -299,29 +325,41 @@
         compiler_params=params,
         name="remap",
     )(*map(far, (flux, weight, dest_tile.T, dest_block.T, count, *state)))
-    recv = lax.all_to_all(send, "tile", 0, 0, tiled=True).reshape(tiles * chunk, LANES)
+    mine, other = send[: chips * share], send[chips * share :]
+    other = lax.ppermute(other, "tile", [(t, t ^ 1) for t in range(tiles)])
+    away, facing = other[chips * share : chips * share + 24], other[chips * share + 24 :]
+    boxes = []
+    for k in range(chips):
+        at = position(k, chips) * share
+        parts = [x[at : at + share] for x in (mine, other)]
+        if beside(k):
+            parts.append(away if k else facing)
+        boxes.append(jnp.concatenate(parts))
+    boxes[1:] = [
+        lax.ppermute(boxes[k], "tile", [(t, t ^ (2 * k)) for t in range(tiles)]) for k in range(1, chips)
+    ]
     message = near((5 + WET + 2) * 16, LANES)
     wet, first, second, left, right = pl.pallas_call(
-        functools.partial(place_kernel, tiles=tiles, fields=fields),
+        functools.partial(place_kernel, fields=fields),
         out_shape=[near(WET * rows, cols), message, message, near(rows, cols), near(rows, cols)],
-        in_specs=[VMEM] * 2,
+        in_specs=[VMEM] * (chips + 1),
         out_specs=[VMEM] * 5,
         compiler_params=params,
         name="place",
-    )(recv, own)
+    )(*boxes, own)
     received = [
         lax.ppermute(x, ("comp", "tile"), swaps(parity, comps, tiles))
         for parity, x in enumerate((first, second))
     ]
     forcing = pl.pallas_call(
-        functools.partial(forcing_kernel, tiles=tiles),
+        forcing_kernel,
         out_shape=jax.ShapeDtypeStruct((fields, rows, cols), F32),
-        in_specs=[VMEM] * 2,
+        in_specs=[VMEM] * (chips + 1),
         out_specs=VMEM,
         compiler_params=params,
         cost_estimate=pl.CostEstimate(flops=10**8, bytes_accessed=4 * 2**20, transcendentals=0),
         name="forcing",
-    )(recv, own)
+    )(*boxes, own)
     outs = pl.pallas_call(
         functools.partial(cycle_kernel, comps=comps),
         out_shape=[plane] * 3,

time: 21.7 us -> 20.2 us (0.931)
  blocking collectives: 11.6 us -> 0 us
  starting transfers between devices: 1.64 us -> 6.74 us
  waiting for transfers between devices: 1.9 us -> 6.83 us
    all_to_all x1 -> x0, blocking collectives: 11.6 us -> none  [local(): lax.all_to_all(send, 'tile', 0, 0, tiled=True).reshape(tiles * chunk, LANES)]
    ppermute x0 -> x4, starting transfers between devices: none -> 5.1 us  [the longest x3 4.58 us: local(): lax.ppermute(boxes[k], 'tile', [(t, t ^ 2 * k) for t in range(tiles)])]
    ppermute x0 -> x4, waiting for transfers between devices: none -> 4.93 us  [the longest x3 3.98 us: local(): lax.ppermute(boxes[k], 'tile', [(t, t ^ 2 * k) for t in range(tiles)])]
  transfers between devices with their start and end apart: 2 -> 6, of which waited for: 1 -> 4; matrix products, arithmetic and copies ran while one was open for 0% -> 0% of each run, Pallas kernels for 5% -> 5%
where the time goes in v4:
time: 20.2 us; the launch traced here: 19.9 us
  waiting for transfers between devices  6.83 us (34%)
  starting transfers between devices  6.74 us (33%)
  Pallas kernels  5.61 us (28%)
  between operations  0.68 us (3%)
    ppermute x3, starting transfers between devices, local(): lax.ppermute(boxes[k], 'tile', [(t, t ^ 2 * k) for t in range(tiles)])  4.58 us
    ppermute x3, waiting for transfers between devices, local(): lax.ppermute(boxes[k], 'tile', [(t, t ^ 2 * k) for t in range(tiles)])  3.98 us
    pallas_call x1, Pallas kernels, local(): pl.pallas_call(functools.partial(remap_kernel, tiles=tiles), out_shape=[n...  2.14 us
    pallas_call x1, Pallas kernels, local(): pl.pallas_call(functools.partial(cycle_kernel, comps=comps), out_shape=[p...  2.14 us
    ppermute x2, waiting for transfers between devices, local(): lax.ppermute(x, ('comp', 'tile'), swaps(parity, comps, tiles))  1.9 us
    ppermute x2, starting transfers between devices, local(): lax.ppermute(x, ('comp', 'tile'), swaps(parity, comps, tiles))  1.64 us
    pallas_call x1, Pallas kernels, local(): pl.pallas_call(forcing_kernel, out_shape=jax.ShapeDtypeStruct((fields, ro...  0.97 us
    ppermute x1, waiting for transfers between devices, local(): other = lax.ppermute(other, 'tile', [(t, t ^ 1) for t in range(tiles)])  0.95 us
  transfers between devices with their start and end apart: 6, of which 4 were waited for; matrix products, arithmetic and copies ran while one was open for 0% of the time, Pallas kernels for 5%

profile of v4, /device:TPU:0, one launch (start us, length us, event | category | flops | bytes accessed | tf_op | source)
XLA Modules:
  0.0 19.9 jit_solution(17558541022999282768)
XLA Ops:
  0.6 2.1 %remap.1 = (f32[368,128]{1,0:T(8,128)S(1)}, f32[160,128]{1,0:T(8,128)S(1)}) custom-call(f32[8,1024]{1,0:T(8,128)} %flux_far.1, f32[8,4,128,128]{3,2,1,0:T(8,128)} %weight.1, s32[4,8]{1,0:T(4,128)} %bitcast.2, s32[4,8]{1,0:T(4,128)} %bitcast.3, s32[8]{0:T(128)} %count_far.1, f32[32,128]{1,0:T(8,128)} %height.1, f32[32,128]{1,0:T(8,128)} %vel_x.1, ...), custom_call_target="tpu_custom_call" | custom-call | tf_op jit(solution)/shard_map/remap/pallas_call | solution.py:308
  2.8 0.5 %collective-permute-start = (f32[208,128]{1,0:T(8,128)S(1)}, f32[208,128]{1,0:T(8,128)S(1)}, u32[]{:S(2)}, u32[]{:S(2)}) collective-permute-start(f32[208,128]{1,0:T(8,128)S(1)} %slice.40), channel_id=1, source_target_pairs={{0,1},{1,0},{2,3},{3,2},{4,5},{5,4},{6,7},{7,6},{8,9},{9,8},{10,11... | collective-permute-start | bytes 319496 | tf_op jit(solution)/shard_map/ppermute | solution.py:329
  3.3 0.9 %collective-permute-done = f32[208,128]{1,0:T(8,128)S(1)} collective-permute-done((f32[208,128]{1,0:T(8,128)S(1)}, f32[208,128]{1,0:T(8,128)S(1)}, u32[]{:S(2)}, u32[]{:S(2)}) %collective-permute-start) | collective-permute-done | bytes 106528 | tf_op jit(solution)/shard_map/ppermute | solution.py:329
  4.3 3.9 %collective-permute-start.3 = (f32[104,128]{1,0:T(8,128)S(1)}, f32[104,128]{1,0:T(8,128)S(1)}, u32[]{:S(2)}, u32[]{:S(2)}) collective-permute-start(f32[104,128]{1,0:T(8,128)S(1)} %pad_maximum_fusion.2), channel_id=1, source_target_pairs={{0,6},{1,7},{2,4},{3,5},{4,2},{5,3},{6,0},{7,1},{8,14},{9,15},{10,... | collective-permute-start | bytes 159752 | tf_op jit(solution)/shard_map/ppermute | solution.py:339
  8.2 0.5 %collective-permute-start.2 = (f32[80,128]{1,0:T(8,128)S(1)}, f32[80,128]{1,0:T(8,128)S(1)}, u32[]{:S(2)}, u32[]{:S(2)}) collective-permute-start(f32[80,128]{1,0:T(8,128)S(1)} %pad_maximum_fusion.3), channel_id=1, source_target_pairs={{0,4},{1,5},{2,6},{3,7},{4,0},{5,1},{6,2},{7,3},{8,12},{9,13},{10,... | collective-permute-start | bytes 122888 | tf_op jit(solution)/shard_map/ppermute | solution.py:339
  8.7 0.2 %collective-permute-start.1 = (f32[104,128]{1,0:T(8,128)S(1)}, f32[104,128]{1,0:T(8,128)S(1)}, u32[]{:S(2)}, u32[]{:S(2)}) collective-permute-start(f32[104,128]{1,0:T(8,128)S(1)} %pad_maximum_fusion.1), channel_id=1, source_target_pairs={{0,2},{1,3},{2,0},{3,1},{4,6},{5,7},{6,4},{7,5},{8,10},{9,11},{10,... | collective-permute-start | bytes 159752 | tf_op jit(solution)/shard_map/ppermute | solution.py:339
  8.9 3.3 %collective-permute-done.2.refs_2_ = f32[80,128]{1,0:T(8,128)S(1)} collective-permute-done((f32[80,128]{1,0:T(8,128)S(1)}, f32[80,128]{1,0:T(8,128)S(1)}, u32[]{:S(2)}, u32[]{:S(2)}) %collective-permute-start.2) | collective-permute-done | bytes 40992 | tf_op jit(solution)/shard_map/ppermute | solution.py:339
  12.2 0.0 collective-permute-done.3.refs_3_
  12.2 0.7 %collective-permute-done.1.refs_1_ = f32[104,128]{1,0:T(8,128)S(1)} collective-permute-done((f32[104,128]{1,0:T(8,128)S(1)}, f32[104,128]{1,0:T(8,128)S(1)}, u32[]{:S(2)}, u32[]{:S(2)}) %collective-permute-start.1) | collective-permute-done | bytes 53280 | tf_op jit(solution)/shard_map/ppermute | solution.py:339
  12.9 0.4 %place.1 = (f32[96,128]{1,0:T(8,128)S(1)}, f32[160,128]{1,0:T(8,128)S(1)}, f32[160,128]{1,0:T(8,128)S(1)}, f32[32,128]{1,0:T(8,128)S(1)}, f32[32,128]{1,0:T(8,128)S(1)}) custom-call(f32[104,128]{1,0:T(8,128)S(1)} %pad_maximum_fusion.refs_0_, f32[104,128]{1,0:T(8,128)S(1)} %collective-permute-done.1.refs_1_, f32[80,128]{1,0:T(8,128)S(1)} %collective-permute-done.2.refs_2_, ...), custom_call_target="tpu_custom_call" | custom-call | tf_op jit(solution)/shard_map/place/pallas_call | solution.py:342
  13.3 1.6 %collective-permute-start.4 = (f32[160,128]{1,0:T(8,128)S(1)}, f32[160,128]{1,0:T(8,128)S(1)}, u32[]{:S(2)}, u32[]{:S(2)}) collective-permute-start(f32[160,128]{1,0:T(8,128)S(1)} %get-tuple-element.19), channel_id=1, source_target_pairs={{0,8},{1,9},{2,10},{3,11},{4,12},{5,13},{6,14},{7,15},{8,0},{9,1},... | collective-permute-start | bytes 245768 | tf_op jit(solution)/shard_map/ppermute | solution.py:351
  14.9 0.0 collective-permute-start.5
  14.9 1.0 %forcing.1 = f32[8,32,128]{2,1,0:T(8,128)} custom-call(f32[104,128]{1,0:T(8,128)S(1)} %pad_maximum_fusion.refs_0_, f32[104,128]{1,0:T(8,128)S(1)} %collective-permute-done.1.refs_1_, f32[80,128]{1,0:T(8,128)S(1)} %collective-permute-done.2.refs_2_, f32[104,128]{1,0:T(8,128)S(1)} %collective-permute-done.3.refs_3_, f32[160,128]{1,0:T(8,128)S(1)} %get-tuple-element.15.refs_4_.state), custom_call_target="tpu_custom_call" | custom-call | flops 100000000 | bytes 4194304 | tf_op jit(solution)/shard_map/forcing/pallas_call | solution.py:354
  15.9 1.9 %collective-permute-done.4.first = f32[160,128]{1,0:T(8,128)S(1)} collective-permute-done((f32[160,128]{1,0:T(8,128)S(1)}, f32[160,128]{1,0:T(8,128)S(1)}, u32[]{:S(2)}, u32[]{:S(2)}) %collective-permute-start.4) | collective-permute-done | bytes 81952 | tf_op jit(solution)/shard_map/ppermute | solution.py:351
  17.8 0.0 collective-permute-done.5.second
  17.8 2.1 %cycles.1 = (f32[32,128]{1,0:T(8,128)}, f32[32,128]{1,0:T(8,128)}, f32[32,128]{1,0:T(8,128)}) custom-call(f32[160,128]{1,0:T(8,128)S(1)} %get-tuple-element.15.refs_4_.state, f32[96,128]{1,0:T(8,128)S(1)} %get-tuple-element.16.wet, f32[32,128]{1,0:T(8,128)S(1)} %get-tuple-element.17.left, f32[32,128]{1,0:T(8,128)S(1)} %get-tuple-element.18.right, ...), custom_call_target="tpu_custom_call" | custom-call | tf_op jit(solution)/shard_map/cycles/pallas_call | solution.py:363
  (9 shorter events, 0.0 us)
Async XLA Ops:
  2.8 1.5 %collective-permute-start = (f32[208,128]{1,0:T(8,128)S(1)}, f32[208,128]{1,0:T(8,128)S(1)}, u32[]{:S(2)}, u32[]{:S(2)}) collective-permute-start(f32[208,128]{1,0:T(8,128)S(1)} %slice.40), channel_id=1, source_target_pairs={{0,1},{1,0},{2,3},{3,2},{4,5},{5,4},{6,7},{7,6},{8,9},{9,8},{10,11... | collective-permute-start | bytes 319496 | tf_op jit(solution)/shard_map/ppermute | solution.py:329
  4.3 7.9 %collective-permute-start.3 = (f32[104,128]{1,0:T(8,128)S(1)}, f32[104,128]{1,0:T(8,128)S(1)}, u32[]{:S(2)}, u32[]{:S(2)}) collective-permute-start(f32[104,128]{1,0:T(8,128)S(1)} %pad_maximum_fusion.2), channel_id=1, source_target_pairs={{0,6},{1,7},{2,4},{3,5},{4,2},{5,3},{6,0},{7,1},{8,14},{9,15},{10,... | collective-permute-start | bytes 159752 | tf_op jit(solution)/shard_map/ppermute | solution.py:339
  8.2 4.0 %collective-permute-start.2 = (f32[80,128]{1,0:T(8,128)S(1)}, f32[80,128]{1,0:T(8,128)S(1)}, u32[]{:S(2)}, u32[]{:S(2)}) collective-permute-start(f32[80,128]{1,0:T(8,128)S(1)} %pad_maximum_fusion.3), channel_id=1, source_target_pairs={{0,4},{1,5},{2,6},{3,7},{4,0},{5,1},{6,2},{7,3},{8,12},{9,13},{10,... | collective-permute-start | bytes 122888 | tf_op jit(solution)/shard_map/ppermute | solution.py:339
  8.7 4.2 %collective-permute-start.1 = (f32[104,128]{1,0:T(8,128)S(1)}, f32[104,128]{1,0:T(8,128)S(1)}, u32[]{:S(2)}, u32[]{:S(2)}) collective-permute-start(f32[104,128]{1,0:T(8,128)S(1)} %pad_maximum_fusion.1), channel_id=1, source_target_pairs={{0,2},{1,3},{2,0},{3,1},{4,6},{5,7},{6,4},{7,5},{8,10},{9,11},{10,... | collective-permute-start | bytes 159752 | tf_op jit(solution)/shard_map/ppermute | solution.py:339
  13.3 4.5 %collective-permute-start.4 = (f32[160,128]{1,0:T(8,128)S(1)}, f32[160,128]{1,0:T(8,128)S(1)}, u32[]{:S(2)}, u32[]{:S(2)}) collective-permute-start(f32[160,128]{1,0:T(8,128)S(1)} %get-tuple-element.19), channel_id=1, source_target_pairs={{0,8},{1,9},{2,10},{3,11},{4,12},{5,13},{6,14},{7,15},{8,0},{9,1},... | collective-permute-start | bytes 245768 | tf_op jit(solution)/shard_map/ppermute | solution.py:351
  14.9 2.9 %collective-permute-start.5 = (f32[160,128]{1,0:T(8,128)S(1)}, f32[160,128]{1,0:T(8,128)S(1)}, u32[]{:S(2)}, u32[]{:S(2)}) collective-permute-start(f32[160,128]{1,0:T(8,128)S(1)} %get-tuple-element.20), channel_id=1, source_target_pairs={{0,1},{1,0},{2,3},{3,2},{4,5},{5,4},{6,7},{7,6},{8,16},{9,17},{10,... | collective-permute-start | bytes 245768 | tf_op jit(solution)/shard_map/ppermute | solution.py:351

commit v5 on v4

--- a/solution.py
+++ b/solution.py
@@ -11,6 +11,7 @@
 HALO = 2 * NSUB
 CAP = 4
 LANES = 128
+ROUNDS = 3
 WET = 3
 F32 = jnp.float32
 BF16 = jnp.bfloat16
@@ -180,8 +181,8 @@
 
 
 def place_kernel(*refs, fields):
-    boxes = refs[:-6]
-    state, wet, first, second, left, right = refs[-6:]
+    boxes = refs[: -4 - ROUNDS]
+    state, wet, left, right, *messages = refs[-4 - ROUNDS :]
     rows = left.shape[0]
     chips = len(boxes)
     values = CAP * fields
@@ -213,21 +214,25 @@
         exists = (me > 0) if which == 0 else (me < 2 * chips - 1)
         full = jnp.where(exists, full, 0.0)
         out[...] = full
-    even = lax.axis_index("comp") % 2 == 0
-    for message, low in ((first, even), (second, jnp.logical_not(even))):
-        start = pl.multiple_of(jnp.where(low, rows - HALO, 0), 8)
+    section = lax.axis_index("comp")
+    for turn, message in enumerate(messages):
+        start = pl.multiple_of(jnp.where(lax.rem(section, ROUNDS) == turn, rows - HALO, 0), 8)
         parts = [(state, q) for q in range(5)] + [(wet, f) for f in range(WET)] + [(left, 0), (right, 0)]
         for i, (ref, q) in enumerate(parts):
             message[i * HALO : (i + 1) * HALO, :] = ref[pl.ds(q * rows + start, HALO), :]
 
 
 def cycle_kernel(
-    state, wet, left, right, first, second, height_out, flow_x, flow_y, *, comps
+    state, wet, left, right, *refs, comps
 ):
+    height_out, flow_x, flow_y = refs[ROUNDS:]
     rows = height_out.shape[0]
-    even = lax.axis_index("comp") % 2 == 0
-    first, second = first[...], second[...]
-    above, below = jnp.where(even, second, first), jnp.where(even, first, second)
+    section = lax.axis_index("comp")
+    messages = [ref[...] for ref in refs[:ROUNDS]]
+    below, above = messages[0], messages[0]
+    for turn in range(1, ROUNDS):
+        below = jnp.where(lax.rem(section, ROUNDS) == turn, messages[turn], below)
+        above = jnp.where(lax.rem(section + ROUNDS - 1, ROUNDS) == turn, messages[turn], above)
     total = rows + 2 * HALO
     count = 5 + WET
     own = [state[q * rows : (q + 1) * rows] for q in range(5)]
@@ -278,10 +283,10 @@
     flow_y[...] = v[HALO : HALO + rows, :LANES]
 
 
-def swaps(parity, comps, tiles):
+def swaps(turn, comps, tiles):
     pairs = []
     for s in range(comps):
-        other = s + 1 if s % 2 == parity else s - 1
+        other = s + 1 if s % ROUNDS == turn else s - 1 if (s - 1) % ROUNDS == turn else -1
         for t in range(tiles):
             there = other * tiles + t if 0 <= other < comps else s * tiles + (t ^ 1)
             pairs.append((s * tiles + t, there))
@@ -339,17 +344,17 @@
         lax.ppermute(boxes[k], "tile", [(t, t ^ (2 * k)) for t in range(tiles)]) for k in range(1, chips)
     ]
     message = near((5 + WET + 2) * 16, LANES)
-    wet, first, second, left, right = pl.pallas_call(
+    wet, left, right, *messages = pl.pallas_call(
         functools.partial(place_kernel, fields=fields),
-        out_shape=[near(WET * rows, cols), message, message, near(rows, cols), near(rows, cols)],
+        out_shape=[near(WET * rows, cols), near(rows, cols), near(rows, cols)] + [message] * ROUNDS,
         in_specs=[VMEM] * (chips + 1),
-        out_specs=[VMEM] * 5,
+        out_specs=[VMEM] * (3 + ROUNDS),
         compiler_params=params,
         name="place",
     )(*boxes, own)
     received = [
-        lax.ppermute(x, ("comp", "tile"), swaps(parity, comps, tiles))
-        for parity, x in enumerate((first, second))
+        lax.ppermute(x, ("comp", "tile"), swaps(turn, comps, tiles))
+        for turn, x in enumerate(messages)
     ]
     forcing = pl.pallas_call(
         forcing_kernel,
@@ -363,7 +368,7 @@
     outs = pl.pallas_call(
         functools.partial(cycle_kernel, comps=comps),
         out_shape=[plane] * 3,
-        in_specs=[VMEM] * 6,
+        in_specs=[VMEM] * (4 + ROUNDS),
         out_specs=[VMEM] * 3,
         compiler_params=params,
         name="cycles",

time: 20.2 us -> 20.1 us (level)
  starting transfers between devices: 6.74 us -> 7.25 us
  waiting for transfers between devices: 6.83 us -> 6.32 us
    ppermute x2 -> x3, starting transfers between devices: 1.64 us -> 2.15 us  [local(): lax.ppermute(x, ('comp', 'tile'), swaps(turn, comps, tiles))]
    ppermute x2 -> x3, waiting for transfers between devices: 1.9 us -> 1.39 us  [local(): lax.ppermute(x, ('comp', 'tile'), swaps(turn, comps, tiles))]
  transfers between devices with their start and end apart: 6 -> 7, of which waited for: 4 -> 4; matrix products, arithmetic and copies ran while one was open for 0% -> 0% of each run, Pallas kernels for 5% -> 5%
where the time goes in v5:
time: 20.1 us; the launch traced here: 19.9 us
  starting transfers between devices  7.25 us (36%)
  waiting for transfers between devices  6.32 us (31%)
  Pallas kernels  5.62 us (28%)
  between operations  0.68 us (3%)
    ppermute x3, starting transfers between devices, local(): lax.ppermute(boxes[k], 'tile', [(t, t ^ 2 * k) for t in range(tiles)])  4.58 us
    ppermute x3, waiting for transfers between devices, local(): lax.ppermute(boxes[k], 'tile', [(t, t ^ 2 * k) for t in range(tiles)])  3.98 us
    ppermute x3, starting transfers between devices, local(): lax.ppermute(x, ('comp', 'tile'), swaps(turn, comps, tiles))  2.15 us
    pallas_call x1, Pallas kernels, local(): pl.pallas_call(functools.partial(cycle_kernel, comps=comps), out_shape=[p...  2.14 us
    pallas_call x1, Pallas kernels, local(): pl.pallas_call(functools.partial(remap_kernel, tiles=tiles), out_shape=[n...  2.14 us
    ppermute x3, waiting for transfers between devices, local(): lax.ppermute(x, ('comp', 'tile'), swaps(turn, comps, tiles))  1.39 us
    pallas_call x1, Pallas kernels, local(): pl.pallas_call(forcing_kernel, out_shape=jax.ShapeDtypeStruct((fields, ro...  0.97 us
    ppermute x1, waiting for transfers between devices, local(): other = lax.ppermute(other, 'tile', [(t, t ^ 1) for t in range(tiles)])  0.95 us
  transfers between devices with their start and end apart: 7, of which 4 were waited for; matrix products, arithmetic and copies ran while one was open for 0% of the time, Pallas kernels for 5%

profile of v5, /device:TPU:0, one launch (start us, length us, event | category | flops | bytes accessed | tf_op | source)
XLA Modules:
  0.0 19.9 jit_solution(13364727876011655264)
XLA Ops:
  0.6 2.1 %remap.1 = (f32[368,128]{1,0:T(8,128)S(1)}, f32[160,128]{1,0:T(8,128)S(1)}) custom-call(f32[8,1024]{1,0:T(8,128)} %flux_far.1, f32[8,4,128,128]{3,2,1,0:T(8,128)} %weight.1, s32[4,8]{1,0:T(4,128)} %bitcast.2, s32[4,8]{1,0:T(4,128)} %bitcast.3, s32[8]{0:T(128)} %count_far.1, f32[32,128]{1,0:T(8,128)} %height.1, f32[32,128]{1,0:T(8,128)} %vel_x.1, ...), custom_call_target="tpu_custom_call" | custom-call | tf_op jit(solution)/shard_map/remap/pallas_call | solution.py:313
  2.8 0.5 %collective-permute-start = (f32[208,128]{1,0:T(8,128)S(1)}, f32[208,128]{1,0:T(8,128)S(1)}, u32[]{:S(2)}, u32[]{:S(2)}) collective-permute-start(f32[208,128]{1,0:T(8,128)S(1)} %slice.40), channel_id=1, source_target_pairs={{0,1},{1,0},{2,3},{3,2},{4,5},{5,4},{6,7},{7,6},{8,9},{9,8},{10,11... | collective-permute-start | bytes 319496 | tf_op jit(solution)/shard_map/ppermute | solution.py:334
  3.3 0.9 %collective-permute-done = f32[208,128]{1,0:T(8,128)S(1)} collective-permute-done((f32[208,128]{1,0:T(8,128)S(1)}, f32[208,128]{1,0:T(8,128)S(1)}, u32[]{:S(2)}, u32[]{:S(2)}) %collective-permute-start) | collective-permute-done | bytes 106528 | tf_op jit(solution)/shard_map/ppermute | solution.py:334
  4.3 3.9 %collective-permute-start.3 = (f32[104,128]{1,0:T(8,128)S(1)}, f32[104,128]{1,0:T(8,128)S(1)}, u32[]{:S(2)}, u32[]{:S(2)}) collective-permute-start(f32[104,128]{1,0:T(8,128)S(1)} %pad_maximum_fusion.2), channel_id=1, source_target_pairs={{0,6},{1,7},{2,4},{3,5},{4,2},{5,3},{6,0},{7,1},{8,14},{9,15},{10,... | collective-permute-start | bytes 159752 | tf_op jit(solution)/shard_map/ppermute | solution.py:344
  8.2 0.5 %collective-permute-start.2 = (f32[80,128]{1,0:T(8,128)S(1)}, f32[80,128]{1,0:T(8,128)S(1)}, u32[]{:S(2)}, u32[]{:S(2)}) collective-permute-start(f32[80,128]{1,0:T(8,128)S(1)} %pad_maximum_fusion.3), channel_id=1, source_target_pairs={{0,4},{1,5},{2,6},{3,7},{4,0},{5,1},{6,2},{7,3},{8,12},{9,13},{10,... | collective-permute-start | bytes 122888 | tf_op jit(solution)/shard_map/ppermute | solution.py:344
  8.7 0.2 %collective-permute-start.1 = (f32[104,128]{1,0:T(8,128)S(1)}, f32[104,128]{1,0:T(8,128)S(1)}, u32[]{:S(2)}, u32[]{:S(2)}) collective-permute-start(f32[104,128]{1,0:T(8,128)S(1)} %pad_maximum_fusion.1), channel_id=1, source_target_pairs={{0,2},{1,3},{2,0},{3,1},{4,6},{5,7},{6,4},{7,5},{8,10},{9,11},{10,... | collective-permute-start | bytes 159752 | tf_op jit(solution)/shard_map/ppermute | solution.py:344
  8.9 3.3 %collective-permute-done.2.refs_2_ = f32[80,128]{1,0:T(8,128)S(1)} collective-permute-done((f32[80,128]{1,0:T(8,128)S(1)}, f32[80,128]{1,0:T(8,128)S(1)}, u32[]{:S(2)}, u32[]{:S(2)}) %collective-permute-start.2) | collective-permute-done | bytes 40992 | tf_op jit(solution)/shard_map/ppermute | solution.py:344
  12.2 0.0 collective-permute-done.3.refs_3_
  12.2 0.7 %collective-permute-done.1.refs_1_ = f32[104,128]{1,0:T(8,128)S(1)} collective-permute-done((f32[104,128]{1,0:T(8,128)S(1)}, f32[104,128]{1,0:T(8,128)S(1)}, u32[]{:S(2)}, u32[]{:S(2)}) %collective-permute-start.1) | collective-permute-done | bytes 53280 | tf_op jit(solution)/shard_map/ppermute | solution.py:344
  12.9 0.4 %place.1 = (f32[96,128]{1,0:T(8,128)S(1)}, f32[32,128]{1,0:T(8,128)S(1)}, f32[32,128]{1,0:T(8,128)S(1)}, f32[160,128]{1,0:T(8,128)S(1)}, f32[160,128]{1,0:T(8,128)S(1)}, /*index=5*/f32[160,128]{1,0:T(8,128)S(1)}) custom-call(f32[104,128]{1,0:T(8,128)S(1)} %pad_maximum_fusion.refs_0_, f32[104,128]{1,0:T(8,128)S(1)} %collective-permute-done.1.refs_1_, ...), custom_call_target="tpu_custom_call" | custom-call | tf_op jit(solution)/shard_map/place/pallas_call | solution.py:347
  13.3 1.6 %collective-permute-start.4 = (f32[160,128]{1,0:T(8,128)S(1)}, f32[160,128]{1,0:T(8,128)S(1)}, u32[]{:S(2)}, u32[]{:S(2)}) collective-permute-start(f32[160,128]{1,0:T(8,128)S(1)} %get-tuple-element.20), channel_id=1, source_target_pairs={{0,8},{1,9},{2,10},{3,11},{4,12},{5,13},{6,14},{7,15},{8,0},{9,1},... | collective-permute-start | bytes 245768 | tf_op jit(solution)/shard_map/ppermute | solution.py:356
  14.9 0.0 collective-permute-start.5
  14.9 0.5 %collective-permute-start.6 = (f32[160,128]{1,0:T(8,128)S(1)}, f32[160,128]{1,0:T(8,128)S(1)}, u32[]{:S(2)}, u32[]{:S(2)}) collective-permute-start(f32[160,128]{1,0:T(8,128)S(1)} %get-tuple-element.22), channel_id=1, source_target_pairs={{0,1},{1,0},{2,3},{3,2},{4,5},{5,4},{6,7},{7,6},{8,9},{9,8},{10,11... | collective-permute-start | bytes 245768 | tf_op jit(solution)/shard_map/ppermute | solution.py:356
  15.4 1.0 %forcing.1 = f32[8,32,128]{2,1,0:T(8,128)} custom-call(f32[104,128]{1,0:T(8,128)S(1)} %pad_maximum_fusion.refs_0_, f32[104,128]{1,0:T(8,128)S(1)} %collective-permute-done.1.refs_1_, f32[80,128]{1,0:T(8,128)S(1)} %collective-permute-done.2.refs_2_, f32[104,128]{1,0:T(8,128)S(1)} %collective-permute-done.3.refs_3_, f32[160,128]{1,0:T(8,128)S(1)} %get-tuple-element.16.refs_4_.state), custom_call_target="tpu_custom_call" | custom-call | flops 100000000 | bytes 4194304 | tf_op jit(solution)/shard_map/forcing/pallas_call | solution.py:359
  16.4 1.4 %collective-permute-done.4.refs_0_ = f32[160,128]{1,0:T(8,128)S(1)} collective-permute-done((f32[160,128]{1,0:T(8,128)S(1)}, f32[160,128]{1,0:T(8,128)S(1)}, u32[]{:S(2)}, u32[]{:S(2)}) %collective-permute-start.4) | collective-permute-done | bytes 81952 | tf_op jit(solution)/shard_map/ppermute | solution.py:356
  17.8 0.0 collective-permute-done.5.refs_1_
  17.8 0.0 collective-permute-done.6.refs_2_
  17.8 2.1 %cycles.1 = (f32[32,128]{1,0:T(8,128)}, f32[32,128]{1,0:T(8,128)}, f32[32,128]{1,0:T(8,128)}) custom-call(f32[160,128]{1,0:T(8,128)S(1)} %get-tuple-element.16.refs_4_.state, f32[96,128]{1,0:T(8,128)S(1)} %get-tuple-element.17.wet, f32[32,128]{1,0:T(8,128)S(1)} %get-tuple-element.18.left, f32[32,128]{1,0:T(8,128)S(1)} %get-tuple-element.19.right, ...), custom_call_target="tpu_custom_call" | custom-call | tf_op jit(solution)/shard_map/cycles/pallas_call | solution.py:368
  (9 shorter events, 0.0 us)
Async XLA Ops:
  2.8 1.5 %collective-permute-start = (f32[208,128]{1,0:T(8,128)S(1)}, f32[208,128]{1,0:T(8,128)S(1)}, u32[]{:S(2)}, u32[]{:S(2)}) collective-permute-start(f32[208,128]{1,0:T(8,128)S(1)} %slice.40), channel_id=1, source_target_pairs={{0,1},{1,0},{2,3},{3,2},{4,5},{5,4},{6,7},{7,6},{8,9},{9,8},{10,11... | collective-permute-start | bytes 319496 | tf_op jit(solution)/shard_map/ppermute | solution.py:334
  4.3 7.9 %collective-permute-start.3 = (f32[104,128]{1,0:T(8,128)S(1)}, f32[104,128]{1,0:T(8,128)S(1)}, u32[]{:S(2)}, u32[]{:S(2)}) collective-permute-start(f32[104,128]{1,0:T(8,128)S(1)} %pad_maximum_fusion.2), channel_id=1, source_target_pairs={{0,6},{1,7},{2,4},{3,5},{4,2},{5,3},{6,0},{7,1},{8,14},{9,15},{10,... | collective-permute-start | bytes 159752 | tf_op jit(solution)/shard_map/ppermute | solution.py:344
  8.2 4.0 %collective-permute-start.2 = (f32[80,128]{1,0:T(8,128)S(1)}, f32[80,128]{1,0:T(8,128)S(1)}, u32[]{:S(2)}, u32[]{:S(2)}) collective-permute-start(f32[80,128]{1,0:T(8,128)S(1)} %pad_maximum_fusion.3), channel_id=1, source_target_pairs={{0,4},{1,5},{2,6},{3,7},{4,0},{5,1},{6,2},{7,3},{8,12},{9,13},{10,... | collective-permute-start | bytes 122888 | tf_op jit(solution)/shard_map/ppermute | solution.py:344
  8.7 4.2 %collective-permute-start.1 = (f32[104,128]{1,0:T(8,128)S(1)}, f32[104,128]{1,0:T(8,128)S(1)}, u32[]{:S(2)}, u32[]{:S(2)}) collective-permute-start(f32[104,128]{1,0:T(8,128)S(1)} %pad_maximum_fusion.1), channel_id=1, source_target_pairs={{0,2},{1,3},{2,0},{3,1},{4,6},{5,7},{6,4},{7,5},{8,10},{9,11},{10,... | collective-permute-start | bytes 159752 | tf_op jit(solution)/shard_map/ppermute | solution.py:344
  13.3 4.5 %collective-permute-start.4 = (f32[160,128]{1,0:T(8,128)S(1)}, f32[160,128]{1,0:T(8,128)S(1)}, u32[]{:S(2)}, u32[]{:S(2)}) collective-permute-start(f32[160,128]{1,0:T(8,128)S(1)} %get-tuple-element.20), channel_id=1, source_target_pairs={{0,8},{1,9},{2,10},{3,11},{4,12},{5,13},{6,14},{7,15},{8,0},{9,1},... | collective-permute-start | bytes 245768 | tf_op jit(solution)/shard_map/ppermute | solution.py:356
  14.9 2.9 %collective-permute-start.5 = (f32[160,128]{1,0:T(8,128)S(1)}, f32[160,128]{1,0:T(8,128)S(1)}, u32[]{:S(2)}, u32[]{:S(2)}) collective-permute-start(f32[160,128]{1,0:T(8,128)S(1)} %get-tuple-element.21), channel_id=1, source_target_pairs={{0,1},{1,0},{2,3},{3,2},{4,5},{5,4},{6,7},{7,6},{8,16},{9,17},{10,... | collective-permute-start | bytes 245768 | tf_op jit(solution)/shard_map/ppermute | solution.py:356
  14.9 2.9 %collective-permute-start.6 = (f32[160,128]{1,0:T(8,128)S(1)}, f32[160,128]{1,0:T(8,128)S(1)}, u32[]{:S(2)}, u32[]{:S(2)}) collective-permute-start(f32[160,128]{1,0:T(8,128)S(1)} %get-tuple-element.22), channel_id=1, source_target_pairs={{0,1},{1,0},{2,3},{3,2},{4,5},{5,4},{6,7},{7,6},{8,9},{9,8},{10,11... | collective-permute-start | bytes 245768 | tf_op jit(solution)/shard_map/ppermute | solution.py:356

commit v6 on v5

--- a/solution.py
+++ b/solution.py
@@ -29,8 +29,11 @@
     return lax.broadcasted_iota(jnp.int32, (rows, LANES), 1)
 
 
-def position(k, chips):
-    return lax.rem(chips - k, chips) if isinstance(k, jax.Array) else (chips - k) % chips
+def route(k, core, chips):
+    alone = (k == 0) | (k == chips - 1)
+    sender = jnp.where(alone, core, lax.rem(k + 1, 2))
+    place = jnp.where(alone, k, (k - 1) // 2 * 2 + 1 + jnp.where(sender == core, 0, 1))
+    return sender, place
 
 
 def remap_kernel(
@@ -124,8 +127,9 @@
             part_r = pltpu.roll(part_r, to, 1)
             part = jnp.concatenate([part_l, part_r], axis=0)
             out = jnp.where((lane8 >= to) & (lane8 < to + 16), part, out)
-        mine = core == t % 2
-        offset = position(lax.bitwise_xor(chip, t // 2), chips) * share
+        sender, place = route(lax.bitwise_xor(chip, t // 2), t % 2, chips)
+        mine = core == sender
+        offset = place * share
         shift = jnp.where(mine, 0, CAP)
         side = jnp.full((8, LANES), -1, jnp.int32)
         main = jnp.zeros((8, LANES), jnp.int32)
@@ -146,6 +150,10 @@
 
 def beside(k):
     return k & (k + 1) == 0
+
+
+def pairs_of(chips):
+    return range(1, chips - 1, 2)
 
 
 def spread(hot, values):
@@ -198,10 +206,10 @@
     core, chip = me % 2, me // 2
     beyond = jnp.where(core == 0, chip - 1, chip + 1)
     at = 16 + 2 * values
-    facing = boxes[0][at : at + 24, :]
-    away = jnp.zeros((24, LANES), F32)
-    for k in filter(beside, range(1, chips)):
-        away = jnp.where(beyond == lax.bitwise_xor(chip, k), boxes[k][at : at + 24, :], away)
+    facing, away = boxes[0][at : at + 24, :], boxes[-1][at : at + 24, :]
+    for k in filter(beside, pairs_of(chips)):
+        direct, passed = boxes[k][2 * at : 2 * at + 24, :], boxes[k + 1][at : at + 24, :]
+        away = jnp.where(beyond == lax.bitwise_xor(chip, k), jnp.where(core == 0, direct, passed), away)
     for which, out in ((0, left), (1, right)):
         edge = jnp.where(core == which, away, facing)
         packed, small = edge[:16], edge[16:]
@@ -333,16 +341,23 @@
     mine, other = send[: chips * share], send[chips * share :]
     other = lax.ppermute(other, "tile", [(t, t ^ 1) for t in range(tiles)])
     away, facing = other[chips * share : chips * share + 24], other[chips * share + 24 :]
-    boxes = []
-    for k in range(chips):
-        at = position(k, chips) * share
-        parts = [x[at : at + share] for x in (mine, other)]
+
+    def joined(place):
+        return [x[place * share : (place + 1) * share] for x in (mine, other)]
+
+    tile = lax.axis_index("tile")
+    outward = send[2 * chips * share : 2 * chips * share + 24]
+    boxes = [jnp.concatenate(joined(0) + [facing])]
+    for k in pairs_of(chips):
+        parts = joined(k) + joined(k + 1)
         if beside(k):
-            parts.append(away if k else facing)
-        boxes.append(jnp.concatenate(parts))
-    boxes[1:] = [
-        lax.ppermute(boxes[k], "tile", [(t, t ^ (2 * k)) for t in range(tiles)]) for k in range(1, chips)
-    ]
+            up = lax.bitwise_xor(tile // 2, k) > tile // 2
+            parts.append(jnp.where(up, away, outward))
+        swap = [(t, t ^ (2 * (k + t % 2))) for t in range(tiles)]
+        box = lax.ppermute(jnp.concatenate(parts), "tile", swap)
+        boxes += [box, lax.ppermute(box[2 * share :], "tile", [(t, t ^ 1) for t in range(tiles)])]
+    swap = [(t, t ^ (2 * (chips - 1))) for t in range(tiles)]
+    boxes.append(lax.ppermute(jnp.concatenate(joined(chips - 1) + [away]), "tile", swap))
     message = near((5 + WET + 2) * 16, LANES)
     wet, left, right, *messages = pl.pallas_call(
         functools.partial(place_kernel, fields=fields),

time: 20.1 us -> 19.6 us (0.975)
  waiting for transfers between devices: 6.32 us -> 5.93 us
    ppermute x3, waiting for transfers between devices: 3.98 us -> 3.59 us  [the longest x1 2.34 us: local(): lax.ppermute(jnp.concatenate(joined(chips - 1) + [away]), 'tile', swap)]
where the time goes in v6:
time: 19.6 us; the launch traced here: 19.4 us
  starting transfers between devices  7.14 us (36%)
  waiting for transfers between devices  5.93 us (30%)
  Pallas kernels  5.62 us (29%)
  between operations  0.7 us (4%)
    ppermute x1, starting transfers between devices, local(): box = lax.ppermute(jnp.concatenate(parts), 'tile', swap)  2.91 us
    ppermute x1, waiting for transfers between devices, local(): lax.ppermute(jnp.concatenate(joined(chips - 1) + [away]), 'tile', swap)  2.34 us
    ppermute x3, starting transfers between devices, local(): lax.ppermute(x, ('comp', 'tile'), swaps(turn, comps, tiles))  2.15 us
    pallas_call x1, Pallas kernels, local(): pl.pallas_call(functools.partial(remap_kernel, tiles=tiles), out_shape=[n...  2.15 us
    pallas_call x1, Pallas kernels, local(): pl.pallas_call(functools.partial(cycle_kernel, comps=comps), out_shape=[p...  2.14 us
    ppermute x1, starting transfers between devices, local(): lax.ppermute(jnp.concatenate(joined(chips - 1) + [away]), 'tile', swap)  1.56 us
    ppermute x3, waiting for transfers between devices, local(): lax.ppermute(x, ('comp', 'tile'), swaps(turn, comps, tiles))  1.39 us
    ppermute x1, waiting for transfers between devices, local(): box = lax.ppermute(jnp.concatenate(parts), 'tile', swap)  1.24 us
  transfers between devices with their start and end apart: 7, of which 4 were waited for; matrix products, arithmetic and copies ran while one was open for 0% of the time, Pallas kernels for 5%

profile of v6, /device:TPU:0, one launch (start us, length us, event | category | flops | bytes accessed | tf_op | source)
XLA Modules:
  0.0 19.4 jit_solution(6828388395069010314)
XLA Ops:
  0.6 2.1 %remap.1 = (f32[368,128]{1,0:T(8,128)S(1)}, f32[160,128]{1,0:T(8,128)S(1)}) custom-call(f32[8,1024]{1,0:T(8,128)} %flux_far.1, f32[8,4,128,128]{3,2,1,0:T(8,128)} %weight.1, s32[4,8]{1,0:T(4,128)} %bitcast.2, s32[4,8]{1,0:T(4,128)} %bitcast.3, s32[8]{0:T(128)} %count_far.1, f32[32,128]{1,0:T(8,128)} %height.1, f32[32,128]{1,0:T(8,128)} %vel_x.1, ...), custom_call_target="tpu_custom_call" | custom-call | tf_op jit(solution)/shard_map/remap/pallas_call | solution.py:321
  2.8 0.5 %collective-permute-start = (f32[208,128]{1,0:T(8,128)S(1)}, f32[208,128]{1,0:T(8,128)S(1)}, u32[]{:S(2)}, u32[]{:S(2)}) collective-permute-start(f32[208,128]{1,0:T(8,128)S(1)} %slice.46), channel_id=1, source_target_pairs={{0,1},{1,0},{2,3},{3,2},{4,5},{5,4},{6,7},{7,6},{8,9},{9,8},{10,11... | collective-permute-start | bytes 319496 | tf_op jit(solution)/shard_map/ppermute | solution.py:342
  3.3 1.0 %collective-permute-done = f32[208,128]{1,0:T(8,128)S(1)} collective-permute-done((f32[208,128]{1,0:T(8,128)S(1)}, f32[208,128]{1,0:T(8,128)S(1)}, u32[]{:S(2)}, u32[]{:S(2)}) %collective-permute-start) | collective-permute-done | bytes 106528 | tf_op jit(solution)/shard_map/ppermute | solution.py:342
  4.3 2.9 %collective-permute-start.1 = (f32[184,128]{1,0:T(8,128)S(1)}, f32[184,128]{1,0:T(8,128)S(1)}, u32[]{:S(2)}, u32[]{:S(2)}) collective-permute-start(f32[184,128]{1,0:T(8,128)S(1)} %get-tuple-element.29), channel_id=1, source_target_pairs={{0,2},{1,5},{2,0},{3,7},{4,6},{5,1},{6,4},{7,3},{8,10},{9,13},{10,... | collective-permute-start | bytes 282632 | tf_op jit(solution)/shard_map/ppermute | solution.py:357
  7.2 1.6 %collective-permute-start.3 = (f32[104,128]{1,0:T(8,128)S(1)}, f32[104,128]{1,0:T(8,128)S(1)}, u32[]{:S(2)}, u32[]{:S(2)}) collective-permute-start(f32[104,128]{1,0:T(8,128)S(1)} %pad_maximum_fusion.1), channel_id=1, source_target_pairs={{0,6},{1,7},{2,4},{3,5},{4,2},{5,3},{6,0},{7,1},{8,14},{9,15},{10,... | collective-permute-start | bytes 159752 | tf_op jit(solution)/shard_map/ppermute | solution.py:360
  8.8 1.2 %collective-permute-done.1.refs_1_ = f32[184,128]{1,0:T(8,128)S(1)} collective-permute-done((f32[184,128]{1,0:T(8,128)S(1)}, f32[184,128]{1,0:T(8,128)S(1)}, u32[]{:S(2)}, u32[]{:S(2)}) %collective-permute-start.1) | collective-permute-done | bytes 94240 | tf_op jit(solution)/shard_map/ppermute | solution.py:357
  10.0 0.0 collective-permute-start.2
  10.1 2.3 %collective-permute-done.3.refs_3_ = f32[104,128]{1,0:T(8,128)S(1)} collective-permute-done((f32[104,128]{1,0:T(8,128)S(1)}, f32[104,128]{1,0:T(8,128)S(1)}, u32[]{:S(2)}, u32[]{:S(2)}) %collective-permute-start.3) | collective-permute-done | bytes 53280 | tf_op jit(solution)/shard_map/ppermute | solution.py:360
  12.4 0.0 collective-permute-done.2.refs_2_
  12.4 0.4 %place.1 = (f32[96,128]{1,0:T(8,128)S(1)}, f32[32,128]{1,0:T(8,128)S(1)}, f32[32,128]{1,0:T(8,128)S(1)}, f32[160,128]{1,0:T(8,128)S(1)}, f32[160,128]{1,0:T(8,128)S(1)}, /*index=5*/f32[160,128]{1,0:T(8,128)S(1)}) custom-call(f32[104,128]{1,0:T(8,128)S(1)} %pad_maximum_fusion.refs_0_, f32[184,128]{1,0:T(8,128)S(1)} %collective-permute-done.1.refs_1_, ...), custom_call_target="tpu_custom_call" | custom-call | tf_op jit(solution)/shard_map/place/pallas_call | solution.py:362
  12.8 1.6 %collective-permute-start.4 = (f32[160,128]{1,0:T(8,128)S(1)}, f32[160,128]{1,0:T(8,128)S(1)}, u32[]{:S(2)}, u32[]{:S(2)}) collective-permute-start(f32[160,128]{1,0:T(8,128)S(1)} %get-tuple-element.20), channel_id=1, source_target_pairs={{0,8},{1,9},{2,10},{3,11},{4,12},{5,13},{6,14},{7,15},{8,0},{9,1},... | collective-permute-start | bytes 245768 | tf_op jit(solution)/shard_map/ppermute | solution.py:371
  14.4 0.0 collective-permute-start.5
  14.4 0.5 %collective-permute-start.6 = (f32[160,128]{1,0:T(8,128)S(1)}, f32[160,128]{1,0:T(8,128)S(1)}, u32[]{:S(2)}, u32[]{:S(2)}) collective-permute-start(f32[160,128]{1,0:T(8,128)S(1)} %get-tuple-element.22), channel_id=1, source_target_pairs={{0,1},{1,0},{2,3},{3,2},{4,5},{5,4},{6,7},{7,6},{8,9},{9,8},{10,11... | collective-permute-start | bytes 245768 | tf_op jit(solution)/shard_map/ppermute | solution.py:371
  14.9 1.0 %forcing.1 = f32[8,32,128]{2,1,0:T(8,128)} custom-call(f32[104,128]{1,0:T(8,128)S(1)} %pad_maximum_fusion.refs_0_, f32[184,128]{1,0:T(8,128)S(1)} %collective-permute-done.1.refs_1_, f32[104,128]{1,0:T(8,128)S(1)} %collective-permute-done.2.refs_2_, f32[104,128]{1,0:T(8,128)S(1)} %collective-permute-done.3.refs_3_, ...), custom_call_target="tpu_custom_call" | custom-call | flops 100000000 | bytes 4194304 | tf_op jit(solution)/shard_map/forcing/pallas_call | solution.py:374
  15.9 1.4 %collective-permute-done.4.refs_0_ = f32[160,128]{1,0:T(8,128)S(1)} collective-permute-done((f32[160,128]{1,0:T(8,128)S(1)}, f32[160,128]{1,0:T(8,128)S(1)}, u32[]{:S(2)}, u32[]{:S(2)}) %collective-permute-start.4) | collective-permute-done | bytes 81952 | tf_op jit(solution)/shard_map/ppermute | solution.py:371
  17.3 0.0 collective-permute-done.5.refs_1_
  17.3 0.0 collective-permute-done.6.refs_2_
  17.3 2.1 %cycles.1 = (f32[32,128]{1,0:T(8,128)}, f32[32,128]{1,0:T(8,128)}, f32[32,128]{1,0:T(8,128)}) custom-call(f32[160,128]{1,0:T(8,128)S(1)} %get-tuple-element.16.refs_4_.state, f32[96,128]{1,0:T(8,128)S(1)} %get-tuple-element.17.wet, f32[32,128]{1,0:T(8,128)S(1)} %get-tuple-element.18.left, f32[32,128]{1,0:T(8,128)S(1)} %get-tuple-element.19.right, ...), custom_call_target="tpu_custom_call" | custom-call | tf_op jit(solution)/shard_map/cycles/pallas_call | solution.py:383
  (10 shorter events, 0.1 us)
Async XLA Ops:
  2.8 1.5 %collective-permute-start = (f32[208,128]{1,0:T(8,128)S(1)}, f32[208,128]{1,0:T(8,128)S(1)}, u32[]{:S(2)}, u32[]{:S(2)}) collective-permute-start(f32[208,128]{1,0:T(8,128)S(1)} %slice.46), channel_id=1, source_target_pairs={{0,1},{1,0},{2,3},{3,2},{4,5},{5,4},{6,7},{7,6},{8,9},{9,8},{10,11... | collective-permute-start | bytes 319496 | tf_op jit(solution)/shard_map/ppermute | solution.py:342
  4.3 5.7 %collective-permute-start.1 = (f32[184,128]{1,0:T(8,128)S(1)}, f32[184,128]{1,0:T(8,128)S(1)}, u32[]{:S(2)}, u32[]{:S(2)}) collective-permute-start(f32[184,128]{1,0:T(8,128)S(1)} %get-tuple-element.29), channel_id=1, source_target_pairs={{0,2},{1,5},{2,0},{3,7},{4,6},{5,1},{6,4},{7,3},{8,10},{9,13},{10,... | collective-permute-start | bytes 282632 | tf_op jit(solution)/shard_map/ppermute | solution.py:357
  7.2 5.2 %collective-permute-start.3 = (f32[104,128]{1,0:T(8,128)S(1)}, f32[104,128]{1,0:T(8,128)S(1)}, u32[]{:S(2)}, u32[]{:S(2)}) collective-permute-start(f32[104,128]{1,0:T(8,128)S(1)} %pad_maximum_fusion.1), channel_id=1, source_target_pairs={{0,6},{1,7},{2,4},{3,5},{4,2},{5,3},{6,0},{7,1},{8,14},{9,15},{10,... | collective-permute-start | bytes 159752 | tf_op jit(solution)/shard_map/ppermute | solution.py:360
  10.0 2.4 %collective-permute-start.2 = (f32[104,128]{1,0:T(8,128)S(1)}, f32[104,128]{1,0:T(8,128)S(1)}, u32[]{:S(2)}, u32[]{:S(2)}) collective-permute-start(f32[104,128]{1,0:T(8,128)S(1)} %slice.63), channel_id=1, source_target_pairs={{0,1},{1,0},{2,3},{3,2},{4,5},{5,4},{6,7},{7,6},{8,9},{9,8},{10,11... | collective-permute-start | bytes 159752 | tf_op jit(solution)/shard_map/ppermute | solution.py:358
  12.8 4.5 %collective-permute-start.4 = (f32[160,128]{1,0:T(8,128)S(1)}, f32[160,128]{1,0:T(8,128)S(1)}, u32[]{:S(2)}, u32[]{:S(2)}) collective-permute-start(f32[160,128]{1,0:T(8,128)S(1)} %get-tuple-element.20), channel_id=1, source_target_pairs={{0,8},{1,9},{2,10},{3,11},{4,12},{5,13},{6,14},{7,15},{8,0},{9,1},... | collective-permute-start | bytes 245768 | tf_op jit(solution)/shard_map/ppermute | solution.py:371
  14.4 2.9 %collective-permute-start.5 = (f32[160,128]{1,0:T(8,128)S(1)}, f32[160,128]{1,0:T(8,128)S(1)}, u32[]{:S(2)}, u32[]{:S(2)}) collective-permute-start(f32[160,128]{1,0:T(8,128)S(1)} %get-tuple-element.21), channel_id=1, source_target_pairs={{0,1},{1,0},{2,3},{3,2},{4,5},{5,4},{6,7},{7,6},{8,16},{9,17},{10,... | collective-permute-start | bytes 245768 | tf_op jit(solution)/shard_map/ppermute | solution.py:371
  14.4 2.9 %collective-permute-start.6 = (f32[160,128]{1,0:T(8,128)S(1)}, f32[160,128]{1,0:T(8,128)S(1)}, u32[]{:S(2)}, u32[]{:S(2)}) collective-permute-start(f32[160,128]{1,0:T(8,128)S(1)} %get-tuple-element.22), channel_id=1, source_target_pairs={{0,1},{1,0},{2,3},{3,2},{4,5},{5,4},{6,7},{7,6},{8,9},{9,8},{10,11... | collective-permute-start | bytes 245768 | tf_op jit(solution)/shard_map/ppermute | solution.py:371

commit v7 on v6

--- a/solution.py
+++ b/solution.py
@@ -31,8 +31,8 @@
 
 def route(k, core, chips):
     alone = (k == 0) | (k == chips - 1)
-    sender = jnp.where(alone, core, lax.rem(k + 1, 2))
-    place = jnp.where(alone, k, (k - 1) // 2 * 2 + 1 + jnp.where(sender == core, 0, 1))
+    sender = jnp.where(k == 0, core, jnp.where(alone, 1 - core, lax.rem(k + 1, 2)))
+    place = jnp.where(alone, k, (k - 1) // 2 * 2 + 1 + jnp.where(sender == core, 1, 0))
     return sender, place
 
 
@@ -209,7 +209,7 @@
     facing, away = boxes[0][at : at + 24, :], boxes[-1][at : at + 24, :]
     for k in filter(beside, pairs_of(chips)):
         direct, passed = boxes[k][2 * at : 2 * at + 24, :], boxes[k + 1][at : at + 24, :]
-        away = jnp.where(beyond == lax.bitwise_xor(chip, k), jnp.where(core == 0, direct, passed), away)
+        away = jnp.where(beyond == lax.bitwise_xor(chip, k), jnp.where(core == 1, direct, passed), away)
     for which, out in ((0, left), (1, right)):
         edge = jnp.where(core == which, away, facing)
         packed, small = edge[:16], edge[16:]
@@ -353,11 +353,11 @@
         if beside(k):
             up = lax.bitwise_xor(tile // 2, k) > tile // 2
             parts.append(jnp.where(up, away, outward))
-        swap = [(t, t ^ (2 * (k + t % 2))) for t in range(tiles)]
+        swap = [(t, t ^ (2 * (k + t % 2)) ^ 1) for t in range(tiles)]
         box = lax.ppermute(jnp.concatenate(parts), "tile", swap)
         boxes += [box, lax.ppermute(box[2 * share :], "tile", [(t, t ^ 1) for t in range(tiles)])]
-    swap = [(t, t ^ (2 * (chips - 1))) for t in range(tiles)]
-    boxes.append(lax.ppermute(jnp.concatenate(joined(chips - 1) + [away]), "tile", swap))
+    swap = [(t, t ^ (2 * (chips - 1)) ^ 1) for t in range(tiles)]
+    boxes.append(lax.ppermute(jnp.concatenate(joined(chips - 1) + [outward]), "tile", swap))
     message = near((5 + WET + 2) * 16, LANES)
     wet, left, right, *messages = pl.pallas_call(
         functools.partial(place_kernel, fields=fields),

time: 19.6 us -> 19.1 us (0.974)
  waiting for transfers between devices: 5.93 us -> 5.47 us
    ppermute x1, waiting for transfers between devices: 1.24 us -> 0.85 us  [local(): box = lax.ppermute(jnp.concatenate(parts), 'tile', swap)]
    ppermute x1, starting transfers between devices: 0.01 us -> 0.33 us  [local(): lax.ppermute(box[2 * share:], 'tile', [(t, t ^ 1) for t in range(tiles)])]
    ppermute x1, starting transfers between devices: 2.91 us -> 2.65 us  [local(): box = lax.ppermute(jnp.concatenate(parts), 'tile', swap)]
where the time goes in v7:
time: 19.1 us; the launch traced here: 18.9 us
  starting transfers between devices  7.08 us (37%)
  Pallas kernels  5.63 us (29%)
  waiting for transfers between devices  5.47 us (29%)
  between operations  0.68 us (4%)
    ppermute x1, starting transfers between devices, local(): box = lax.ppermute(jnp.concatenate(parts), 'tile', swap)  2.65 us
    ppermute x1, waiting for transfers between devices, local(): lax.ppermute(jnp.concatenate(joined(chips - 1) + [outward]), 'tile', swap)  2.19 us
    ppermute x3, starting transfers between devices, local(): lax.ppermute(x, ('comp', 'tile'), swaps(turn, comps, tiles))  2.15 us
    pallas_call x1, Pallas kernels, local(): pl.pallas_call(functools.partial(remap_kernel, tiles=tiles), out_shape=[n...  2.15 us
    pallas_call x1, Pallas kernels, local(): pl.pallas_call(functools.partial(cycle_kernel, comps=comps), out_shape=[p...  2.14 us
    ppermute x3, waiting for transfers between devices, local(): lax.ppermute(x, ('comp', 'tile'), swaps(turn, comps, tiles))  1.48 us
    ppermute x1, starting transfers between devices, local(): lax.ppermute(jnp.concatenate(joined(chips - 1) + [outward]), 'tile', swap)  1.43 us
    pallas_call x1, Pallas kernels, local(): pl.pallas_call(forcing_kernel, out_shape=jax.ShapeDtypeStruct((fields, ro...  0.97 us
  transfers between devices with their start and end apart: 7, of which 4 were waited for; matrix products, arithmetic and copies ran while one was open for 0% of the time, Pallas kernels for 5%

profile of v7, /device:TPU:0, one launch (start us, length us, event | category | flops | bytes accessed | tf_op | source)
XLA Modules:
  0.0 18.9 jit_solution(3623054361480975239)
XLA Ops:
  0.6 2.2 %remap.1 = (f32[368,128]{1,0:T(8,128)S(1)}, f32[160,128]{1,0:T(8,128)S(1)}) custom-call(f32[8,1024]{1,0:T(8,128)} %flux_far.1, f32[8,4,128,128]{3,2,1,0:T(8,128)} %weight.1, s32[4,8]{1,0:T(4,128)} %bitcast.2, s32[4,8]{1,0:T(4,128)} %bitcast.3, s32[8]{0:T(128)} %count_far.1, f32[32,128]{1,0:T(8,128)} %height.1, f32[32,128]{1,0:T(8,128)} %vel_x.1, ...), custom_call_target="tpu_custom_call" | custom-call | tf_op jit(solution)/shard_map/remap/pallas_call | solution.py:321
  2.8 0.5 %collective-permute-start = (f32[208,128]{1,0:T(8,128)S(1)}, f32[208,128]{1,0:T(8,128)S(1)}, u32[]{:S(2)}, u32[]{:S(2)}) collective-permute-start(f32[208,128]{1,0:T(8,128)S(1)} %slice.45), channel_id=1, source_target_pairs={{0,1},{1,0},{2,3},{3,2},{4,5},{5,4},{6,7},{7,6},{8,9},{9,8},{10,11... | collective-permute-start | bytes 319496 | tf_op jit(solution)/shard_map/ppermute | solution.py:342
  3.3 1.0 %collective-permute-done = f32[208,128]{1,0:T(8,128)S(1)} collective-permute-done((f32[208,128]{1,0:T(8,128)S(1)}, f32[208,128]{1,0:T(8,128)S(1)}, u32[]{:S(2)}, u32[]{:S(2)}) %collective-permute-start) | collective-permute-done | bytes 106528 | tf_op jit(solution)/shard_map/ppermute | solution.py:342
  4.3 2.7 %collective-permute-start.1 = (f32[184,128]{1,0:T(8,128)S(1)}, f32[184,128]{1,0:T(8,128)S(1)}, u32[]{:S(2)}, u32[]{:S(2)}) collective-permute-start(f32[184,128]{1,0:T(8,128)S(1)} %get-tuple-element.30), channel_id=1, source_target_pairs={{0,3},{1,4},{2,1},{3,6},{4,7},{5,0},{6,5},{7,2},{8,11},{9,12},{10,... | collective-permute-start | bytes 282632 | tf_op jit(solution)/shard_map/ppermute | solution.py:357
  7.0 1.4 %collective-permute-start.3 = (f32[104,128]{1,0:T(8,128)S(1)}, f32[104,128]{1,0:T(8,128)S(1)}, u32[]{:S(2)}, u32[]{:S(2)}) collective-permute-start(f32[104,128]{1,0:T(8,128)S(1)} %pad_maximum_fusion.1), channel_id=1, source_target_pairs={{0,7},{1,6},{2,5},{3,4},{4,3},{5,2},{6,1},{7,0},{8,15},{9,14},{10,... | collective-permute-start | bytes 159752 | tf_op jit(solution)/shard_map/ppermute | solution.py:360
  8.4 0.9 %collective-permute-done.1.refs_1_ = f32[184,128]{1,0:T(8,128)S(1)} collective-permute-done((f32[184,128]{1,0:T(8,128)S(1)}, f32[184,128]{1,0:T(8,128)S(1)}, u32[]{:S(2)}, u32[]{:S(2)}) %collective-permute-start.1) | collective-permute-done | bytes 94240 | tf_op jit(solution)/shard_map/ppermute | solution.py:357
  9.3 0.3 %collective-permute-start.2 = (f32[104,128]{1,0:T(8,128)S(1)}, f32[104,128]{1,0:T(8,128)S(1)}, u32[]{:S(2)}, u32[]{:S(2)}) collective-permute-start(f32[104,128]{1,0:T(8,128)S(1)} %slice.62), channel_id=1, source_target_pairs={{0,1},{1,0},{2,3},{3,2},{4,5},{5,4},{6,7},{7,6},{8,9},{9,8},{10,11... | collective-permute-start | bytes 159752 | tf_op jit(solution)/shard_map/ppermute | solution.py:358
  9.6 2.2 %collective-permute-done.3.refs_3_ = f32[104,128]{1,0:T(8,128)S(1)} collective-permute-done((f32[104,128]{1,0:T(8,128)S(1)}, f32[104,128]{1,0:T(8,128)S(1)}, u32[]{:S(2)}, u32[]{:S(2)}) %collective-permute-start.3) | collective-permute-done | bytes 53280 | tf_op jit(solution)/shard_map/ppermute | solution.py:360
  11.8 0.0 collective-permute-done.2.refs_2_
  11.8 0.4 %place.1 = (f32[96,128]{1,0:T(8,128)S(1)}, f32[32,128]{1,0:T(8,128)S(1)}, f32[32,128]{1,0:T(8,128)S(1)}, f32[160,128]{1,0:T(8,128)S(1)}, f32[160,128]{1,0:T(8,128)S(1)}, /*index=5*/f32[160,128]{1,0:T(8,128)S(1)}) custom-call(f32[104,128]{1,0:T(8,128)S(1)} %pad_maximum_fusion.refs_0_, f32[184,128]{1,0:T(8,128)S(1)} %collective-permute-done.1.refs_1_, ...), custom_call_target="tpu_custom_call" | custom-call | tf_op jit(solution)/shard_map/place/pallas_call | solution.py:362
  12.2 1.6 %collective-permute-start.4 = (f32[160,128]{1,0:T(8,128)S(1)}, f32[160,128]{1,0:T(8,128)S(1)}, u32[]{:S(2)}, u32[]{:S(2)}) collective-permute-start(f32[160,128]{1,0:T(8,128)S(1)} %get-tuple-element.20), channel_id=1, source_target_pairs={{0,8},{1,9},{2,10},{3,11},{4,12},{5,13},{6,14},{7,15},{8,0},{9,1},... | collective-permute-start | bytes 245768 | tf_op jit(solution)/shard_map/ppermute | solution.py:371
  13.8 0.0 collective-permute-start.5
  13.8 0.5 %collective-permute-start.6 = (f32[160,128]{1,0:T(8,128)S(1)}, f32[160,128]{1,0:T(8,128)S(1)}, u32[]{:S(2)}, u32[]{:S(2)}) collective-permute-start(f32[160,128]{1,0:T(8,128)S(1)} %get-tuple-element.22), channel_id=1, source_target_pairs={{0,1},{1,0},{2,3},{3,2},{4,5},{5,4},{6,7},{7,6},{8,9},{9,8},{10,11... | collective-permute-start | bytes 245768 | tf_op jit(solution)/shard_map/ppermute | solution.py:371
  14.3 1.0 %forcing.1 = f32[8,32,128]{2,1,0:T(8,128)} custom-call(f32[104,128]{1,0:T(8,128)S(1)} %pad_maximum_fusion.refs_0_, f32[184,128]{1,0:T(8,128)S(1)} %collective-permute-done.1.refs_1_, f32[104,128]{1,0:T(8,128)S(1)} %collective-permute-done.2.refs_2_, f32[104,128]{1,0:T(8,128)S(1)} %collective-permute-done.3.refs_3_, ...), custom_call_target="tpu_custom_call" | custom-call | flops 100000000 | bytes 4194304 | tf_op jit(solution)/shard_map/forcing/pallas_call | solution.py:374
  15.3 1.5 %collective-permute-done.4.refs_0_ = f32[160,128]{1,0:T(8,128)S(1)} collective-permute-done((f32[160,128]{1,0:T(8,128)S(1)}, f32[160,128]{1,0:T(8,128)S(1)}, u32[]{:S(2)}, u32[]{:S(2)}) %collective-permute-start.4) | collective-permute-done | bytes 81952 | tf_op jit(solution)/shard_map/ppermute | solution.py:371
  16.8 0.0 collective-permute-done.5.refs_1_
  16.8 0.0 collective-permute-done.6.refs_2_
  16.8 2.1 %cycles.1 = (f32[32,128]{1,0:T(8,128)}, f32[32,128]{1,0:T(8,128)}, f32[32,128]{1,0:T(8,128)}) custom-call(f32[160,128]{1,0:T(8,128)S(1)} %get-tuple-element.16.refs_4_.state, f32[96,128]{1,0:T(8,128)S(1)} %get-tuple-element.17.wet, f32[32,128]{1,0:T(8,128)S(1)} %get-tuple-element.18.left, f32[32,128]{1,0:T(8,128)S(1)} %get-tuple-element.19.right, ...), custom_call_target="tpu_custom_call" | custom-call | tf_op jit(solution)/shard_map/cycles/pallas_call | solution.py:383
  (9 shorter events, 0.1 us)
Async XLA Ops:
  2.8 1.5 %collective-permute-start = (f32[208,128]{1,0:T(8,128)S(1)}, f32[208,128]{1,0:T(8,128)S(1)}, u32[]{:S(2)}, u32[]{:S(2)}) collective-permute-start(f32[208,128]{1,0:T(8,128)S(1)} %slice.45), channel_id=1, source_target_pairs={{0,1},{1,0},{2,3},{3,2},{4,5},{5,4},{6,7},{7,6},{8,9},{9,8},{10,11... | collective-permute-start | bytes 319496 | tf_op jit(solution)/shard_map/ppermute | solution.py:342
  4.3 4.9 %collective-permute-start.1 = (f32[184,128]{1,0:T(8,128)S(1)}, f32[184,128]{1,0:T(8,128)S(1)}, u32[]{:S(2)}, u32[]{:S(2)}) collective-permute-start(f32[184,128]{1,0:T(8,128)S(1)} %get-tuple-element.30), channel_id=1, source_target_pairs={{0,3},{1,4},{2,1},{3,6},{4,7},{5,0},{6,5},{7,2},{8,11},{9,12},{10,... | collective-permute-start | bytes 282632 | tf_op jit(solution)/shard_map/ppermute | solution.py:357
  7.0 4.8 %collective-permute-start.3 = (f32[104,128]{1,0:T(8,128)S(1)}, f32[104,128]{1,0:T(8,128)S(1)}, u32[]{:S(2)}, u32[]{:S(2)}) collective-permute-start(f32[104,128]{1,0:T(8,128)S(1)} %pad_maximum_fusion.1), channel_id=1, source_target_pairs={{0,7},{1,6},{2,5},{3,4},{4,3},{5,2},{6,1},{7,0},{8,15},{9,14},{10,... | collective-permute-start | bytes 159752 | tf_op jit(solution)/shard_map/ppermute | solution.py:360
  9.3 2.5 %collective-permute-start.2 = (f32[104,128]{1,0:T(8,128)S(1)}, f32[104,128]{1,0:T(8,128)S(1)}, u32[]{:S(2)}, u32[]{:S(2)}) collective-permute-start(f32[104,128]{1,0:T(8,128)S(1)} %slice.62), channel_id=1, source_target_pairs={{0,1},{1,0},{2,3},{3,2},{4,5},{5,4},{6,7},{7,6},{8,9},{9,8},{10,11... | collective-permute-start | bytes 159752 | tf_op jit(solution)/shard_map/ppermute | solution.py:358
  12.2 4.6 %collective-permute-start.4 = (f32[160,128]{1,0:T(8,128)S(1)}, f32[160,128]{1,0:T(8,128)S(1)}, u32[]{:S(2)}, u32[]{:S(2)}) collective-permute-start(f32[160,128]{1,0:T(8,128)S(1)} %get-tuple-element.20), channel_id=1, source_target_pairs={{0,8},{1,9},{2,10},{3,11},{4,12},{5,13},{6,14},{7,15},{8,0},{9,1},... | collective-permute-start | bytes 245768 | tf_op jit(solution)/shard_map/ppermute | solution.py:371
  13.8 3.0 %collective-permute-start.5 = (f32[160,128]{1,0:T(8,128)S(1)}, f32[160,128]{1,0:T(8,128)S(1)}, u32[]{:S(2)}, u32[]{:S(2)}) collective-permute-start(f32[160,128]{1,0:T(8,128)S(1)} %get-tuple-element.21), channel_id=1, source_target_pairs={{0,1},{1,0},{2,3},{3,2},{4,5},{5,4},{6,7},{7,6},{8,16},{9,17},{10,... | collective-permute-start | bytes 245768 | tf_op jit(solution)/shard_map/ppermute | solution.py:371
  13.8 3.0 %collective-permute-start.6 = (f32[160,128]{1,0:T(8,128)S(1)}, f32[160,128]{1,0:T(8,128)S(1)}, u32[]{:S(2)}, u32[]{:S(2)}) collective-permute-start(f32[160,128]{1,0:T(8,128)S(1)} %get-tuple-element.22), channel_id=1, source_target_pairs={{0,1},{1,0},{2,3},{3,2},{4,5},{5,4},{6,7},{7,6},{8,9},{9,8},{10,11... | collective-permute-start | bytes 245768 | tf_op jit(solution)/shard_map/ppermute | solution.py:371

commit v8 on v7

--- a/solution.py
+++ b/solution.py
@@ -118,19 +118,20 @@
 
     for t in range(tiles):
         lefts, rights = max(t - 1, 0), min(t + 1, tiles - 1)
-        out = jnp.zeros((8, LANES), F32)
-        for f in range(WET):
-            to = 64 + 16 * f
-            part_l = held[pl.ds(lefts * values + f, CAP, stride=fields), :]
-            part_r = held[pl.ds(rights * values + f, CAP, stride=fields), :]
-            part_l = pltpu.roll(part_l, (to - (LANES - HALO)) % LANES, 1)
-            part_r = pltpu.roll(part_r, to, 1)
-            part = jnp.concatenate([part_l, part_r], axis=0)
-            out = jnp.where((lane8 >= to) & (lane8 < to + 16), part, out)
         sender, place = route(lax.bitwise_xor(chip, t // 2), t % 2, chips)
         mine = core == sender
         offset = place * share
         shift = jnp.where(mine, 0, CAP)
+        first_lane = jnp.where(mine, 0, 64)
+        out = jnp.zeros((8, LANES), F32)
+        for f in range(WET):
+            to = first_lane + 16 * f
+            part_l = held[pl.ds(lefts * values + f, CAP, stride=fields), :]
+            part_r = held[pl.ds(rights * values + f, CAP, stride=fields), :]
+            part_l = pltpu.roll(part_l, to + HALO, 1)
+            part_r = pltpu.roll(part_r, to, 1)
+            part = jnp.concatenate([part_l, part_r], axis=0)
+            out = jnp.where((lane8 >= to) & (lane8 < to + 16), part, out)
         side = jnp.full((8, LANES), -1, jnp.int32)
         main = jnp.zeros((8, LANES), jnp.int32)
         for r in range(CAP):
@@ -140,7 +141,7 @@
                 named = table[rights * CAP + r]
                 side = jnp.where(row8 == CAP + r, jnp.where(named < 0, -1, named + 32), side)
             main = jnp.where(row8 == r + shift, table[t * CAP + r], main)
-        out = jnp.where(lane8 == 112, side.astype(F32), out)
+        out = jnp.where(lane8 == first_lane + 48, side.astype(F32), out)
         out = jnp.where(lane8 == 113, main.astype(F32), out)
         at_names = jnp.where(mine, offset, chips * share + offset + values)
         at_values = jnp.where(mine, offset + 8, chips * share + offset)
@@ -170,19 +171,18 @@
     return jnp.concatenate([box[pl.ds(8 + f, 2 * CAP, stride=fields), :] for box in boxes], axis=0)
 
 
-def names_of(box, values):
-    return box[0:8, :], box[8 + 2 * values : 16 + 2 * values, :]
-
-
-def hot_slots(boxes, values, rows):
-    ids = [sum(names_of(box, values)) for box in boxes]
-    return one_hot(jnp.concatenate(ids, axis=0)[:, 113:114])[:rows]
+def names_of(boxes):
+    return jnp.concatenate([box[0:8, :] for box in boxes], axis=0)
+
+
+def hot_slots(names, rows):
+    return one_hot(names[:, 113:114])[:rows]
 
 
 def forcing_kernel(*refs):
     boxes, state, forcing = refs[:-2], refs[-2], refs[-1]
     fields, rows = forcing.shape[:2]
-    hot = hot_slots(boxes, CAP * fields, rows)
+    hot = hot_slots(names_of(boxes), rows)
     sea = state[4 * rows : 5 * rows]
     for f in range(fields):
         forcing[f] = spread(hot, field_values(boxes, f, fields)) * sea
@@ -194,18 +194,18 @@
     rows = left.shape[0]
     chips = len(boxes)
     values = CAP * fields
-    names = jnp.concatenate([x for box in boxes for x in names_of(box, values)], axis=0)
-    hot_side = one_hot(names[:, 112:113])[: 2 * rows]
-    hot_main = hot_slots(boxes, values, rows)
+    names = names_of(boxes)
+    hot_mine, hot_other = (one_hot(names[:, at : at + 1])[: 2 * rows] for at in (48, 112))
+    hot_main = hot_slots(names, rows)
     sea = state[4 * rows : 5 * rows]
     for f in range(WET):
         wet[f * rows : (f + 1) * rows] = spread(hot_main, field_values(boxes, f, fields)) * sea
-    sides = spread(hot_side, names)
+    sides = pltpu.roll(spread(hot_mine, names), 80, 1) + pltpu.roll(spread(hot_other, names), 16, 1)
     lane = lanes_of(rows)
     me = lax.axis_index("tile")
     core, chip = me % 2, me // 2
     beyond = jnp.where(core == 0, chip - 1, chip + 1)
-    at = 16 + 2 * values
+    at = 8 + 2 * values
     facing, away = boxes[0][at : at + 24, :], boxes[-1][at : at + 24, :]
     for k in filter(beside, pairs_of(chips)):
         direct, passed = boxes[k][2 * at : 2 * at + 24, :], boxes[k + 1][at : at + 24, :]
@@ -217,7 +217,7 @@
         sea_part = jnp.concatenate(
             [pltpu.roll(small, (64 - 16 * g) % LANES, 1) for g in range(4)], axis=0
         )
-        driven = pltpu.roll(sides[which * rows : (which + 1) * rows], 16, 1)
+        driven = sides[which * rows : (which + 1) * rows]
         full = jnp.where(lane < 64, whole, jnp.where(lane < 80, sea_part, driven))
         exists = (me > 0) if which == 0 else (me < 2 * chips - 1)
         full = jnp.where(exists, full, 0.0)
@@ -254,10 +254,11 @@
         center = jnp.concatenate(
             [above[16 * q : 16 * q + 16], own[q], below[16 * q : 16 * q + 16]], axis=0
         )
-        from_l = pltpu.roll(side_l, (LANES - HALO - 16 * q) % LANES, 1)
-        from_r = pltpu.roll(side_r, (LANES - 16 * q) % LANES, 1)
-        side = jnp.where(lane < HALO, from_r, jnp.where(lane >= LANES - HALO, from_l, 0.0))
-        wide.append(jnp.concatenate([center, side], axis=1))
+        from_l = pltpu.roll(side_l, (LANES - 16 * q) % LANES, 1)
+        from_r = pltpu.roll(side_r, (LANES - HALO - 16 * q) % LANES, 1)
+        west = jnp.where(lane < HALO, from_l, pltpu.roll(center, HALO, 1))
+        east = jnp.where(lane < LANES - HALO, pltpu.roll(center, LANES - HALO, 1), from_r)
+        wide.append(jnp.concatenate([west, east], axis=1))
     eta, u, v, deep, sea, push_x, push_y, rain = wide
     shape = (total, 2 * LANES)
     row = lax.axis_index("comp") * rows - HALO + lax.broadcasted_iota(jnp.int32, shape, 0)
@@ -273,22 +274,31 @@
     deep = 0.2 * deep
 
     def cols(x):
-        return pltpu.roll(x, 2 * LANES - 1, 1) - pltpu.roll(x, 1, 1)
+        spans = (x[:, :LANES], x[:, LANES:])
+        return jnp.concatenate([pltpu.roll(y, LANES - 1, 1) - pltpu.roll(y, 1, 1) for y in spans], axis=1)
 
     def lines(x):
-        return pltpu.roll(x, total - 1, 0) - pltpu.roll(x, 1, 0)
+        return pltpu.roll(x, x.shape[0] - 1, 0) - pltpu.roll(x, 1, 0)
 
     through_x, through_y = deep * u, deep * v
     eta, u, v = sea * eta, sea * u, sea * v
-    for _ in range(NSUB):
+    top = HALO
+    for cycle in range(NSUB):
         eta = eta + fresh - sea * (cols(through_x) + lines(through_y))
-        next_u = 0.98 * u - slope * cols(eta) + turn * v + wind_x
-        next_v = 0.98 * v - slope * lines(eta) - turn * u + wind_y
+        slope_x, slope_y = cols(eta), lines(eta)
+        if cycle == NSUB // 2 - 1:
+            top = HALO // 2
+            fields = (eta, u, v, sea, slope, turn, fresh, wind_x, wind_y, deep, slope_x, slope_y)
+            fields = [x[HALO - top : total - HALO + top] for x in fields]
+            eta, u, v, sea, slope, turn, fresh, wind_x, wind_y, deep, slope_x, slope_y = fields
+        next_u = 0.98 * u - slope * slope_x + turn * v + wind_x
+        next_v = 0.98 * v - slope * slope_y - turn * u + wind_y
         u, v = next_u, next_v
         through_x, through_y = deep * u, deep * v
-    height_out[...] = eta[HALO : HALO + rows, :LANES]
-    flow_x[...] = u[HALO : HALO + rows, :LANES]
-    flow_y[...] = v[HALO : HALO + rows, :LANES]
+    half = lanes_of(rows) < LANES // 2
+    for out, field in ((height_out, eta), (flow_x, u), (flow_y, v)):
+        west, east = field[top : top + rows, :LANES], field[top : top + rows, LANES:]
+        out[...] = jnp.where(half, pltpu.roll(west, LANES - HALO, 1), pltpu.roll(east, HALO, 1))
 
 
 def swaps(turn, comps, tiles):
@@ -343,7 +353,8 @@
     away, facing = other[chips * share : chips * share + 24], other[chips * share + 24 :]
 
     def joined(place):
-        return [x[place * share : (place + 1) * share] for x in (mine, other)]
+        left, right = (x[place * share : (place + 1) * share] for x in (mine, other))
+        return [left[:8] + right[values:], left[8:], right[:values]]
 
     tile = lax.axis_index("tile")
     outward = send[2 * chips * share : 2 * chips * share + 24]
@@ -355,7 +366,7 @@
             parts.append(jnp.where(up, away, outward))
         swap = [(t, t ^ (2 * (k + t % 2)) ^ 1) for t in range(tiles)]
         box = lax.ppermute(jnp.concatenate(parts), "tile", swap)
-        boxes += [box, lax.ppermute(box[2 * share :], "tile", [(t, t ^ 1) for t in range(tiles)])]
+        boxes += [box, lax.ppermute(box[8 + 2 * values :], "tile", [(t, t ^ 1) for t in range(tiles)])]
     swap = [(t, t ^ (2 * (chips - 1)) ^ 1) for t in range(tiles)]
     boxes.append(lax.ppermute(jnp.concatenate(joined(chips - 1) + [outward]), "tile", swap))
     message = near((5 + WET + 2) * 16, LANES)

time: 19.1 us -> 18.9 us (0.990)
  no operation moved by 1% of the time
where the time goes in v8:
time: 18.9 us; the launch traced here: 18.7 us
  starting transfers between devices  7.09 us (38%)
  Pallas kernels  5.59 us (30%)
  waiting for transfers between devices  5.3 us (28%)
  between operations  0.69 us (4%)
    ppermute x1, starting transfers between devices, local(): box = lax.ppermute(jnp.concatenate(parts), 'tile', swap)  2.65 us
    ppermute x3, starting transfers between devices, local(): lax.ppermute(x, ('comp', 'tile'), swaps(turn, comps, tiles))  2.15 us
    pallas_call x1, Pallas kernels, local(): pl.pallas_call(functools.partial(remap_kernel, tiles=tiles), out_shape=[n...  2.14 us
    pallas_call x1, Pallas kernels, local(): pl.pallas_call(functools.partial(cycle_kernel, comps=comps), out_shape=[p...  2.09 us
    ppermute x1, waiting for transfers between devices, local(): lax.ppermute(jnp.concatenate(joined(chips - 1) + [outward]), 'tile', swap)  2 us
    ppermute x3, waiting for transfers between devices, local(): lax.ppermute(x, ('comp', 'tile'), swaps(turn, comps, tiles))  1.58 us
    ppermute x1, starting transfers between devices, local(): lax.ppermute(jnp.concatenate(joined(chips - 1) + [outward]), 'tile', swap)  1.43 us
    pallas_call x1, Pallas kernels, local(): pl.pallas_call(forcing_kernel, out_shape=jax.ShapeDtypeStruct((fields, ro...  0.96 us
  transfers between devices with their start and end apart: 7, of which 4 were waited for; matrix products, arithmetic and copies ran while one was open for 0% of the time, Pallas kernels for 5%

profile of v8, /device:TPU:0, one launch (start us, length us, event | category | flops | bytes accessed | tf_op | source)
XLA Modules:
  0.0 18.7 jit_solution(3050246366454688030)
XLA Ops:
  0.6 2.1 %remap.1 = (f32[368,128]{1,0:T(8,128)S(1)}, f32[160,128]{1,0:T(8,128)S(1)}) custom-call(f32[8,1024]{1,0:T(8,128)} %flux_far.1, f32[8,4,128,128]{3,2,1,0:T(8,128)} %weight.1, s32[4,8]{1,0:T(4,128)} %bitcast.2, s32[4,8]{1,0:T(4,128)} %bitcast.3, s32[8]{0:T(128)} %count_far.1, f32[32,128]{1,0:T(8,128)} %height.1, f32[32,128]{1,0:T(8,128)} %vel_x.1, ...), custom_call_target="tpu_custom_call" | custom-call | tf_op jit(solution)/shard_map/remap/pallas_call | solution.py:331
  2.8 0.5 %collective-permute-start = (f32[208,128]{1,0:T(8,128)S(1)}, f32[208,128]{1,0:T(8,128)S(1)}, u32[]{:S(2)}, u32[]{:S(2)}) collective-permute-start(f32[208,128]{1,0:T(8,128)S(1)} %slice.93), channel_id=1, source_target_pairs={{0,1},{1,0},{2,3},{3,2},{4,5},{5,4},{6,7},{7,6},{8,9},{9,8},{10,11... | collective-permute-start | bytes 319496 | tf_op jit(solution)/shard_map/ppermute | solution.py:352
  3.3 1.0 %collective-permute-done = f32[208,128]{1,0:T(8,128)S(1)} collective-permute-done((f32[208,128]{1,0:T(8,128)S(1)}, f32[208,128]{1,0:T(8,128)S(1)}, u32[]{:S(2)}, u32[]{:S(2)}) %collective-permute-start) | collective-permute-done | bytes 106528 | tf_op jit(solution)/shard_map/ppermute | solution.py:352
  4.3 2.7 %collective-permute-start.1 = (f32[168,128]{1,0:T(8,128)S(1)}, f32[168,128]{1,0:T(8,128)S(1)}, u32[]{:S(2)}, u32[]{:S(2)}) collective-permute-start(f32[168,128]{1,0:T(8,128)S(1)} %get-tuple-element.33), channel_id=1, source_target_pairs={{0,3},{1,4},{2,1},{3,6},{4,7},{5,0},{6,5},{7,2},{8,11},{9,12},{10,... | collective-permute-start | bytes 258056 | tf_op jit(solution)/shard_map/ppermute | solution.py:368
  7.0 1.4 %collective-permute-start.3 = (f32[96,128]{1,0:T(8,128)S(1)}, f32[96,128]{1,0:T(8,128)S(1)}, u32[]{:S(2)}, u32[]{:S(2)}) collective-permute-start(f32[96,128]{1,0:T(8,128)S(1)} %pad_maximum_fusion.1), channel_id=1, source_target_pairs={{0,7},{1,6},{2,5},{3,4},{4,3},{5,2},{6,1},{7,0},{8,15},{9,14},{10,... | collective-permute-start | bytes 147464 | tf_op jit(solution)/shard_map/ppermute | solution.py:371
  8.4 0.8 %collective-permute-done.1.refs_1_ = f32[168,128]{1,0:T(8,128)S(1)} collective-permute-done((f32[168,128]{1,0:T(8,128)S(1)}, f32[168,128]{1,0:T(8,128)S(1)}, u32[]{:S(2)}, u32[]{:S(2)}) %collective-permute-start.1) | collective-permute-done | bytes 86048 | tf_op jit(solution)/shard_map/ppermute | solution.py:368
  9.2 0.3 %collective-permute-start.2 = (f32[96,128]{1,0:T(8,128)S(1)}, f32[96,128]{1,0:T(8,128)S(1)}, u32[]{:S(2)}, u32[]{:S(2)}) collective-permute-start(f32[96,128]{1,0:T(8,128)S(1)} %slice.121), channel_id=1, source_target_pairs={{0,1},{1,0},{2,3},{3,2},{4,5},{5,4},{6,7},{7,6},{8,9},{9,8},{10,11... | collective-permute-start | bytes 147464 | tf_op jit(solution)/shard_map/ppermute | solution.py:369
  9.5 2.0 %collective-permute-done.3.refs_3_ = f32[96,128]{1,0:T(8,128)S(1)} collective-permute-done((f32[96,128]{1,0:T(8,128)S(1)}, f32[96,128]{1,0:T(8,128)S(1)}, u32[]{:S(2)}, u32[]{:S(2)}) %collective-permute-start.3) | collective-permute-done | bytes 49184 | tf_op jit(solution)/shard_map/ppermute | solution.py:371
  11.5 0.0 collective-permute-done.2.refs_2_
  11.5 0.4 %place.1 = (f32[96,128]{1,0:T(8,128)S(1)}, f32[32,128]{1,0:T(8,128)S(1)}, f32[32,128]{1,0:T(8,128)S(1)}, f32[160,128]{1,0:T(8,128)S(1)}, f32[160,128]{1,0:T(8,128)S(1)}, /*index=5*/f32[160,128]{1,0:T(8,128)S(1)}) custom-call(f32[96,128]{1,0:T(8,128)S(1)} %pad_maximum_fusion.refs_0_, f32[168,128]{1,0:T(8,128)S(1)} %collective-permute-done.1.refs_1_, ...), custom_call_target="tpu_custom_call" | custom-call | tf_op jit(solution)/shard_map/place/pallas_call | solution.py:373
  11.9 1.6 %collective-permute-start.4 = (f32[160,128]{1,0:T(8,128)S(1)}, f32[160,128]{1,0:T(8,128)S(1)}, u32[]{:S(2)}, u32[]{:S(2)}) collective-permute-start(f32[160,128]{1,0:T(8,128)S(1)} %get-tuple-element.20), channel_id=1, source_target_pairs={{0,8},{1,9},{2,10},{3,11},{4,12},{5,13},{6,14},{7,15},{8,0},{9,1},... | collective-permute-start | bytes 245768 | tf_op jit(solution)/shard_map/ppermute | solution.py:382
  13.6 0.0 collective-permute-start.5
  13.6 0.5 %collective-permute-start.6 = (f32[160,128]{1,0:T(8,128)S(1)}, f32[160,128]{1,0:T(8,128)S(1)}, u32[]{:S(2)}, u32[]{:S(2)}) collective-permute-start(f32[160,128]{1,0:T(8,128)S(1)} %get-tuple-element.22), channel_id=1, source_target_pairs={{0,1},{1,0},{2,3},{3,2},{4,5},{5,4},{6,7},{7,6},{8,9},{9,8},{10,11... | collective-permute-start | bytes 245768 | tf_op jit(solution)/shard_map/ppermute | solution.py:382
  14.1 1.0 %forcing.1 = f32[8,32,128]{2,1,0:T(8,128)} custom-call(f32[96,128]{1,0:T(8,128)S(1)} %pad_maximum_fusion.refs_0_, f32[168,128]{1,0:T(8,128)S(1)} %collective-permute-done.1.refs_1_, f32[96,128]{1,0:T(8,128)S(1)} %collective-permute-done.2.refs_2_, f32[96,128]{1,0:T(8,128)S(1)} %collective-permute-done.3.refs_3_, f32[160,128]{1,0:T(8,128)S(1)} %get-tuple-element.16.refs_4_.state), custom_call_target="tpu_custom_call" | custom-call | flops 100000000 | bytes 4194304 | tf_op jit(solution)/shard_map/forcing/pallas_call | solution.py:385
  15.0 1.6 %collective-permute-done.4.refs_0_ = f32[160,128]{1,0:T(8,128)S(1)} collective-permute-done((f32[160,128]{1,0:T(8,128)S(1)}, f32[160,128]{1,0:T(8,128)S(1)}, u32[]{:S(2)}, u32[]{:S(2)}) %collective-permute-start.4) | collective-permute-done | bytes 81952 | tf_op jit(solution)/shard_map/ppermute | solution.py:382
  16.6 0.0 collective-permute-done.5.refs_1_
  16.6 0.0 collective-permute-done.6.refs_2_
  16.6 2.1 %cycles.1 = (f32[32,128]{1,0:T(8,128)}, f32[32,128]{1,0:T(8,128)}, f32[32,128]{1,0:T(8,128)}) custom-call(f32[160,128]{1,0:T(8,128)S(1)} %get-tuple-element.16.refs_4_.state, f32[96,128]{1,0:T(8,128)S(1)} %get-tuple-element.17.wet, f32[32,128]{1,0:T(8,128)S(1)} %get-tuple-element.18.left, f32[32,128]{1,0:T(8,128)S(1)} %get-tuple-element.19.right, ...), custom_call_target="tpu_custom_call" | custom-call | tf_op jit(solution)/shard_map/cycles/pallas_call | solution.py:394
  (11 shorter events, 0.1 us)
Async XLA Ops:
  2.8 1.5 %collective-permute-start = (f32[208,128]{1,0:T(8,128)S(1)}, f32[208,128]{1,0:T(8,128)S(1)}, u32[]{:S(2)}, u32[]{:S(2)}) collective-permute-start(f32[208,128]{1,0:T(8,128)S(1)} %slice.93), channel_id=1, source_target_pairs={{0,1},{1,0},{2,3},{3,2},{4,5},{5,4},{6,7},{7,6},{8,9},{9,8},{10,11... | collective-permute-start | bytes 319496 | tf_op jit(solution)/shard_map/ppermute | solution.py:352
  4.3 4.9 %collective-permute-start.1 = (f32[168,128]{1,0:T(8,128)S(1)}, f32[168,128]{1,0:T(8,128)S(1)}, u32[]{:S(2)}, u32[]{:S(2)}) collective-permute-start(f32[168,128]{1,0:T(8,128)S(1)} %get-tuple-element.33), channel_id=1, source_target_pairs={{0,3},{1,4},{2,1},{3,6},{4,7},{5,0},{6,5},{7,2},{8,11},{9,12},{10,... | collective-permute-start | bytes 258056 | tf_op jit(solution)/shard_map/ppermute | solution.py:368
  7.0 4.5 %collective-permute-start.3 = (f32[96,128]{1,0:T(8,128)S(1)}, f32[96,128]{1,0:T(8,128)S(1)}, u32[]{:S(2)}, u32[]{:S(2)}) collective-permute-start(f32[96,128]{1,0:T(8,128)S(1)} %pad_maximum_fusion.1), channel_id=1, source_target_pairs={{0,7},{1,6},{2,5},{3,4},{4,3},{5,2},{6,1},{7,0},{8,15},{9,14},{10,... | collective-permute-start | bytes 147464 | tf_op jit(solution)/shard_map/ppermute | solution.py:371
  9.2 2.3 %collective-permute-start.2 = (f32[96,128]{1,0:T(8,128)S(1)}, f32[96,128]{1,0:T(8,128)S(1)}, u32[]{:S(2)}, u32[]{:S(2)}) collective-permute-start(f32[96,128]{1,0:T(8,128)S(1)} %slice.121), channel_id=1, source_target_pairs={{0,1},{1,0},{2,3},{3,2},{4,5},{5,4},{6,7},{7,6},{8,9},{9,8},{10,11... | collective-permute-start | bytes 147464 | tf_op jit(solution)/shard_map/ppermute | solution.py:369
  11.9 4.7 %collective-permute-start.4 = (f32[160,128]{1,0:T(8,128)S(1)}, f32[160,128]{1,0:T(8,128)S(1)}, u32[]{:S(2)}, u32[]{:S(2)}) collective-permute-start(f32[160,128]{1,0:T(8,128)S(1)} %get-tuple-element.20), channel_id=1, source_target_pairs={{0,8},{1,9},{2,10},{3,11},{4,12},{5,13},{6,14},{7,15},{8,0},{9,1},... | collective-permute-start | bytes 245768 | tf_op jit(solution)/shard_map/ppermute | solution.py:382
  13.6 3.1 %collective-permute-start.5 = (f32[160,128]{1,0:T(8,128)S(1)}, f32[160,128]{1,0:T(8,128)S(1)}, u32[]{:S(2)}, u32[]{:S(2)}) collective-permute-start(f32[160,128]{1,0:T(8,128)S(1)} %get-tuple-element.21), channel_id=1, source_target_pairs={{0,1},{1,0},{2,3},{3,2},{4,5},{5,4},{6,7},{7,6},{8,16},{9,17},{10,... | collective-permute-start | bytes 245768 | tf_op jit(solution)/shard_map/ppermute | solution.py:382
  13.6 3.1 %collective-permute-start.6 = (f32[160,128]{1,0:T(8,128)S(1)}, f32[160,128]{1,0:T(8,128)S(1)}, u32[]{:S(2)}, u32[]{:S(2)}) collective-permute-start(f32[160,128]{1,0:T(8,128)S(1)} %get-tuple-element.22), channel_id=1, source_target_pairs={{0,1},{1,0},{2,3},{3,2},{4,5},{5,4},{6,7},{7,6},{8,9},{9,8},{10,11... | collective-permute-start | bytes 245768 | tf_op jit(solution)/shard_map/ppermute | solution.py:382

commit v9 on v8

--- a/solution.py
+++ b/solution.py
@@ -11,7 +11,8 @@
 HALO = 2 * NSUB
 CAP = 4
 LANES = 128
-ROUNDS = 3
+EARLY = 3
+ROUNDS = 2
 WET = 3
 F32 = jnp.float32
 BF16 = jnp.bfloat16
@@ -38,8 +39,10 @@
 
 def remap_kernel(
     flux_far, weight, tile_far, block_far, count_far, height, vel_x, vel_y, depth, mask,
-    send, own, flux, stage, held, dest_tile, dest_block, count, sea_int, table, seen, sems, *, tiles,
+    send, own, *refs, tiles,
 ):
+    early = refs[:EARLY]
+    flux, stage, held, dest_tile, dest_block, count, sea_int, table, seen, sems = refs[EARLY:]
     slots, blocks = dest_tile.shape
     fields, rows = flux.shape[0], height.shape[0]
     values = CAP * fields
@@ -73,6 +76,10 @@
     state = [own[q * rows : (q + 1) * rows] for q in range(4)]
     sea = sea_int[...].astype(F32)
     own[4 * rows : 5 * rows] = sea
+    for turn, message in enumerate(early):
+        low = lax.rem(lax.axis_index("comp"), EARLY) == turn
+        for q, x in enumerate(state + [sea]):
+            message[q * HALO : (q + 1) * HALO, :] = jnp.where(low, x[rows - HALO :], x[:HALO])
     lane16 = lanes_of(16)
     lane8 = lanes_of(8)
     row8 = lax.broadcasted_iota(jnp.int32, (8, LANES), 0)
@@ -225,7 +232,7 @@
     section = lax.axis_index("comp")
     for turn, message in enumerate(messages):
         start = pl.multiple_of(jnp.where(lax.rem(section, ROUNDS) == turn, rows - HALO, 0), 8)
-        parts = [(state, q) for q in range(5)] + [(wet, f) for f in range(WET)] + [(left, 0), (right, 0)]
+        parts = [(wet, f) for f in range(WET)] + [(left, 0), (right, 0)]
         for i, (ref, q) in enumerate(parts):
             message[i * HALO : (i + 1) * HALO, :] = ref[pl.ds(q * rows + start, HALO), :]
 
@@ -233,14 +240,20 @@
 def cycle_kernel(
     state, wet, left, right, *refs, comps
 ):
-    height_out, flow_x, flow_y = refs[ROUNDS:]
+    height_out, flow_x, flow_y = refs[EARLY + ROUNDS :]
     rows = height_out.shape[0]
     section = lax.axis_index("comp")
-    messages = [ref[...] for ref in refs[:ROUNDS]]
-    below, above = messages[0], messages[0]
-    for turn in range(1, ROUNDS):
-        below = jnp.where(lax.rem(section, ROUNDS) == turn, messages[turn], below)
-        above = jnp.where(lax.rem(section + ROUNDS - 1, ROUNDS) == turn, messages[turn], above)
+
+    def halves_of(messages):
+        turns = len(messages)
+        below, above = messages[0][...], messages[0][...]
+        for turn in range(1, turns):
+            below = jnp.where(lax.rem(section, turns) == turn, messages[turn][...], below)
+            above = jnp.where(lax.rem(section + turns - 1, turns) == turn, messages[turn][...], above)
+        return above, below
+
+    parts = zip(halves_of(refs[:EARLY]), halves_of(refs[EARLY : EARLY + ROUNDS]))
+    above, below = (jnp.concatenate(part, axis=0) for part in parts)
     total = rows + 2 * HALO
     count = 5 + WET
     own = [state[q * rows : (q + 1) * rows] for q in range(5)]
@@ -301,10 +314,10 @@
         out[...] = jnp.where(half, pltpu.roll(west, LANES - HALO, 1), pltpu.roll(east, HALO, 1))
 
 
-def swaps(turn, comps, tiles):
+def swaps(turn, rounds, comps, tiles):
     pairs = []
     for s in range(comps):
-        other = s + 1 if s % ROUNDS == turn else s - 1 if (s - 1) % ROUNDS == turn else -1
+        other = s + 1 if s % rounds == turn else s - 1 if (s - 1) % rounds == turn else -1
         for t in range(tiles):
             there = other * tiles + t if 0 <= other < comps else s * tiles + (t ^ 1)
             pairs.append((s * tiles + t, there))
@@ -328,11 +341,11 @@
     values = CAP * fields
     share = values + 8
     chips = tiles // 2
-    send, own = pl.pallas_call(
+    send, own, *early = pl.pallas_call(
         functools.partial(remap_kernel, tiles=tiles),
-        out_shape=[near(2 * chips * share + 48, LANES), near(5 * rows, cols)],
+        out_shape=[near(2 * chips * share + 48, LANES), near(5 * rows, cols)] + [near(5 * HALO, LANES)] * EARLY,
         in_specs=[HBM] * 10,
-        out_specs=[VMEM] * 2,
+        out_specs=[VMEM] * (2 + EARLY),
         scratch_shapes=[
             pltpu.VMEM(flux.shape, F32),
             pltpu.VMEM(weight.shape, F32),
@@ -369,7 +382,9 @@
         boxes += [box, lax.ppermute(box[8 + 2 * values :], "tile", [(t, t ^ 1) for t in range(tiles)])]
     swap = [(t, t ^ (2 * (chips - 1)) ^ 1) for t in range(tiles)]
     boxes.append(lax.ppermute(jnp.concatenate(joined(chips - 1) + [outward]), "tile", swap))
-    message = near((5 + WET + 2) * 16, LANES)
+    message = near((WET + 2) * HALO, LANES)
+    early, boxes[1] = lax.optimization_barrier((early, boxes[1]))
+    early = [lax.ppermute(x, ("comp", "tile"), swaps(turn, EARLY, comps, tiles)) for turn, x in enumerate(early)]
     wet, left, right, *messages = pl.pallas_call(
         functools.partial(place_kernel, fields=fields),
         out_shape=[near(WET * rows, cols), near(rows, cols), near(rows, cols)] + [message] * ROUNDS,
@@ -379,7 +394,7 @@
         name="place",
     )(*boxes, own)
     received = [
-        lax.ppermute(x, ("comp", "tile"), swaps(turn, comps, tiles))
+        lax.ppermute(x, ("comp", "tile"), swaps(turn, ROUNDS, comps, tiles))
         for turn, x in enumerate(messages)
     ]
     forcing = pl.pallas_call(
@@ -394,11 +409,11 @@
     outs = pl.pallas_call(
         functools.partial(cycle_kernel, comps=comps),
         out_shape=[plane] * 3,
-        in_specs=[VMEM] * (4 + ROUNDS),
+        in_specs=[VMEM] * (4 + EARLY + ROUNDS),
         out_specs=[VMEM] * 3,
         compiler_params=params,
         name="cycles",
-    )(own, wet, left, right, *received)
+    )(own, wet, left, right, *early, *received)
     return (forcing, *outs)
 
 

time: 18.9 us -> 18.7 us (0.989)
  waiting for transfers between devices: 5.3 us -> 3.11 us
  starting transfers between devices: 7.09 us -> 9.04 us
    ppermute x1, waiting for transfers between devices: 2 us -> 0.01 us  [local(): lax.ppermute(jnp.concatenate(joined(chips - 1) + [outward]), 'tile', swap)]
    ppermute x3 -> x5, starting transfers between devices: 2.15 us -> 4.09 us  [the longest x3 2.38 us: local(): lax.ppermute(x, ('comp', 'tile'), swaps(turn, EARLY, comps, tiles))]
    ppermute x3 -> x5, waiting for transfers between devices: 1.58 us -> 1.39 us  [the longest x2 1.38 us: local(): lax.ppermute(x, ('comp', 'tile'), swaps(turn, ROUNDS, comps, tiles))]
  transfers between devices with their start and end apart: 7 -> 9, of which waited for: 4 -> 3; matrix products, arithmetic and copies ran while one was open for 0% -> 0% of each run, Pallas kernels for 5% -> 7%
where the time goes in v9:
time: 18.7 us; the launch traced here: 18.5 us
  starting transfers between devices  9.04 us (48%)
  Pallas kernels  5.59 us (30%)
  waiting for transfers between devices  3.11 us (17%)
  between operations  0.7 us (4%)
    ppermute x1, starting transfers between devices, local(): box = lax.ppermute(jnp.concatenate(parts), 'tile', swap)  2.66 us
    ppermute x3, starting transfers between devices, local(): lax.ppermute(x, ('comp', 'tile'), swaps(turn, EARLY, comps, tiles))  2.38 us
    pallas_call x1, Pallas kernels, local(): pl.pallas_call(functools.partial(remap_kernel, tiles=tiles), out_shape=[n...  2.14 us
    pallas_call x1, Pallas kernels, local(): pl.pallas_call(functools.partial(cycle_kernel, comps=comps), out_shape=[p...  2.1 us
    ppermute x2, starting transfers between devices, local(): lax.ppermute(x, ('comp', 'tile'), swaps(turn, ROUNDS, comps, tiles))  1.71 us
    ppermute x1, starting transfers between devices, local(): lax.ppermute(jnp.concatenate(joined(chips - 1) + [outward]), 'tile', swap)  1.43 us
    ppermute x2, waiting for transfers between devices, local(): lax.ppermute(x, ('comp', 'tile'), swaps(turn, ROUNDS, comps, tiles))  1.38 us
    pallas_call x1, Pallas kernels, local(): pl.pallas_call(forcing_kernel, out_shape=jax.ShapeDtypeStruct((fields, ro...  0.96 us
  transfers between devices with their start and end apart: 9, of which 3 were waited for; matrix products, arithmetic and copies ran while one was open for 0% of the time, Pallas kernels for 7%

profile of v9, /device:TPU:0, one launch (start us, length us, event | category | flops | bytes accessed | tf_op | source)
XLA Modules:
  0.0 18.5 jit_solution(5056620268122993850)
XLA Ops:
  0.6 2.1 %remap.1 = (f32[368,128]{1,0:T(8,128)S(1)}, f32[160,128]{1,0:T(8,128)S(1)}, f32[80,128]{1,0:T(8,128)S(1)}, f32[80,128]{1,0:T(8,128)S(1)}, f32[80,128]{1,0:T(8,128)S(1)}) custom-call(f32[8,1024]{1,0:T(8,128)} %flux_far.1, f32[8,4,128,128]{3,2,1,0:T(8,128)} %weight.1, s32[4,8]{1,0:T(4,128)} %bitcast.2, s32[4,8]{1,0:T(4,128)} %bitcast.3, s32[8]{0:T(128)} %count_far.1, ...), custom_call_target="tpu_custom_call" | custom-call | tf_op jit(solution)/shard_map/remap/pallas_call | solution.py:344
  2.8 0.5 %collective-permute-start = (f32[208,128]{1,0:T(8,128)S(1)}, f32[208,128]{1,0:T(8,128)S(1)}, u32[]{:S(2)}, u32[]{:S(2)}) collective-permute-start(f32[208,128]{1,0:T(8,128)S(1)} %slice.93), channel_id=1, source_target_pairs={{0,1},{1,0},{2,3},{3,2},{4,5},{5,4},{6,7},{7,6},{8,9},{9,8},{10,11... | collective-permute-start | bytes 319496 | tf_op jit(solution)/shard_map/ppermute | solution.py:365
  3.3 1.0 %collective-permute-done = f32[208,128]{1,0:T(8,128)S(1)} collective-permute-done((f32[208,128]{1,0:T(8,128)S(1)}, f32[208,128]{1,0:T(8,128)S(1)}, u32[]{:S(2)}, u32[]{:S(2)}) %collective-permute-start) | collective-permute-done | bytes 106528 | tf_op jit(solution)/shard_map/ppermute | solution.py:365
  4.3 2.7 %collective-permute-start.1 = (f32[168,128]{1,0:T(8,128)S(1)}, f32[168,128]{1,0:T(8,128)S(1)}, u32[]{:S(2)}, u32[]{:S(2)}) collective-permute-start(f32[168,128]{1,0:T(8,128)S(1)} %get-tuple-element.45), channel_id=1, source_target_pairs={{0,3},{1,4},{2,1},{3,6},{4,7},{5,0},{6,5},{7,2},{8,11},{9,12},{10,... | collective-permute-start | bytes 258056 | tf_op jit(solution)/shard_map/ppermute | solution.py:381
  7.0 1.4 %collective-permute-start.3 = (f32[96,128]{1,0:T(8,128)S(1)}, f32[96,128]{1,0:T(8,128)S(1)}, u32[]{:S(2)}, u32[]{:S(2)}) collective-permute-start(f32[96,128]{1,0:T(8,128)S(1)} %pad_maximum_fusion.1), channel_id=1, source_target_pairs={{0,7},{1,6},{2,5},{3,4},{4,3},{5,2},{6,1},{7,0},{8,15},{9,14},{10,... | collective-permute-start | bytes 147464 | tf_op jit(solution)/shard_map/ppermute | solution.py:384
  8.4 0.8 %collective-permute-done.1.refs_1_ = f32[168,128]{1,0:T(8,128)S(1)} collective-permute-done((f32[168,128]{1,0:T(8,128)S(1)}, f32[168,128]{1,0:T(8,128)S(1)}, u32[]{:S(2)}, u32[]{:S(2)}) %collective-permute-start.1) | collective-permute-done | bytes 86048 | tf_op jit(solution)/shard_map/ppermute | solution.py:381
  9.2 0.3 %collective-permute-start.2 = (f32[96,128]{1,0:T(8,128)S(1)}, f32[96,128]{1,0:T(8,128)S(1)}, u32[]{:S(2)}, u32[]{:S(2)}) collective-permute-start(f32[96,128]{1,0:T(8,128)S(1)} %slice.121), channel_id=1, source_target_pairs={{0,1},{1,0},{2,3},{3,2},{4,5},{5,4},{6,7},{7,6},{8,9},{9,8},{10,11... | collective-permute-start | bytes 147464 | tf_op jit(solution)/shard_map/ppermute | solution.py:382
  9.5 1.9 %collective-permute-start.4 = (f32[80,128]{1,0:T(8,128)S(1)}, f32[80,128]{1,0:T(8,128)S(1)}, u32[]{:S(2)}, u32[]{:S(2)}) collective-permute-start(f32[80,128]{1,0:T(8,128)S(1)} %get-tuple-element.30), channel_id=1, source_target_pairs={{0,8},{1,9},{2,10},{3,11},{4,12},{5,13},{6,14},{7,15},{8,0},{9,1},... | collective-permute-start | bytes 122888 | tf_op jit(solution)/shard_map/ppermute | solution.py:387
  11.4 0.1 collective-permute-start.5
  11.5 0.4 %collective-permute-start.6 = (f32[80,128]{1,0:T(8,128)S(1)}, f32[80,128]{1,0:T(8,128)S(1)}, u32[]{:S(2)}, u32[]{:S(2)}) collective-permute-start(f32[80,128]{1,0:T(8,128)S(1)} %get-tuple-element.32), channel_id=1, source_target_pairs={{0,1},{1,0},{2,3},{3,2},{4,5},{5,4},{6,7},{7,6},{8,9},{9,8},{10,11... | collective-permute-start | bytes 122888 | tf_op jit(solution)/shard_map/ppermute | solution.py:387
  11.9 0.0 collective-permute-done.3.refs_3_
  11.9 0.0 collective-permute-done.2.refs_2_
  11.9 0.4 %place.1 = (f32[96,128]{1,0:T(8,128)S(1)}, f32[32,128]{1,0:T(8,128)S(1)}, f32[32,128]{1,0:T(8,128)S(1)}, f32[80,128]{1,0:T(8,128)S(1)}, f32[80,128]{1,0:T(8,128)S(1)}) custom-call(f32[96,128]{1,0:T(8,128)S(1)} %pad_maximum_fusion.refs_0_, f32[168,128]{1,0:T(8,128)S(1)} %collective-permute-done.1.refs_1_, f32[96,128]{1,0:T(8,128)S(1)} %collective-permute-done.2.refs_2_, ...), custom_call_target="tpu_custom_call" | custom-call | tf_op jit(solution)/shard_map/place/pallas_call | solution.py:388
  12.3 1.5 %collective-permute-start.7 = (f32[80,128]{1,0:T(8,128)S(1)}, f32[80,128]{1,0:T(8,128)S(1)}, u32[]{:S(2)}, u32[]{:S(2)}) collective-permute-start(f32[80,128]{1,0:T(8,128)S(1)} %get-tuple-element.33), channel_id=1, source_target_pairs={{0,8},{1,9},{2,10},{3,11},{4,12},{5,13},{6,14},{7,15},{8,0},{9,1},... | collective-permute-start | bytes 122888 | tf_op jit(solution)/shard_map/ppermute | solution.py:397
  13.8 0.2 %collective-permute-start.8 = (f32[80,128]{1,0:T(8,128)S(1)}, f32[80,128]{1,0:T(8,128)S(1)}, u32[]{:S(2)}, u32[]{:S(2)}) collective-permute-start(f32[80,128]{1,0:T(8,128)S(1)} %get-tuple-element.34), channel_id=1, source_target_pairs={{0,1},{1,0},{2,3},{3,2},{4,5},{5,4},{6,7},{7,6},{8,16},{9,17},{10,... | collective-permute-start | bytes 122888 | tf_op jit(solution)/shard_map/ppermute | solution.py:397
  14.0 1.0 %forcing.1 = f32[8,32,128]{2,1,0:T(8,128)} custom-call(f32[96,128]{1,0:T(8,128)S(1)} %pad_maximum_fusion.refs_0_, f32[168,128]{1,0:T(8,128)S(1)} %collective-permute-done.1.refs_1_, f32[96,128]{1,0:T(8,128)S(1)} %collective-permute-done.2.refs_2_, f32[96,128]{1,0:T(8,128)S(1)} %collective-permute-done.3.refs_3_, f32[160,128]{1,0:T(8,128)S(1)} %get-tuple-element.26.refs_4_.state), custom_call_target="tpu_custom_call" | custom-call | flops 100000000 | bytes 4194304 | tf_op jit(solution)/shard_map/forcing/pallas_call | solution.py:400
  15.0 0.0 collective-permute-done.4.refs_0_
  15.0 0.0 collective-permute-done.5.refs_1_
  15.0 0.0 collective-permute-done.6.refs_2_
  15.0 1.4 %collective-permute-done.7.refs_3_ = f32[80,128]{1,0:T(8,128)S(1)} collective-permute-done((f32[80,128]{1,0:T(8,128)S(1)}, f32[80,128]{1,0:T(8,128)S(1)}, u32[]{:S(2)}, u32[]{:S(2)}) %collective-permute-start.7) | collective-permute-done | bytes 40992 | tf_op jit(solution)/shard_map/ppermute | solution.py:397
  16.4 0.0 collective-permute-done.8.refs_4_
  16.4 2.1 %cycles.1 = (f32[32,128]{1,0:T(8,128)}, f32[32,128]{1,0:T(8,128)}, f32[32,128]{1,0:T(8,128)}) custom-call(f32[160,128]{1,0:T(8,128)S(1)} %get-tuple-element.26.refs_4_.state, f32[96,128]{1,0:T(8,128)S(1)} %get-tuple-element.27.wet, f32[32,128]{1,0:T(8,128)S(1)} %get-tuple-element.28.left, f32[32,128]{1,0:T(8,128)S(1)} %get-tuple-element.29.right, ...), custom_call_target="tpu_custom_call" | custom-call | tf_op jit(solution)/shard_map/cycles/pallas_call | solution.py:409
  (11 shorter events, 0.1 us)
Async XLA Ops:
  2.8 1.5 %collective-permute-start = (f32[208,128]{1,0:T(8,128)S(1)}, f32[208,128]{1,0:T(8,128)S(1)}, u32[]{:S(2)}, u32[]{:S(2)}) collective-permute-start(f32[208,128]{1,0:T(8,128)S(1)} %slice.93), channel_id=1, source_target_pairs={{0,1},{1,0},{2,3},{3,2},{4,5},{5,4},{6,7},{7,6},{8,9},{9,8},{10,11... | collective-permute-start | bytes 319496 | tf_op jit(solution)/shard_map/ppermute | solution.py:365
  4.3 4.9 %collective-permute-start.1 = (f32[168,128]{1,0:T(8,128)S(1)}, f32[168,128]{1,0:T(8,128)S(1)}, u32[]{:S(2)}, u32[]{:S(2)}) collective-permute-start(f32[168,128]{1,0:T(8,128)S(1)} %get-tuple-element.45), channel_id=1, source_target_pairs={{0,3},{1,4},{2,1},{3,6},{4,7},{5,0},{6,5},{7,2},{8,11},{9,12},{10,... | collective-permute-start | bytes 258056 | tf_op jit(solution)/shard_map/ppermute | solution.py:381
  7.0 4.9 %collective-permute-start.3 = (f32[96,128]{1,0:T(8,128)S(1)}, f32[96,128]{1,0:T(8,128)S(1)}, u32[]{:S(2)}, u32[]{:S(2)}) collective-permute-start(f32[96,128]{1,0:T(8,128)S(1)} %pad_maximum_fusion.1), channel_id=1, source_target_pairs={{0,7},{1,6},{2,5},{3,4},{4,3},{5,2},{6,1},{7,0},{8,15},{9,14},{10,... | collective-permute-start | bytes 147464 | tf_op jit(solution)/shard_map/ppermute | solution.py:384
  9.2 2.7 %collective-permute-start.2 = (f32[96,128]{1,0:T(8,128)S(1)}, f32[96,128]{1,0:T(8,128)S(1)}, u32[]{:S(2)}, u32[]{:S(2)}) collective-permute-start(f32[96,128]{1,0:T(8,128)S(1)} %slice.121), channel_id=1, source_target_pairs={{0,1},{1,0},{2,3},{3,2},{4,5},{5,4},{6,7},{7,6},{8,9},{9,8},{10,11... | collective-permute-start | bytes 147464 | tf_op jit(solution)/shard_map/ppermute | solution.py:382
  9.5 5.5 %collective-permute-start.4 = (f32[80,128]{1,0:T(8,128)S(1)}, f32[80,128]{1,0:T(8,128)S(1)}, u32[]{:S(2)}, u32[]{:S(2)}) collective-permute-start(f32[80,128]{1,0:T(8,128)S(1)} %get-tuple-element.30), channel_id=1, source_target_pairs={{0,8},{1,9},{2,10},{3,11},{4,12},{5,13},{6,14},{7,15},{8,0},{9,1},... | collective-permute-start | bytes 122888 | tf_op jit(solution)/shard_map/ppermute | solution.py:387
  11.4 3.6 %collective-permute-start.5 = (f32[80,128]{1,0:T(8,128)S(1)}, f32[80,128]{1,0:T(8,128)S(1)}, u32[]{:S(2)}, u32[]{:S(2)}) collective-permute-start(f32[80,128]{1,0:T(8,128)S(1)} %get-tuple-element.31), channel_id=1, source_target_pairs={{0,1},{1,0},{2,3},{3,2},{4,5},{5,4},{6,7},{7,6},{8,16},{9,17},{10,... | collective-permute-start | bytes 122888 | tf_op jit(solution)/shard_map/ppermute | solution.py:387
  11.5 3.5 %collective-permute-start.6 = (f32[80,128]{1,0:T(8,128)S(1)}, f32[80,128]{1,0:T(8,128)S(1)}, u32[]{:S(2)}, u32[]{:S(2)}) collective-permute-start(f32[80,128]{1,0:T(8,128)S(1)} %get-tuple-element.32), channel_id=1, source_target_pairs={{0,1},{1,0},{2,3},{3,2},{4,5},{5,4},{6,7},{7,6},{8,9},{9,8},{10,11... | collective-permute-start | bytes 122888 | tf_op jit(solution)/shard_map/ppermute | solution.py:387
  12.3 4.1 %collective-permute-start.7 = (f32[80,128]{1,0:T(8,128)S(1)}, f32[80,128]{1,0:T(8,128)S(1)}, u32[]{:S(2)}, u32[]{:S(2)}) collective-permute-start(f32[80,128]{1,0:T(8,128)S(1)} %get-tuple-element.33), channel_id=1, source_target_pairs={{0,8},{1,9},{2,10},{3,11},{4,12},{5,13},{6,14},{7,15},{8,0},{9,1},... | collective-permute-start | bytes 122888 | tf_op jit(solution)/shard_map/ppermute | solution.py:397
  13.8 2.6 %collective-permute-start.8 = (f32[80,128]{1,0:T(8,128)S(1)}, f32[80,128]{1,0:T(8,128)S(1)}, u32[]{:S(2)}, u32[]{:S(2)}) collective-permute-start(f32[80,128]{1,0:T(8,128)S(1)} %get-tuple-element.34), channel_id=1, source_target_pairs={{0,1},{1,0},{2,3},{3,2},{4,5},{5,4},{6,7},{7,6},{8,16},{9,17},{10,... | collective-permute-start | bytes 122888 | tf_op jit(solution)/shard_map/ppermute | solution.py:397

commit v10 on v9

--- a/solution.py
+++ b/solution.py
@@ -116,12 +116,15 @@
             ],
             axis=1,
         )
-        for k in range(slots):
-            w_high, w_low = halves(stage[b, k])
+        for first in range(0, slots, 4):
+            group = range(first, min(first + 4, slots))
+            w_high, w_low = halves(jnp.concatenate([stage[b, k] for k in group], axis=1))
             both = jnp.dot(
                 left, jnp.concatenate([w_high, w_low], axis=0), preferred_element_type=F32
             )
-            held[pl.ds(places[b * slots + k], fields), :] = both[:fields] + both[fields:]
+            both = both[:fields] + both[fields:]
+            for i, k in enumerate(group):
+                held[pl.ds(places[b * slots + k], fields), :] = both[:, i * LANES : (i + 1) * LANES]
 
     for t in range(tiles):
         lefts, rights = max(t - 1, 0), min(t + 1, tiles - 1)

time: 18.7 us -> 18.7 us (level)
  no operation moved by 1% of the time
where the time goes in v10:
time: 18.7 us; the launch traced here: 18.5 us
  starting transfers between devices  9.03 us (48%)
  Pallas kernels  5.59 us (30%)
  waiting for transfers between devices  3.1 us (17%)
  between operations  0.7 us (4%)
    ppermute x1, starting transfers between devices, local(): box = lax.ppermute(jnp.concatenate(parts), 'tile', swap)  2.65 us
    ppermute x3, starting transfers between devices, local(): lax.ppermute(x, ('comp', 'tile'), swaps(turn, EARLY, comps, tiles))  2.38 us
    pallas_call x1, Pallas kernels, local(): pl.pallas_call(functools.partial(remap_kernel, tiles=tiles), out_shape=[n...  2.14 us
    pallas_call x1, Pallas kernels, local(): pl.pallas_call(functools.partial(cycle_kernel, comps=comps), out_shape=[p...  2.1 us
    ppermute x2, starting transfers between devices, local(): lax.ppermute(x, ('comp', 'tile'), swaps(turn, ROUNDS, comps, tiles))  1.71 us
    ppermute x1, starting transfers between devices, local(): lax.ppermute(jnp.concatenate(joined(chips - 1) + [outward]), 'tile', swap)  1.43 us
    ppermute x2, waiting for transfers between devices, local(): lax.ppermute(x, ('comp', 'tile'), swaps(turn, ROUNDS, comps, tiles))  1.38 us
    pallas_call x1, Pallas kernels, local(): pl.pallas_call(forcing_kernel, out_shape=jax.ShapeDtypeStruct((fields, ro...  0.97 us
  transfers between devices with their start and end apart: 9, of which 3 were waited for; matrix products, arithmetic and copies ran while one was open for 0% of the time, Pallas kernels for 7%

profile of v10, /device:TPU:0, one launch (start us, length us, event | category | flops | bytes accessed | tf_op | source)
XLA Modules:
  0.0 18.5 jit_solution(7918711895592356734)
XLA Ops:
  0.6 2.1 %remap.1 = (f32[368,128]{1,0:T(8,128)S(1)}, f32[160,128]{1,0:T(8,128)S(1)}, f32[80,128]{1,0:T(8,128)S(1)}, f32[80,128]{1,0:T(8,128)S(1)}, f32[80,128]{1,0:T(8,128)S(1)}) custom-call(f32[8,1024]{1,0:T(8,128)} %flux_far.1, f32[8,4,128,128]{3,2,1,0:T(8,128)} %weight.1, s32[4,8]{1,0:T(4,128)} %bitcast.2, s32[4,8]{1,0:T(4,128)} %bitcast.3, s32[8]{0:T(128)} %count_far.1, ...), custom_call_target="tpu_custom_call" | custom-call | tf_op jit(solution)/shard_map/remap/pallas_call | solution.py:347
  2.8 0.5 %collective-permute-start = (f32[208,128]{1,0:T(8,128)S(1)}, f32[208,128]{1,0:T(8,128)S(1)}, u32[]{:S(2)}, u32[]{:S(2)}) collective-permute-start(f32[208,128]{1,0:T(8,128)S(1)} %slice.93), channel_id=1, source_target_pairs={{0,1},{1,0},{2,3},{3,2},{4,5},{5,4},{6,7},{7,6},{8,9},{9,8},{10,11... | collective-permute-start | bytes 319496 | tf_op jit(solution)/shard_map/ppermute | solution.py:368
  3.3 1.0 %collective-permute-done = f32[208,128]{1,0:T(8,128)S(1)} collective-permute-done((f32[208,128]{1,0:T(8,128)S(1)}, f32[208,128]{1,0:T(8,128)S(1)}, u32[]{:S(2)}, u32[]{:S(2)}) %collective-permute-start) | collective-permute-done | bytes 106528 | tf_op jit(solution)/shard_map/ppermute | solution.py:368
  4.3 2.7 %collective-permute-start.1 = (f32[168,128]{1,0:T(8,128)S(1)}, f32[168,128]{1,0:T(8,128)S(1)}, u32[]{:S(2)}, u32[]{:S(2)}) collective-permute-start(f32[168,128]{1,0:T(8,128)S(1)} %get-tuple-element.45), channel_id=1, source_target_pairs={{0,3},{1,4},{2,1},{3,6},{4,7},{5,0},{6,5},{7,2},{8,11},{9,12},{10,... | collective-permute-start | bytes 258056 | tf_op jit(solution)/shard_map/ppermute | solution.py:384
  7.0 1.4 %collective-permute-start.3 = (f32[96,128]{1,0:T(8,128)S(1)}, f32[96,128]{1,0:T(8,128)S(1)}, u32[]{:S(2)}, u32[]{:S(2)}) collective-permute-start(f32[96,128]{1,0:T(8,128)S(1)} %pad_maximum_fusion.1), channel_id=1, source_target_pairs={{0,7},{1,6},{2,5},{3,4},{4,3},{5,2},{6,1},{7,0},{8,15},{9,14},{10,... | collective-permute-start | bytes 147464 | tf_op jit(solution)/shard_map/ppermute | solution.py:387
  8.4 0.8 %collective-permute-done.1.refs_1_ = f32[168,128]{1,0:T(8,128)S(1)} collective-permute-done((f32[168,128]{1,0:T(8,128)S(1)}, f32[168,128]{1,0:T(8,128)S(1)}, u32[]{:S(2)}, u32[]{:S(2)}) %collective-permute-start.1) | collective-permute-done | bytes 86048 | tf_op jit(solution)/shard_map/ppermute | solution.py:384
  9.2 0.3 %collective-permute-start.2 = (f32[96,128]{1,0:T(8,128)S(1)}, f32[96,128]{1,0:T(8,128)S(1)}, u32[]{:S(2)}, u32[]{:S(2)}) collective-permute-start(f32[96,128]{1,0:T(8,128)S(1)} %slice.121), channel_id=1, source_target_pairs={{0,1},{1,0},{2,3},{3,2},{4,5},{5,4},{6,7},{7,6},{8,9},{9,8},{10,11... | collective-permute-start | bytes 147464 | tf_op jit(solution)/shard_map/ppermute | solution.py:385
  9.5 1.9 %collective-permute-start.4 = (f32[80,128]{1,0:T(8,128)S(1)}, f32[80,128]{1,0:T(8,128)S(1)}, u32[]{:S(2)}, u32[]{:S(2)}) collective-permute-start(f32[80,128]{1,0:T(8,128)S(1)} %get-tuple-element.30), channel_id=1, source_target_pairs={{0,8},{1,9},{2,10},{3,11},{4,12},{5,13},{6,14},{7,15},{8,0},{9,1},... | collective-permute-start | bytes 122888 | tf_op jit(solution)/shard_map/ppermute | solution.py:390
  11.4 0.1 collective-permute-start.5
  11.5 0.4 %collective-permute-start.6 = (f32[80,128]{1,0:T(8,128)S(1)}, f32[80,128]{1,0:T(8,128)S(1)}, u32[]{:S(2)}, u32[]{:S(2)}) collective-permute-start(f32[80,128]{1,0:T(8,128)S(1)} %get-tuple-element.32), channel_id=1, source_target_pairs={{0,1},{1,0},{2,3},{3,2},{4,5},{5,4},{6,7},{7,6},{8,9},{9,8},{10,11... | collective-permute-start | bytes 122888 | tf_op jit(solution)/shard_map/ppermute | solution.py:390
  11.9 0.0 collective-permute-done.3.refs_3_
  11.9 0.0 collective-permute-done.2.refs_2_
  11.9 0.4 %place.1 = (f32[96,128]{1,0:T(8,128)S(1)}, f32[32,128]{1,0:T(8,128)S(1)}, f32[32,128]{1,0:T(8,128)S(1)}, f32[80,128]{1,0:T(8,128)S(1)}, f32[80,128]{1,0:T(8,128)S(1)}) custom-call(f32[96,128]{1,0:T(8,128)S(1)} %pad_maximum_fusion.refs_0_, f32[168,128]{1,0:T(8,128)S(1)} %collective-permute-done.1.refs_1_, f32[96,128]{1,0:T(8,128)S(1)} %collective-permute-done.2.refs_2_, ...), custom_call_target="tpu_custom_call" | custom-call | tf_op jit(solution)/shard_map/place/pallas_call | solution.py:391
  12.3 1.5 %collective-permute-start.7 = (f32[80,128]{1,0:T(8,128)S(1)}, f32[80,128]{1,0:T(8,128)S(1)}, u32[]{:S(2)}, u32[]{:S(2)}) collective-permute-start(f32[80,128]{1,0:T(8,128)S(1)} %get-tuple-element.33), channel_id=1, source_target_pairs={{0,8},{1,9},{2,10},{3,11},{4,12},{5,13},{6,14},{7,15},{8,0},{9,1},... | collective-permute-start | bytes 122888 | tf_op jit(solution)/shard_map/ppermute | solution.py:400
  13.8 0.2 %collective-permute-start.8 = (f32[80,128]{1,0:T(8,128)S(1)}, f32[80,128]{1,0:T(8,128)S(1)}, u32[]{:S(2)}, u32[]{:S(2)}) collective-permute-start(f32[80,128]{1,0:T(8,128)S(1)} %get-tuple-element.34), channel_id=1, source_target_pairs={{0,1},{1,0},{2,3},{3,2},{4,5},{5,4},{6,7},{7,6},{8,16},{9,17},{10,... | collective-permute-start | bytes 122888 | tf_op jit(solution)/shard_map/ppermute | solution.py:400
  14.0 1.0 %forcing.1 = f32[8,32,128]{2,1,0:T(8,128)} custom-call(f32[96,128]{1,0:T(8,128)S(1)} %pad_maximum_fusion.refs_0_, f32[168,128]{1,0:T(8,128)S(1)} %collective-permute-done.1.refs_1_, f32[96,128]{1,0:T(8,128)S(1)} %collective-permute-done.2.refs_2_, f32[96,128]{1,0:T(8,128)S(1)} %collective-permute-done.3.refs_3_, f32[160,128]{1,0:T(8,128)S(1)} %get-tuple-element.26.refs_4_.state), custom_call_target="tpu_custom_call" | custom-call | flops 100000000 | bytes 4194304 | tf_op jit(solution)/shard_map/forcing/pallas_call | solution.py:403
  15.0 0.0 collective-permute-done.4.refs_0_
  15.0 0.0 collective-permute-done.5.refs_1_
  15.0 0.0 collective-permute-done.6.refs_2_
  15.0 1.4 %collective-permute-done.7.refs_3_ = f32[80,128]{1,0:T(8,128)S(1)} collective-permute-done((f32[80,128]{1,0:T(8,128)S(1)}, f32[80,128]{1,0:T(8,128)S(1)}, u32[]{:S(2)}, u32[]{:S(2)}) %collective-permute-start.7) | collective-permute-done | bytes 40992 | tf_op jit(solution)/shard_map/ppermute | solution.py:400
  16.4 0.0 collective-permute-done.8.refs_4_
  16.4 2.1 %cycles.1 = (f32[32,128]{1,0:T(8,128)}, f32[32,128]{1,0:T(8,128)}, f32[32,128]{1,0:T(8,128)}) custom-call(f32[160,128]{1,0:T(8,128)S(1)} %get-tuple-element.26.refs_4_.state, f32[96,128]{1,0:T(8,128)S(1)} %get-tuple-element.27.wet, f32[32,128]{1,0:T(8,128)S(1)} %get-tuple-element.28.left, f32[32,128]{1,0:T(8,128)S(1)} %get-tuple-element.29.right, ...), custom_call_target="tpu_custom_call" | custom-call | tf_op jit(solution)/shard_map/cycles/pallas_call | solution.py:412
  (11 shorter events, 0.1 us)
Async XLA Ops:
  2.8 1.5 %collective-permute-start = (f32[208,128]{1,0:T(8,128)S(1)}, f32[208,128]{1,0:T(8,128)S(1)}, u32[]{:S(2)}, u32[]{:S(2)}) collective-permute-start(f32[208,128]{1,0:T(8,128)S(1)} %slice.93), channel_id=1, source_target_pairs={{0,1},{1,0},{2,3},{3,2},{4,5},{5,4},{6,7},{7,6},{8,9},{9,8},{10,11... | collective-permute-start | bytes 319496 | tf_op jit(solution)/shard_map/ppermute | solution.py:368
  4.3 4.9 %collective-permute-start.1 = (f32[168,128]{1,0:T(8,128)S(1)}, f32[168,128]{1,0:T(8,128)S(1)}, u32[]{:S(2)}, u32[]{:S(2)}) collective-permute-start(f32[168,128]{1,0:T(8,128)S(1)} %get-tuple-element.45), channel_id=1, source_target_pairs={{0,3},{1,4},{2,1},{3,6},{4,7},{5,0},{6,5},{7,2},{8,11},{9,12},{10,... | collective-permute-start | bytes 258056 | tf_op jit(solution)/shard_map/ppermute | solution.py:384
  7.0 4.9 %collective-permute-start.3 = (f32[96,128]{1,0:T(8,128)S(1)}, f32[96,128]{1,0:T(8,128)S(1)}, u32[]{:S(2)}, u32[]{:S(2)}) collective-permute-start(f32[96,128]{1,0:T(8,128)S(1)} %pad_maximum_fusion.1), channel_id=1, source_target_pairs={{0,7},{1,6},{2,5},{3,4},{4,3},{5,2},{6,1},{7,0},{8,15},{9,14},{10,... | collective-permute-start | bytes 147464 | tf_op jit(solution)/shard_map/ppermute | solution.py:387
  9.2 2.7 %collective-permute-start.2 = (f32[96,128]{1,0:T(8,128)S(1)}, f32[96,128]{1,0:T(8,128)S(1)}, u32[]{:S(2)}, u32[]{:S(2)}) collective-permute-start(f32[96,128]{1,0:T(8,128)S(1)} %slice.121), channel_id=1, source_target_pairs={{0,1},{1,0},{2,3},{3,2},{4,5},{5,4},{6,7},{7,6},{8,9},{9,8},{10,11... | collective-permute-start | bytes 147464 | tf_op jit(solution)/shard_map/ppermute | solution.py:385
  9.5 5.5 %collective-permute-start.4 = (f32[80,128]{1,0:T(8,128)S(1)}, f32[80,128]{1,0:T(8,128)S(1)}, u32[]{:S(2)}, u32[]{:S(2)}) collective-permute-start(f32[80,128]{1,0:T(8,128)S(1)} %get-tuple-element.30), channel_id=1, source_target_pairs={{0,8},{1,9},{2,10},{3,11},{4,12},{5,13},{6,14},{7,15},{8,0},{9,1},... | collective-permute-start | bytes 122888 | tf_op jit(solution)/shard_map/ppermute | solution.py:390
  11.4 3.6 %collective-permute-start.5 = (f32[80,128]{1,0:T(8,128)S(1)}, f32[80,128]{1,0:T(8,128)S(1)}, u32[]{:S(2)}, u32[]{:S(2)}) collective-permute-start(f32[80,128]{1,0:T(8,128)S(1)} %get-tuple-element.31), channel_id=1, source_target_pairs={{0,1},{1,0},{2,3},{3,2},{4,5},{5,4},{6,7},{7,6},{8,16},{9,17},{10,... | collective-permute-start | bytes 122888 | tf_op jit(solution)/shard_map/ppermute | solution.py:390
  11.5 3.5 %collective-permute-start.6 = (f32[80,128]{1,0:T(8,128)S(1)}, f32[80,128]{1,0:T(8,128)S(1)}, u32[]{:S(2)}, u32[]{:S(2)}) collective-permute-start(f32[80,128]{1,0:T(8,128)S(1)} %get-tuple-element.32), channel_id=1, source_target_pairs={{0,1},{1,0},{2,3},{3,2},{4,5},{5,4},{6,7},{7,6},{8,9},{9,8},{10,11... | collective-permute-start | bytes 122888 | tf_op jit(solution)/shard_map/ppermute | solution.py:390
  12.3 4.1 %collective-permute-start.7 = (f32[80,128]{1,0:T(8,128)S(1)}, f32[80,128]{1,0:T(8,128)S(1)}, u32[]{:S(2)}, u32[]{:S(2)}) collective-permute-start(f32[80,128]{1,0:T(8,128)S(1)} %get-tuple-element.33), channel_id=1, source_target_pairs={{0,8},{1,9},{2,10},{3,11},{4,12},{5,13},{6,14},{7,15},{8,0},{9,1},... | collective-permute-start | bytes 122888 | tf_op jit(solution)/shard_map/ppermute | solution.py:400
  13.8 2.6 %collective-permute-start.8 = (f32[80,128]{1,0:T(8,128)S(1)}, f32[80,128]{1,0:T(8,128)S(1)}, u32[]{:S(2)}, u32[]{:S(2)}) collective-permute-start(f32[80,128]{1,0:T(8,128)S(1)} %get-tuple-element.34), channel_id=1, source_target_pairs={{0,1},{1,0},{2,3},{3,2},{4,5},{5,4},{6,7},{7,6},{8,16},{9,17},{10,... | collective-permute-start | bytes 122888 | tf_op jit(solution)/shard_map/ppermute | solution.py:400

commit v11 on v9

--- a/solution.py
+++ b/solution.py
@@ -32,7 +32,7 @@
 
 def route(k, core, chips):
     alone = (k == 0) | (k == chips - 1)
-    sender = jnp.where(k == 0, core, jnp.where(alone, 1 - core, lax.rem(k + 1, 2)))
+    sender = jnp.where(k == 0, core, jnp.where(alone, 1 - core, lax.rem(k, 2)))
     place = jnp.where(alone, k, (k - 1) // 2 * 2 + 1 + jnp.where(sender == core, 1, 0))
     return sender, place
 
@@ -216,7 +216,7 @@
     facing, away = boxes[0][at : at + 24, :], boxes[-1][at : at + 24, :]
     for k in filter(beside, pairs_of(chips)):
         direct, passed = boxes[k][2 * at : 2 * at + 24, :], boxes[k + 1][at : at + 24, :]
-        away = jnp.where(beyond == lax.bitwise_xor(chip, k), jnp.where(core == 1, direct, passed), away)
+        away = jnp.where(beyond == lax.bitwise_xor(chip, k), jnp.where(core == 0, direct, passed), away)
     for which, out in ((0, left), (1, right)):
         edge = jnp.where(core == which, away, facing)
         packed, small = edge[:16], edge[16:]
@@ -376,8 +376,8 @@
         parts = joined(k) + joined(k + 1)
         if beside(k):
             up = lax.bitwise_xor(tile // 2, k) > tile // 2
-            parts.append(jnp.where(up, away, outward))
-        swap = [(t, t ^ (2 * (k + t % 2)) ^ 1) for t in range(tiles)]
+            parts.append(jnp.where(up, outward, away))
+        swap = [(t, t ^ (2 * (k + 1 - t % 2)) ^ 1) for t in range(tiles)]
         box = lax.ppermute(jnp.concatenate(parts), "tile", swap)
         boxes += [box, lax.ppermute(box[8 + 2 * values :], "tile", [(t, t ^ 1) for t in range(tiles)])]
     swap = [(t, t ^ (2 * (chips - 1)) ^ 1) for t in range(tiles)]

time: 18.7 us -> 18.7 us (level)
  no operation moved by 1% of the time
where the time goes in v11:
time: 18.7 us; the launch traced here: 18.5 us
  starting transfers between devices  9.09 us (49%)
  Pallas kernels  5.6 us (30%)
  waiting for transfers between devices  3.05 us (16%)
  between operations  0.7 us (4%)
    ppermute x1, starting transfers between devices, local(): box = lax.ppermute(jnp.concatenate(parts), 'tile', swap)  2.68 us
    ppermute x3, starting transfers between devices, local(): lax.ppermute(x, ('comp', 'tile'), swaps(turn, EARLY, comps, tiles))  2.35 us
    pallas_call x1, Pallas kernels, local(): pl.pallas_call(functools.partial(remap_kernel, tiles=tiles), out_shape=[n...  2.15 us
    pallas_call x1, Pallas kernels, local(): pl.pallas_call(functools.partial(cycle_kernel, comps=comps), out_shape=[p...  2.1 us
    ppermute x2, starting transfers between devices, local(): lax.ppermute(x, ('comp', 'tile'), swaps(turn, ROUNDS, comps, tiles))  1.72 us
    ppermute x1, starting transfers between devices, local(): lax.ppermute(jnp.concatenate(joined(chips - 1) + [outward]), 'tile', swap)  1.43 us
    ppermute x2, waiting for transfers between devices, local(): lax.ppermute(x, ('comp', 'tile'), swaps(turn, ROUNDS, comps, tiles))  1.38 us
    pallas_call x1, Pallas kernels, local(): pl.pallas_call(forcing_kernel, out_shape=jax.ShapeDtypeStruct((fields, ro...  0.97 us
  transfers between devices with their start and end apart: 9, of which 3 were waited for; matrix products, arithmetic and copies ran while one was open for 0% of the time, Pallas kernels for 7%

profile of v11, /device:TPU:0, one launch (start us, length us, event | category | flops | bytes accessed | tf_op | source)
XLA Modules:
  0.0 18.5 jit_solution(9559597357072854666)
XLA Ops:
  0.6 2.1 %remap.1 = (f32[368,128]{1,0:T(8,128)S(1)}, f32[160,128]{1,0:T(8,128)S(1)}, f32[80,128]{1,0:T(8,128)S(1)}, f32[80,128]{1,0:T(8,128)S(1)}, f32[80,128]{1,0:T(8,128)S(1)}) custom-call(f32[8,1024]{1,0:T(8,128)} %flux_far.1, f32[8,4,128,128]{3,2,1,0:T(8,128)} %weight.1, s32[4,8]{1,0:T(4,128)} %bitcast.2, s32[4,8]{1,0:T(4,128)} %bitcast.3, s32[8]{0:T(128)} %count_far.1, ...), custom_call_target="tpu_custom_call" | custom-call | tf_op jit(solution)/shard_map/remap/pallas_call | solution.py:344
  2.8 0.5 %collective-permute-start = (f32[208,128]{1,0:T(8,128)S(1)}, f32[208,128]{1,0:T(8,128)S(1)}, u32[]{:S(2)}, u32[]{:S(2)}) collective-permute-start(f32[208,128]{1,0:T(8,128)S(1)} %slice.93), channel_id=1, source_target_pairs={{0,1},{1,0},{2,3},{3,2},{4,5},{5,4},{6,7},{7,6},{8,9},{9,8},{10,11... | collective-permute-start | bytes 319496 | tf_op jit(solution)/shard_map/ppermute | solution.py:365
  3.3 1.0 %collective-permute-done = f32[208,128]{1,0:T(8,128)S(1)} collective-permute-done((f32[208,128]{1,0:T(8,128)S(1)}, f32[208,128]{1,0:T(8,128)S(1)}, u32[]{:S(2)}, u32[]{:S(2)}) %collective-permute-start) | collective-permute-done | bytes 106528 | tf_op jit(solution)/shard_map/ppermute | solution.py:365
  4.3 2.7 %collective-permute-start.1 = (f32[168,128]{1,0:T(8,128)S(1)}, f32[168,128]{1,0:T(8,128)S(1)}, u32[]{:S(2)}, u32[]{:S(2)}) collective-permute-start(f32[168,128]{1,0:T(8,128)S(1)} %get-tuple-element.45), channel_id=1, source_target_pairs={{0,5},{1,2},{2,7},{3,0},{4,1},{5,6},{6,3},{7,4},{8,13},{9,10},{10,... | collective-permute-start | bytes 258056 | tf_op jit(solution)/shard_map/ppermute | solution.py:381
  7.0 1.4 %collective-permute-start.3 = (f32[96,128]{1,0:T(8,128)S(1)}, f32[96,128]{1,0:T(8,128)S(1)}, u32[]{:S(2)}, u32[]{:S(2)}) collective-permute-start(f32[96,128]{1,0:T(8,128)S(1)} %pad_maximum_fusion.1), channel_id=1, source_target_pairs={{0,7},{1,6},{2,5},{3,4},{4,3},{5,2},{6,1},{7,0},{8,15},{9,14},{10,... | collective-permute-start | bytes 147464 | tf_op jit(solution)/shard_map/ppermute | solution.py:384
  8.5 0.7 %collective-permute-done.1.refs_1_ = f32[168,128]{1,0:T(8,128)S(1)} collective-permute-done((f32[168,128]{1,0:T(8,128)S(1)}, f32[168,128]{1,0:T(8,128)S(1)}, u32[]{:S(2)}, u32[]{:S(2)}) %collective-permute-start.1) | collective-permute-done | bytes 86048 | tf_op jit(solution)/shard_map/ppermute | solution.py:381
  9.2 0.4 %collective-permute-start.2 = (f32[96,128]{1,0:T(8,128)S(1)}, f32[96,128]{1,0:T(8,128)S(1)}, u32[]{:S(2)}, u32[]{:S(2)}) collective-permute-start(f32[96,128]{1,0:T(8,128)S(1)} %slice.121), channel_id=1, source_target_pairs={{0,1},{1,0},{2,3},{3,2},{4,5},{5,4},{6,7},{7,6},{8,9},{9,8},{10,11... | collective-permute-start | bytes 147464 | tf_op jit(solution)/shard_map/ppermute | solution.py:382
  9.6 1.8 %collective-permute-start.4 = (f32[80,128]{1,0:T(8,128)S(1)}, f32[80,128]{1,0:T(8,128)S(1)}, u32[]{:S(2)}, u32[]{:S(2)}) collective-permute-start(f32[80,128]{1,0:T(8,128)S(1)} %get-tuple-element.30), channel_id=1, source_target_pairs={{0,8},{1,9},{2,10},{3,11},{4,12},{5,13},{6,14},{7,15},{8,0},{9,1},... | collective-permute-start | bytes 122888 | tf_op jit(solution)/shard_map/ppermute | solution.py:387
  11.4 0.1 collective-permute-start.5
  11.5 0.4 %collective-permute-start.6 = (f32[80,128]{1,0:T(8,128)S(1)}, f32[80,128]{1,0:T(8,128)S(1)}, u32[]{:S(2)}, u32[]{:S(2)}) collective-permute-start(f32[80,128]{1,0:T(8,128)S(1)} %get-tuple-element.32), channel_id=1, source_target_pairs={{0,1},{1,0},{2,3},{3,2},{4,5},{5,4},{6,7},{7,6},{8,9},{9,8},{10,11... | collective-permute-start | bytes 122888 | tf_op jit(solution)/shard_map/ppermute | solution.py:387
  11.9 0.0 collective-permute-done.3.refs_3_
  11.9 0.0 collective-permute-done.2.refs_2_
  11.9 0.4 %place.1 = (f32[96,128]{1,0:T(8,128)S(1)}, f32[32,128]{1,0:T(8,128)S(1)}, f32[32,128]{1,0:T(8,128)S(1)}, f32[80,128]{1,0:T(8,128)S(1)}, f32[80,128]{1,0:T(8,128)S(1)}) custom-call(f32[96,128]{1,0:T(8,128)S(1)} %pad_maximum_fusion.refs_0_, f32[168,128]{1,0:T(8,128)S(1)} %collective-permute-done.1.refs_1_, f32[96,128]{1,0:T(8,128)S(1)} %collective-permute-done.2.refs_2_, ...), custom_call_target="tpu_custom_call" | custom-call | tf_op jit(solution)/shard_map/place/pallas_call | solution.py:388
  12.3 1.5 %collective-permute-start.7 = (f32[80,128]{1,0:T(8,128)S(1)}, f32[80,128]{1,0:T(8,128)S(1)}, u32[]{:S(2)}, u32[]{:S(2)}) collective-permute-start(f32[80,128]{1,0:T(8,128)S(1)} %get-tuple-element.33), channel_id=1, source_target_pairs={{0,8},{1,9},{2,10},{3,11},{4,12},{5,13},{6,14},{7,15},{8,0},{9,1},... | collective-permute-start | bytes 122888 | tf_op jit(solution)/shard_map/ppermute | solution.py:397
  13.8 0.2 %collective-permute-start.8 = (f32[80,128]{1,0:T(8,128)S(1)}, f32[80,128]{1,0:T(8,128)S(1)}, u32[]{:S(2)}, u32[]{:S(2)}) collective-permute-start(f32[80,128]{1,0:T(8,128)S(1)} %get-tuple-element.34), channel_id=1, source_target_pairs={{0,1},{1,0},{2,3},{3,2},{4,5},{5,4},{6,7},{7,6},{8,16},{9,17},{10,... | collective-permute-start | bytes 122888 | tf_op jit(solution)/shard_map/ppermute | solution.py:397
  14.0 1.0 %forcing.1 = f32[8,32,128]{2,1,0:T(8,128)} custom-call(f32[96,128]{1,0:T(8,128)S(1)} %pad_maximum_fusion.refs_0_, f32[168,128]{1,0:T(8,128)S(1)} %collective-permute-done.1.refs_1_, f32[96,128]{1,0:T(8,128)S(1)} %collective-permute-done.2.refs_2_, f32[96,128]{1,0:T(8,128)S(1)} %collective-permute-done.3.refs_3_, f32[160,128]{1,0:T(8,128)S(1)} %get-tuple-element.26.refs_4_.state), custom_call_target="tpu_custom_call" | custom-call | flops 100000000 | bytes 4194304 | tf_op jit(solution)/shard_map/forcing/pallas_call | solution.py:400
  15.0 0.0 collective-permute-done.4.refs_0_
  15.0 0.0 collective-permute-done.5.refs_1_
  15.0 0.0 collective-permute-done.6.refs_2_
  15.0 1.4 %collective-permute-done.7.refs_3_ = f32[80,128]{1,0:T(8,128)S(1)} collective-permute-done((f32[80,128]{1,0:T(8,128)S(1)}, f32[80,128]{1,0:T(8,128)S(1)}, u32[]{:S(2)}, u32[]{:S(2)}) %collective-permute-start.7) | collective-permute-done | bytes 40992 | tf_op jit(solution)/shard_map/ppermute | solution.py:397
  16.4 0.0 collective-permute-done.8.refs_4_
  16.4 2.1 %cycles.1 = (f32[32,128]{1,0:T(8,128)}, f32[32,128]{1,0:T(8,128)}, f32[32,128]{1,0:T(8,128)}) custom-call(f32[160,128]{1,0:T(8,128)S(1)} %get-tuple-element.26.refs_4_.state, f32[96,128]{1,0:T(8,128)S(1)} %get-tuple-element.27.wet, f32[32,128]{1,0:T(8,128)S(1)} %get-tuple-element.28.left, f32[32,128]{1,0:T(8,128)S(1)} %get-tuple-element.29.right, ...), custom_call_target="tpu_custom_call" | custom-call | tf_op jit(solution)/shard_map/cycles/pallas_call | solution.py:409
  (11 shorter events, 0.1 us)
Async XLA Ops:
  2.8 1.5 %collective-permute-start = (f32[208,128]{1,0:T(8,128)S(1)}, f32[208,128]{1,0:T(8,128)S(1)}, u32[]{:S(2)}, u32[]{:S(2)}) collective-permute-start(f32[208,128]{1,0:T(8,128)S(1)} %slice.93), channel_id=1, source_target_pairs={{0,1},{1,0},{2,3},{3,2},{4,5},{5,4},{6,7},{7,6},{8,9},{9,8},{10,11... | collective-permute-start | bytes 319496 | tf_op jit(solution)/shard_map/ppermute | solution.py:365
  4.3 4.8 %collective-permute-start.1 = (f32[168,128]{1,0:T(8,128)S(1)}, f32[168,128]{1,0:T(8,128)S(1)}, u32[]{:S(2)}, u32[]{:S(2)}) collective-permute-start(f32[168,128]{1,0:T(8,128)S(1)} %get-tuple-element.45), channel_id=1, source_target_pairs={{0,5},{1,2},{2,7},{3,0},{4,1},{5,6},{6,3},{7,4},{8,13},{9,10},{10,... | collective-permute-start | bytes 258056 | tf_op jit(solution)/shard_map/ppermute | solution.py:381
  7.0 4.9 %collective-permute-start.3 = (f32[96,128]{1,0:T(8,128)S(1)}, f32[96,128]{1,0:T(8,128)S(1)}, u32[]{:S(2)}, u32[]{:S(2)}) collective-permute-start(f32[96,128]{1,0:T(8,128)S(1)} %pad_maximum_fusion.1), channel_id=1, source_target_pairs={{0,7},{1,6},{2,5},{3,4},{4,3},{5,2},{6,1},{7,0},{8,15},{9,14},{10,... | collective-permute-start | bytes 147464 | tf_op jit(solution)/shard_map/ppermute | solution.py:384
  9.2 2.8 %collective-permute-start.2 = (f32[96,128]{1,0:T(8,128)S(1)}, f32[96,128]{1,0:T(8,128)S(1)}, u32[]{:S(2)}, u32[]{:S(2)}) collective-permute-start(f32[96,128]{1,0:T(8,128)S(1)} %slice.121), channel_id=1, source_target_pairs={{0,1},{1,0},{2,3},{3,2},{4,5},{5,4},{6,7},{7,6},{8,9},{9,8},{10,11... | collective-permute-start | bytes 147464 | tf_op jit(solution)/shard_map/ppermute | solution.py:382
  9.6 5.4 %collective-permute-start.4 = (f32[80,128]{1,0:T(8,128)S(1)}, f32[80,128]{1,0:T(8,128)S(1)}, u32[]{:S(2)}, u32[]{:S(2)}) collective-permute-start(f32[80,128]{1,0:T(8,128)S(1)} %get-tuple-element.30), channel_id=1, source_target_pairs={{0,8},{1,9},{2,10},{3,11},{4,12},{5,13},{6,14},{7,15},{8,0},{9,1},... | collective-permute-start | bytes 122888 | tf_op jit(solution)/shard_map/ppermute | solution.py:387
  11.4 3.6 %collective-permute-start.5 = (f32[80,128]{1,0:T(8,128)S(1)}, f32[80,128]{1,0:T(8,128)S(1)}, u32[]{:S(2)}, u32[]{:S(2)}) collective-permute-start(f32[80,128]{1,0:T(8,128)S(1)} %get-tuple-element.31), channel_id=1, source_target_pairs={{0,1},{1,0},{2,3},{3,2},{4,5},{5,4},{6,7},{7,6},{8,16},{9,17},{10,... | collective-permute-start | bytes 122888 | tf_op jit(solution)/shard_map/ppermute | solution.py:387
  11.5 3.5 %collective-permute-start.6 = (f32[80,128]{1,0:T(8,128)S(1)}, f32[80,128]{1,0:T(8,128)S(1)}, u32[]{:S(2)}, u32[]{:S(2)}) collective-permute-start(f32[80,128]{1,0:T(8,128)S(1)} %get-tuple-element.32), channel_id=1, source_target_pairs={{0,1},{1,0},{2,3},{3,2},{4,5},{5,4},{6,7},{7,6},{8,9},{9,8},{10,11... | collective-permute-start | bytes 122888 | tf_op jit(solution)/shard_map/ppermute | solution.py:387
  12.3 4.1 %collective-permute-start.7 = (f32[80,128]{1,0:T(8,128)S(1)}, f32[80,128]{1,0:T(8,128)S(1)}, u32[]{:S(2)}, u32[]{:S(2)}) collective-permute-start(f32[80,128]{1,0:T(8,128)S(1)} %get-tuple-element.33), channel_id=1, source_target_pairs={{0,8},{1,9},{2,10},{3,11},{4,12},{5,13},{6,14},{7,15},{8,0},{9,1},... | collective-permute-start | bytes 122888 | tf_op jit(solution)/shard_map/ppermute | solution.py:397
  13.8 2.6 %collective-permute-start.8 = (f32[80,128]{1,0:T(8,128)S(1)}, f32[80,128]{1,0:T(8,128)S(1)}, u32[]{:S(2)}, u32[]{:S(2)}) collective-permute-start(f32[80,128]{1,0:T(8,128)S(1)} %get-tuple-element.34), channel_id=1, source_target_pairs={{0,1},{1,0},{2,3},{3,2},{4,5},{5,4},{6,7},{7,6},{8,16},{9,17},{10,... | collective-permute-start | bytes 122888 | tf_op jit(solution)/shard_map/ppermute | solution.py:397

commit v12 on v9

--- a/solution.py
+++ b/solution.py
@@ -205,8 +205,10 @@
     hot_mine, hot_other = (one_hot(names[:, at : at + 1])[: 2 * rows] for at in (48, 112))
     hot_main = hot_slots(names, rows)
     sea = state[4 * rows : 5 * rows]
+    driven_by = jnp.concatenate([field_values(boxes, f, fields) for f in range(WET)], axis=1)
+    grids = spread(hot_main, driven_by)
     for f in range(WET):
-        wet[f * rows : (f + 1) * rows] = spread(hot_main, field_values(boxes, f, fields)) * sea
+        wet[f * rows : (f + 1) * rows] = grids[:, f * LANES : (f + 1) * LANES] * sea
     sides = pltpu.roll(spread(hot_mine, names), 80, 1) + pltpu.roll(spread(hot_other, names), 16, 1)
     lane = lanes_of(rows)
     me = lax.axis_index("tile")

time: 18.7 us -> 18.7 us (level)
  no operation moved by 1% of the time
where the time goes in v12:
time: 18.7 us; the launch traced here: 18.5 us
  starting transfers between devices  9.03 us (48%)
  Pallas kernels  5.6 us (30%)
  waiting for transfers between devices  3.11 us (17%)
  between operations  0.7 us (4%)
    ppermute x1, starting transfers between devices, local(): box = lax.ppermute(jnp.concatenate(parts), 'tile', swap)  2.65 us
    ppermute x3, starting transfers between devices, local(): lax.ppermute(x, ('comp', 'tile'), swaps(turn, EARLY, comps, tiles))  2.38 us
    pallas_call x1, Pallas kernels, local(): pl.pallas_call(functools.partial(remap_kernel, tiles=tiles), out_shape=[n...  2.15 us
    pallas_call x1, Pallas kernels, local(): pl.pallas_call(functools.partial(cycle_kernel, comps=comps), out_shape=[p...  2.1 us
    ppermute x2, starting transfers between devices, local(): lax.ppermute(x, ('comp', 'tile'), swaps(turn, ROUNDS, comps, tiles))  1.71 us
    ppermute x1, starting transfers between devices, local(): lax.ppermute(jnp.concatenate(joined(chips - 1) + [outward]), 'tile', swap)  1.43 us
    ppermute x2, waiting for transfers between devices, local(): lax.ppermute(x, ('comp', 'tile'), swaps(turn, ROUNDS, comps, tiles))  1.38 us
    pallas_call x1, Pallas kernels, local(): pl.pallas_call(forcing_kernel, out_shape=jax.ShapeDtypeStruct((fields, ro...  0.96 us
  transfers between devices with their start and end apart: 9, of which 3 were waited for; matrix products, arithmetic and copies ran while one was open for 0% of the time, Pallas kernels for 7%

profile of v12, /device:TPU:0, one launch (start us, length us, event | category | flops | bytes accessed | tf_op | source)
XLA Modules:
  0.0 18.5 jit_solution(10524290483273755060)
XLA Ops:
  0.6 2.1 %remap.1 = (f32[368,128]{1,0:T(8,128)S(1)}, f32[160,128]{1,0:T(8,128)S(1)}, f32[80,128]{1,0:T(8,128)S(1)}, f32[80,128]{1,0:T(8,128)S(1)}, f32[80,128]{1,0:T(8,128)S(1)}) custom-call(f32[8,1024]{1,0:T(8,128)} %flux_far.1, f32[8,4,128,128]{3,2,1,0:T(8,128)} %weight.1, s32[4,8]{1,0:T(4,128)} %bitcast.2, s32[4,8]{1,0:T(4,128)} %bitcast.3, s32[8]{0:T(128)} %count_far.1, ...), custom_call_target="tpu_custom_call" | custom-call | tf_op jit(solution)/shard_map/remap/pallas_call | solution.py:346
  2.8 0.5 %collective-permute-start = (f32[208,128]{1,0:T(8,128)S(1)}, f32[208,128]{1,0:T(8,128)S(1)}, u32[]{:S(2)}, u32[]{:S(2)}) collective-permute-start(f32[208,128]{1,0:T(8,128)S(1)} %slice.93), channel_id=1, source_target_pairs={{0,1},{1,0},{2,3},{3,2},{4,5},{5,4},{6,7},{7,6},{8,9},{9,8},{10,11... | collective-permute-start | bytes 319496 | tf_op jit(solution)/shard_map/ppermute | solution.py:367
  3.3 1.0 %collective-permute-done = f32[208,128]{1,0:T(8,128)S(1)} collective-permute-done((f32[208,128]{1,0:T(8,128)S(1)}, f32[208,128]{1,0:T(8,128)S(1)}, u32[]{:S(2)}, u32[]{:S(2)}) %collective-permute-start) | collective-permute-done | bytes 106528 | tf_op jit(solution)/shard_map/ppermute | solution.py:367
  4.3 2.7 %collective-permute-start.1 = (f32[168,128]{1,0:T(8,128)S(1)}, f32[168,128]{1,0:T(8,128)S(1)}, u32[]{:S(2)}, u32[]{:S(2)}) collective-permute-start(f32[168,128]{1,0:T(8,128)S(1)} %get-tuple-element.45), channel_id=1, source_target_pairs={{0,3},{1,4},{2,1},{3,6},{4,7},{5,0},{6,5},{7,2},{8,11},{9,12},{10,... | collective-permute-start | bytes 258056 | tf_op jit(solution)/shard_map/ppermute | solution.py:383
  7.0 1.4 %collective-permute-start.3 = (f32[96,128]{1,0:T(8,128)S(1)}, f32[96,128]{1,0:T(8,128)S(1)}, u32[]{:S(2)}, u32[]{:S(2)}) collective-permute-start(f32[96,128]{1,0:T(8,128)S(1)} %pad_maximum_fusion.1), channel_id=1, source_target_pairs={{0,7},{1,6},{2,5},{3,4},{4,3},{5,2},{6,1},{7,0},{8,15},{9,14},{10,... | collective-permute-start | bytes 147464 | tf_op jit(solution)/shard_map/ppermute | solution.py:386
  8.4 0.8 %collective-permute-done.1.refs_1_ = f32[168,128]{1,0:T(8,128)S(1)} collective-permute-done((f32[168,128]{1,0:T(8,128)S(1)}, f32[168,128]{1,0:T(8,128)S(1)}, u32[]{:S(2)}, u32[]{:S(2)}) %collective-permute-start.1) | collective-permute-done | bytes 86048 | tf_op jit(solution)/shard_map/ppermute | solution.py:383
  9.2 0.3 %collective-permute-start.2 = (f32[96,128]{1,0:T(8,128)S(1)}, f32[96,128]{1,0:T(8,128)S(1)}, u32[]{:S(2)}, u32[]{:S(2)}) collective-permute-start(f32[96,128]{1,0:T(8,128)S(1)} %slice.121), channel_id=1, source_target_pairs={{0,1},{1,0},{2,3},{3,2},{4,5},{5,4},{6,7},{7,6},{8,9},{9,8},{10,11... | collective-permute-start | bytes 147464 | tf_op jit(solution)/shard_map/ppermute | solution.py:384
  9.5 1.9 %collective-permute-start.4 = (f32[80,128]{1,0:T(8,128)S(1)}, f32[80,128]{1,0:T(8,128)S(1)}, u32[]{:S(2)}, u32[]{:S(2)}) collective-permute-start(f32[80,128]{1,0:T(8,128)S(1)} %get-tuple-element.30), channel_id=1, source_target_pairs={{0,8},{1,9},{2,10},{3,11},{4,12},{5,13},{6,14},{7,15},{8,0},{9,1},... | collective-permute-start | bytes 122888 | tf_op jit(solution)/shard_map/ppermute | solution.py:389
  11.4 0.1 collective-permute-start.5
  11.5 0.4 %collective-permute-start.6 = (f32[80,128]{1,0:T(8,128)S(1)}, f32[80,128]{1,0:T(8,128)S(1)}, u32[]{:S(2)}, u32[]{:S(2)}) collective-permute-start(f32[80,128]{1,0:T(8,128)S(1)} %get-tuple-element.32), channel_id=1, source_target_pairs={{0,1},{1,0},{2,3},{3,2},{4,5},{5,4},{6,7},{7,6},{8,9},{9,8},{10,11... | collective-permute-start | bytes 122888 | tf_op jit(solution)/shard_map/ppermute | solution.py:389
  11.9 0.0 collective-permute-done.3.refs_3_
  11.9 0.0 collective-permute-done.2.refs_2_
  11.9 0.4 %place.1 = (f32[96,128]{1,0:T(8,128)S(1)}, f32[32,128]{1,0:T(8,128)S(1)}, f32[32,128]{1,0:T(8,128)S(1)}, f32[80,128]{1,0:T(8,128)S(1)}, f32[80,128]{1,0:T(8,128)S(1)}) custom-call(f32[96,128]{1,0:T(8,128)S(1)} %pad_maximum_fusion.refs_0_, f32[168,128]{1,0:T(8,128)S(1)} %collective-permute-done.1.refs_1_, f32[96,128]{1,0:T(8,128)S(1)} %collective-permute-done.2.refs_2_, ...), custom_call_target="tpu_custom_call" | custom-call | tf_op jit(solution)/shard_map/place/pallas_call | solution.py:390
  12.3 1.5 %collective-permute-start.7 = (f32[80,128]{1,0:T(8,128)S(1)}, f32[80,128]{1,0:T(8,128)S(1)}, u32[]{:S(2)}, u32[]{:S(2)}) collective-permute-start(f32[80,128]{1,0:T(8,128)S(1)} %get-tuple-element.33), channel_id=1, source_target_pairs={{0,8},{1,9},{2,10},{3,11},{4,12},{5,13},{6,14},{7,15},{8,0},{9,1},... | collective-permute-start | bytes 122888 | tf_op jit(solution)/shard_map/ppermute | solution.py:399
  13.8 0.2 %collective-permute-start.8 = (f32[80,128]{1,0:T(8,128)S(1)}, f32[80,128]{1,0:T(8,128)S(1)}, u32[]{:S(2)}, u32[]{:S(2)}) collective-permute-start(f32[80,128]{1,0:T(8,128)S(1)} %get-tuple-element.34), channel_id=1, source_target_pairs={{0,1},{1,0},{2,3},{3,2},{4,5},{5,4},{6,7},{7,6},{8,16},{9,17},{10,... | collective-permute-start | bytes 122888 | tf_op jit(solution)/shard_map/ppermute | solution.py:399
  14.0 1.0 %forcing.1 = f32[8,32,128]{2,1,0:T(8,128)} custom-call(f32[96,128]{1,0:T(8,128)S(1)} %pad_maximum_fusion.refs_0_, f32[168,128]{1,0:T(8,128)S(1)} %collective-permute-done.1.refs_1_, f32[96,128]{1,0:T(8,128)S(1)} %collective-permute-done.2.refs_2_, f32[96,128]{1,0:T(8,128)S(1)} %collective-permute-done.3.refs_3_, f32[160,128]{1,0:T(8,128)S(1)} %get-tuple-element.26.refs_4_.state), custom_call_target="tpu_custom_call" | custom-call | flops 100000000 | bytes 4194304 | tf_op jit(solution)/shard_map/forcing/pallas_call | solution.py:402
  15.0 0.0 collective-permute-done.4.refs_0_
  15.0 0.0 collective-permute-done.5.refs_1_
  15.0 0.0 collective-permute-done.6.refs_2_
  15.0 1.4 %collective-permute-done.7.refs_3_ = f32[80,128]{1,0:T(8,128)S(1)} collective-permute-done((f32[80,128]{1,0:T(8,128)S(1)}, f32[80,128]{1,0:T(8,128)S(1)}, u32[]{:S(2)}, u32[]{:S(2)}) %collective-permute-start.7) | collective-permute-done | bytes 40992 | tf_op jit(solution)/shard_map/ppermute | solution.py:399
  16.4 0.0 collective-permute-done.8.refs_4_
  16.4 2.1 %cycles.1 = (f32[32,128]{1,0:T(8,128)}, f32[32,128]{1,0:T(8,128)}, f32[32,128]{1,0:T(8,128)}) custom-call(f32[160,128]{1,0:T(8,128)S(1)} %get-tuple-element.26.refs_4_.state, f32[96,128]{1,0:T(8,128)S(1)} %get-tuple-element.27.wet, f32[32,128]{1,0:T(8,128)S(1)} %get-tuple-element.28.left, f32[32,128]{1,0:T(8,128)S(1)} %get-tuple-element.29.right, ...), custom_call_target="tpu_custom_call" | custom-call | tf_op jit(solution)/shard_map/cycles/pallas_call | solution.py:411
  (11 shorter events, 0.1 us)
Async XLA Ops:
  2.8 1.5 %collective-permute-start = (f32[208,128]{1,0:T(8,128)S(1)}, f32[208,128]{1,0:T(8,128)S(1)}, u32[]{:S(2)}, u32[]{:S(2)}) collective-permute-start(f32[208,128]{1,0:T(8,128)S(1)} %slice.93), channel_id=1, source_target_pairs={{0,1},{1,0},{2,3},{3,2},{4,5},{5,4},{6,7},{7,6},{8,9},{9,8},{10,11... | collective-permute-start | bytes 319496 | tf_op jit(solution)/shard_map/ppermute | solution.py:367
  4.3 4.8 %collective-permute-start.1 = (f32[168,128]{1,0:T(8,128)S(1)}, f32[168,128]{1,0:T(8,128)S(1)}, u32[]{:S(2)}, u32[]{:S(2)}) collective-permute-start(f32[168,128]{1,0:T(8,128)S(1)} %get-tuple-element.45), channel_id=1, source_target_pairs={{0,3},{1,4},{2,1},{3,6},{4,7},{5,0},{6,5},{7,2},{8,11},{9,12},{10,... | collective-permute-start | bytes 258056 | tf_op jit(solution)/shard_map/ppermute | solution.py:383
  7.0 4.9 %collective-permute-start.3 = (f32[96,128]{1,0:T(8,128)S(1)}, f32[96,128]{1,0:T(8,128)S(1)}, u32[]{:S(2)}, u32[]{:S(2)}) collective-permute-start(f32[96,128]{1,0:T(8,128)S(1)} %pad_maximum_fusion.1), channel_id=1, source_target_pairs={{0,7},{1,6},{2,5},{3,4},{4,3},{5,2},{6,1},{7,0},{8,15},{9,14},{10,... | collective-permute-start | bytes 147464 | tf_op jit(solution)/shard_map/ppermute | solution.py:386
  9.2 2.7 %collective-permute-start.2 = (f32[96,128]{1,0:T(8,128)S(1)}, f32[96,128]{1,0:T(8,128)S(1)}, u32[]{:S(2)}, u32[]{:S(2)}) collective-permute-start(f32[96,128]{1,0:T(8,128)S(1)} %slice.121), channel_id=1, source_target_pairs={{0,1},{1,0},{2,3},{3,2},{4,5},{5,4},{6,7},{7,6},{8,9},{9,8},{10,11... | collective-permute-start | bytes 147464 | tf_op jit(solution)/shard_map/ppermute | solution.py:384
  9.5 5.5 %collective-permute-start.4 = (f32[80,128]{1,0:T(8,128)S(1)}, f32[80,128]{1,0:T(8,128)S(1)}, u32[]{:S(2)}, u32[]{:S(2)}) collective-permute-start(f32[80,128]{1,0:T(8,128)S(1)} %get-tuple-element.30), channel_id=1, source_target_pairs={{0,8},{1,9},{2,10},{3,11},{4,12},{5,13},{6,14},{7,15},{8,0},{9,1},... | collective-permute-start | bytes 122888 | tf_op jit(solution)/shard_map/ppermute | solution.py:389
  11.4 3.6 %collective-permute-start.5 = (f32[80,128]{1,0:T(8,128)S(1)}, f32[80,128]{1,0:T(8,128)S(1)}, u32[]{:S(2)}, u32[]{:S(2)}) collective-permute-start(f32[80,128]{1,0:T(8,128)S(1)} %get-tuple-element.31), channel_id=1, source_target_pairs={{0,1},{1,0},{2,3},{3,2},{4,5},{5,4},{6,7},{7,6},{8,16},{9,17},{10,... | collective-permute-start | bytes 122888 | tf_op jit(solution)/shard_map/ppermute | solution.py:389
  11.5 3.5 %collective-permute-start.6 = (f32[80,128]{1,0:T(8,128)S(1)}, f32[80,128]{1,0:T(8,128)S(1)}, u32[]{:S(2)}, u32[]{:S(2)}) collective-permute-start(f32[80,128]{1,0:T(8,128)S(1)} %get-tuple-element.32), channel_id=1, source_target_pairs={{0,1},{1,0},{2,3},{3,2},{4,5},{5,4},{6,7},{7,6},{8,9},{9,8},{10,11... | collective-permute-start | bytes 122888 | tf_op jit(solution)/shard_map/ppermute | solution.py:389
  12.3 4.1 %collective-permute-start.7 = (f32[80,128]{1,0:T(8,128)S(1)}, f32[80,128]{1,0:T(8,128)S(1)}, u32[]{:S(2)}, u32[]{:S(2)}) collective-permute-start(f32[80,128]{1,0:T(8,128)S(1)} %get-tuple-element.33), channel_id=1, source_target_pairs={{0,8},{1,9},{2,10},{3,11},{4,12},{5,13},{6,14},{7,15},{8,0},{9,1},... | collective-permute-start | bytes 122888 | tf_op jit(solution)/shard_map/ppermute | solution.py:399
  13.8 2.6 %collective-permute-start.8 = (f32[80,128]{1,0:T(8,128)S(1)}, f32[80,128]{1,0:T(8,128)S(1)}, u32[]{:S(2)}, u32[]{:S(2)}) collective-permute-start(f32[80,128]{1,0:T(8,128)S(1)} %get-tuple-element.34), channel_id=1, source_target_pairs={{0,1},{1,0},{2,3},{3,2},{4,5},{5,4},{6,7},{7,6},{8,16},{9,17},{10,... | collective-permute-start | bytes 122888 | tf_op jit(solution)/shard_map/ppermute | solution.py:399
